TPU v7x, 128 devices: a whole 4x4x4 slice. The times are simulated.
128 devices in a mesh: grp: 4 (over z), sub: 32 (over y, x, core).
Axes of the slice: x: 4, y: 4, z: 4, core: 2. Of those that a mesh axis runs over, the one named last changes fastest.
Arguments:
- loads: float32 [512, 8, 32, 128], P(('grp', 'sub')), may hold values from -20 to 20
- schur: bfloat16 [512, 1024, 1024], P(('grp', 'sub')), may hold values from 0 to 8, as said below
- local_inverse: bfloat16 [512, 1024, 1024], P(('grp', 'sub')), may hold values from 0 to 1, as said below
- coarse_basis: float32 [512, 8, 8, 128], P(('grp', 'sub')), may hold values from -0.375 to 0.375
- coarse_inverse: float32 [2048, 2048], P('sub'), may hold values from 0 to 1, as said below
- primal_index: int32 [512, 8], P(('grp', 'sub')), may hold values from 0 to 2047
- nbr_sub: int32 [512, 8], P(('grp', 'sub')), may hold values from -1 to 511, as said below
- nbr_block: int32 [512, 8], P(('grp', 'sub')), may hold values from -1 to 7, as said below
Outputs:
- solution: float32 [512, 8, 32, 128], P(('grp', 'sub'))
- precond: float32 [512, 8, 32, 128], P(('grp', 'sub'))
Inputs may be any that keep to these rules, and one draw needn't show every extreme that they name: `nbr_sub`: for a face b < 6, the partner subdomain lies on another device with the same grp index, and its entry names this face back. No device has more than 2 such faces whose partners lie on one other device; some pair of devices has exactly 2. Face 8 - 2 of a subdomain pairs with face 8 - 1 of the subdomain at the same place on the device with the next grp index and the same sub index, face 8 - 1 with face 8 - 2 on the device with the previous grp index; none (-1) at the first and last grp index. `nbr_block`: the partner's face index, -1 where there is no partner. `schur`: each subdomain's matrix is symmetric positive definite. `local_inverse`: each subdomain's matrix is symmetric positive definite. `coarse_inverse`: symmetric positive definite.
All inputs are finite; a program needn't handle non-finite values.
Results may differ from a plain program's by a relative error of at most 0.0026.
Values sent between devices are 32-bit elements; how exact they have to be, the bound alone decides.
No kernel may reach another device: no remote copies, remote signals or barrier semaphores. Data moves between devices by JAX's collectives and lax.ppermute only.
A program may use at most 128 MiB of HBM per device.

v0:
```python
import jax
import jax.numpy as jnp
from jax import lax
from jax.sharding import PartitionSpec as P

ITERS = 2


PRECISE = lax.Precision.HIGHEST


def extended(shard, sides, width):
    for axis, dim in sides:
        devices, length = (lax.axis_size(axis), shard.shape[dim])
        up = [(i, (i + 1) % devices) for i in range(devices - 1)]
        down = [(j, i) for i, j in up]
        last = lax.slice_in_dim(shard, length - width, length, axis=dim)
        leading = lax.slice_in_dim(shard, 0, width, axis=dim)
        before = lax.ppermute(last, axis, up)
        after = lax.ppermute(leading, axis, down)
        shard = jnp.concatenate([before, shard, after], axis=dim)
    return shard


def face_routes(nbr_sub, nbr_block, peer_count, capacity):
    sub_here = nbr_sub.shape[0]
    face_count = nbr_sub.shape[1] - 2
    partner = nbr_sub[:, :face_count].reshape(-1)
    peer_index = partner // sub_here % peer_count
    partner_place = partner % sub_here * face_count + nbr_block[:, :face_count].reshape(-1)
    places = jnp.arange(sub_here * face_count, dtype=jnp.int32)
    same_peer = peer_index[:, None] == peer_index[None, :]
    send_rank = jnp.sum(same_peer & (places[None, :] < places[:, None]), axis=1)
    recv_rank = jnp.sum(same_peer & (partner_place[None, :] < partner_place[:, None]), axis=1)
    send_slot = peer_index * capacity + send_rank
    recv_slot = peer_index * capacity + recv_rank
    slot_ids = jnp.arange(peer_count * capacity, dtype=jnp.int32)
    matches = slot_ids[:, None] == send_slot[None, :]
    source = jnp.sum(jnp.where(matches, places[None, :], 0), axis=1)
    filled = jnp.any(matches, axis=1)
    return (source, filled, recv_slot)


def assemble(partial_sum, routes):
    source, filled, recv_slot = routes
    sub_here, blocks, case_count, block_width = partial_sum.shape
    face_count = blocks - 2
    shared = partial_sum[:, :face_count].reshape(sub_here * face_count, case_count, block_width)
    outgoing = jnp.where(filled[:, None, None], shared[source], 0.0)
    incoming = lax.all_to_all(outgoing, "sub", split_axis=0, concat_axis=0, tiled=True)
    shared = shared + incoming[recv_slot]
    slab_rims = jnp.stack([partial_sum[:, blocks - 1], partial_sum[:, blocks - 2]])
    padded = extended(slab_rims, (("grp", 0),), 1)
    upper_face = partial_sum[:, blocks - 2] + padded[3]
    lower_face = partial_sum[:, blocks - 1] + padded[0]
    return jnp.concatenate(
        [
            shared.reshape(sub_here, face_count, case_count, block_width),
            upper_face[:, None],
            lower_face[:, None],
        ],
        axis=1,
    )


def apply_blocks(matrices, field):
    sub_here, blocks, case_count, block_width = field.shape
    shaped = matrices.reshape(sub_here, blocks, block_width, blocks, block_width)
    return jnp.einsum(
        "sbrk,sbkcl->scrl", field.astype(jnp.bfloat16), shaped, preferred_element_type=jnp.float32
    )


def coarse_part(field, weights, coarse_basis, onehot):
    projected = jnp.einsum("scbk,sbrk->scr", coarse_basis, weights * field, precision=PRECISE)
    return jnp.einsum(
        "pn,pr->nr", onehot, projected.reshape(-1, projected.shape[-1]), precision=PRECISE
    )


def coarse_sum(field, weights, coarse_basis, onehot):
    return lax.psum(coarse_part(field, weights, coarse_basis, onehot), ("grp", "sub"))


def global_dot(resid, precond, weights):
    return lax.psum(jnp.sum(weights * resid * precond, axis=(0, 1, 3)), ("grp", "sub"))


def coarse_solve(coarse_total, coarse_rows):
    piece = jnp.dot(coarse_rows, coarse_total, precision=PRECISE)
    return lax.all_gather(piece, "sub", axis=0, tiled=True)


def precondition(
    resid, coarse_total, weights, local_inverse, coarse_basis, coarse_rows, onehot, routes
):
    sub_here = resid.shape[0]
    weighted = weights * resid
    local_part = apply_blocks(local_inverse, weighted)
    coarse_values = coarse_solve(coarse_total, coarse_rows)
    picked = jnp.dot(onehot, coarse_values, precision=PRECISE).reshape(
        sub_here, -1, coarse_values.shape[-1]
    )
    corrected = local_part + jnp.einsum("scbk,scr->sbrk", coarse_basis, picked, precision=PRECISE)
    return assemble(weights * corrected, routes)


def local(
    loads, schur, local_inverse, coarse_basis, coarse_inverse, primal_index, nbr_sub, nbr_block
):
    sub_here, blocks, case_count, block_width = loads.shape
    peer_count = lax.axis_size("sub")
    face_count = blocks - 2
    capacity = max(2, (sub_here * face_count + peer_count - 2) // (peer_count - 1))
    routes = face_routes(nbr_sub, nbr_block, peer_count, capacity)
    weights = (1.0 / (1.0 + (nbr_sub >= 0).astype(jnp.float32)))[:, :, None, None]
    prim_count = coarse_inverse.shape[1]
    onehot = (
        primal_index.reshape(-1)[:, None] == jnp.arange(prim_count, dtype=jnp.int32)[None, :]
    ).astype(jnp.float32)
    resid = assemble(loads, routes)
    coarse_total = coarse_sum(resid, weights, coarse_basis, onehot)
    precond = precondition(
        resid, coarse_total, weights, local_inverse, coarse_basis, coarse_inverse, onehot, routes
    )
    resid_dot = global_dot(resid, precond, weights)
    direction = precond
    solution = jnp.zeros_like(loads)
    for iteration in range(ITERS):
        product = apply_blocks(schur, direction)
        curvature_local = jnp.sum(direction * product, axis=(0, 1, 3))
        image = assemble(product, routes)
        curvature = lax.psum(curvature_local, ("grp", "sub"))
        step_size = resid_dot / curvature
        solution = solution + step_size[None, None, :, None] * direction
        resid = resid - step_size[None, None, :, None] * image
        coarse_total = coarse_sum(resid, weights, coarse_basis, onehot)
        precond = precondition(
            resid,
            coarse_total,
            weights,
            local_inverse,
            coarse_basis,
            coarse_inverse,
            onehot,
            routes,
        )
        if iteration + 1 < ITERS:
            dot_next = global_dot(resid, precond, weights)
            direction = precond + (dot_next / resid_dot)[None, None, :, None] * direction
            resid_dot = dot_next
    return (solution, precond)


def solution(mesh):
    in_specs = (
        P(("grp", "sub"), None, None, None),
        P(("grp", "sub"), None, None),
        P(("grp", "sub"), None, None),
        P(("grp", "sub"), None, None, None),
        P("sub", None),
        P(("grp", "sub"), None),
        P(("grp", "sub"), None),
        P(("grp", "sub"), None),
    )
    out_specs = (P(("grp", "sub"), None, None, None), P(("grp", "sub"), None, None, None))
    return jax.shard_map(local, mesh=mesh, in_specs=in_specs, out_specs=out_specs, check_vma=False)
```

profile of v0, /device:TPU:1, one launch (start us, length us, event | category | flops | bytes accessed | tf_op | source)
XLA Modules:
  0.0 882.7 jit_solution(7072367132781546228)
XLA Ops:
  12.1 8.6 all-to-all-start
  21.6 3.5 collective-permute-start.1
  28.0 8.9 %copy.223 = bf16[512,8,8,128]{3,2,1,0:T(8,128)(2,1)} copy(bf16[512,8,8,128]{3,1,2,0:T(8,128)(2,1)} %bitcast.226) | data formatting | bytes 16777216
  40.2 5.0 fusion.22
  45.2 138.9 %all-reduce.5.cloned.1.call-done = f32[2048,32]{0,1:T(8,128)} async-done(((f32[2048,32]{0,1:T(8,128)}), f32[2048,32]{0,1:T(8,128)}) %all-reduce.5.cloned.1.call-update) | async-done | bytes 262160 | tf_op jit(solution)/shard_map/psum | solution.py:82
  185.6 24.1 %all-gather = f32[32,64,32]{1,2,0:T(8,128)S(1)} all-gather(f32[1,64,32]{1,2,0:T(8,128)S(1)} %convolution_bitcast_fusion.7), channel_id=1, replica_groups=mesh['grp'=4,'sub'=32] {'sub'}, dimensions={0}, use_global_device_ids=true | all-gather | bytes 270336 | tf_op jit(solution)/shard_map/all_gather | solution.py:91
  213.1 4.6 all-to-all-start.1
  219.0 8.8 copy.224
  227.8 4.2 collective-permute-start.3
  237.2 5.7 fusion.35
  244.9 6.8 all-to-all-start.2
  253.1 5.0 collective-permute-done.4
  258.7 3.0 collective-permute-start.5
  261.8 65.6 %all-reduce = (f32[32]{0:T(128)S(1)}, f32[32]{0:T(128)S(1)}) all-reduce(f32[32]{0:T(128)} %get-tuple-element.21, f32[32]{0:T(128)} %get-tuple-element.30), channel_id=1, replica_groups=mesh['grp'=4,'sub'=32] {'grp','sub'}, use_global_device_ids=true, to_apply=%region_6.7 | all-reduce | flops 64 | bytes 512 | tf_op jit(solution)/shard_map/psum | solution.py:86
  332.1 5.0 fusion.16
  337.1 133.3 %all-reduce.7.cloned.1.call-done = f32[2048,32]{0,1:T(8,128)} async-done(((f32[2048,32]{0,1:T(8,128)}), f32[2048,32]{0,1:T(8,128)}) %all-reduce.7.cloned.1.call-update) | async-done | bytes 262160 | tf_op jit(solution)/shard_map/psum | solution.py:82
  471.8 24.1 %all-gather.1 = f32[32,64,32]{1,2,0:T(8,128)S(1)} all-gather(f32[1,64,32]{1,2,0:T(8,128)S(1)} %convolution_bitcast_fusion.4), channel_id=1, replica_groups=mesh['grp'=4,'sub'=32] {'sub'}, dimensions={0}, use_global_device_ids=true | all-gather | bytes 270336 | tf_op jit(solution)/shard_map/all_gather | solution.py:91
  499.3 4.6 all-to-all-start.3
  505.3 4.1 collective-permute-done.6
  514.7 6.5 all-to-all-done.3
  524.7 63.3 %psum.53 = f32[32]{0:T(128)S(1)} all-reduce(f32[32]{0:T(128)S(1)} %multiply_reduce_fusion), channel_id=1, replica_groups=mesh['grp'=4,'sub'=32] {'grp','sub'}, use_global_device_ids=true, to_apply=%region_11.12 | all-reduce | flops 32 | bytes 256 | tf_op jit(solution)/shard_map/psum | solution.py:86
  589.7 5.6 fusion.34
  598.1 4.7 all-to-all-start.4
  605.0 4.1 collective-permute-done.8
  612.7 65.8 %psum.54 = f32[32]{0:T(128)S(1)} all-reduce(f32[32]{0:T(128)} %get-tuple-element.32), channel_id=1, replica_groups=mesh['grp'=4,'sub'=32] {'grp','sub'}, use_global_device_ids=true, to_apply=%region_13.14 | all-reduce | flops 32 | bytes 256 | tf_op jit(solution)/shard_map/psum | solution.py:133
  685.6 5.1 fusion.19
  690.6 133.1 %all-reduce.9.cloned.1.call-done = f32[2048,32]{0,1:T(8,128)} async-done(((f32[2048,32]{0,1:T(8,128)}), f32[2048,32]{0,1:T(8,128)}) %all-reduce.9.cloned.1.call-update) | async-done | bytes 262160 | tf_op jit(solution)/shard_map/psum | solution.py:82
  825.2 24.1 %all-gather.2 = f32[32,64,32]{1,2,0:T(8,128)S(1)} all-gather(f32[1,64,32]{1,2,0:T(8,128)S(1)} %convolution_bitcast_fusion.1), channel_id=1, replica_groups=mesh['grp'=4,'sub'=32] {'sub'}, dimensions={0}, use_global_device_ids=true | all-gather | bytes 270336 | tf_op jit(solution)/shard_map/all_gather | solution.py:91
  852.7 4.6 all-to-all-start.5
  858.6 4.1 collective-permute-done.10
  862.7 2.7 collective-permute-start.11
  867.3 7.2 all-to-all-done.5
  (155 shorter events, 73.8 us)
Async XLA Ops:
  7.2 176.9 %copy-start = (f32[64,2048]{1,0:T(8,128)S(1)}, f32[64,2048]{1,0:T(8,128)}, u32[]{:S(2)}) copy-start(f32[64,2048]{1,0:T(8,128)} %param.12) | copy-start | bytes 1572868
  9.2 27.7 %copy-start.11 = (s32[1024]{0:T(1024)}, s32[1024]{0:T(1024)S(1)}, u32[]{:S(2)}) copy-start(s32[1024]{0:T(1024)S(1)} %pad_clamp_fusion.1) | copy-start | bytes 12292
  12.1 25.8 %all-to-all-start = ((f32[64,32,128]{2,1,0:T(8,128)}), f32[64,32,128]{2,1,0:T(8,128)S(1)}, u32[]{:S(2)}, u32[]{:S(2)}) async-start(f32[64,32,128]{2,1,0:T(8,128)} %broadcast_select_fusion.5), calls=%async_computation | async-start | bytes 2097152 | tf_op jit(solution)/shard_map/all_to_all | solution.py:50
  20.7 163.4 %all-reduce.5.cloned.1.call-start = ((), (), s32[]{:S(2)}) async-start(), calls=%async_computation.6 | async-start | bytes 524288 | tf_op jit(solution)/shard_map/psum | solution.py:82
  21.6 15.3 %collective-permute-start.1 = (f32[1,4,32,128]{3,2,1,0:T(8,128)S(1)}, f32[1,4,32,128]{3,2,1,0:T(8,128)S(1)}, u32[]{:S(2)}, u32[]{:S(2)}) collective-permute-start(f32[1,4,32,128]{3,2,1,0:T(8,128)S(1)} %get-tuple-element.27), channel_id=1, source_target_pairs={{0,32},{32,64},{64,96},{1,33},{33,65},{65,97},{2,34},{34,66},{66,9... | collective-permute-start | bytes 196616 | tf_op jit(solution)/shard_map/ppermute | solution.py:19
  25.2 11.8 %collective-permute-start = (f32[1,4,32,128]{3,2,1,0:T(8,128)S(1)}, f32[1,4,32,128]{3,2,1,0:T(8,128)S(1)}, u32[]{:S(2)}, u32[]{:S(2)}) collective-permute-start(f32[1,4,32,128]{3,2,1,0:T(8,128)S(1)} %get-tuple-element.26), channel_id=1, source_target_pairs={{32,0},{64,32},{96,64},{33,1},{65,33},{97,65},{34,2},{66,34},{98,6... | collective-permute-start | bytes 196616 | tf_op jit(solution)/shard_map/ppermute | solution.py:20
  28.0 8.9 %copy-start.10 = (s32[4,8]{1,0:T(4,128)S(1)}, s32[4,8]{1,0:T(4,128)}, u32[]{:S(2)}) copy-start(s32[4,8]{1,0:T(4,128)} %param.14) | copy-start | bytes 388
  28.0 8.9 %copy-start.2 = (f32[4,8,32,128]{3,2,1,0:T(8,128)S(1)}, f32[4,8,32,128]{3,2,1,0:T(8,128)}, u32[]{:S(2)}) copy-start(f32[4,8,32,128]{3,2,1,0:T(8,128)} %param.8) | copy-start | bytes 1572868
  28.0 10.5 %copy-start.1 = (f32[4,8,8,128]{3,2,1,0:T(8,128)S(1)}, f32[4,8,8,128]{3,2,1,0:T(8,128)}, u32[]{:S(2)}) copy-start(f32[4,8,8,128]{3,2,1,0:T(8,128)} %param.11) | copy-start | bytes 393220
  36.9 198.0 %copy-start.12 = (s32[1024]{0:T(1024)}, s32[1024]{0:T(1024)S(1)}, u32[]{:S(2)}) copy-start(s32[1024]{0:T(1024)S(1)} %pad_clamp_fusion) | copy-start | bytes 12292
  37.0 174.2 %copy-start.6 = (f32[4,1,32,128]{3,2,1,0:T(8,128)}, f32[4,1,32,128]{3,2,1,0:T(8,128)S(1)}, u32[]{:S(2)}) copy-start(f32[4,1,32,128]{3,2,1,0:T(8,128)S(1)} %bitcast_add_fusion.11) | copy-start | bytes 196612
  37.0 174.2 %copy-start.8 = (f32[4,1,32,128]{3,2,1,0:T(8,128)}, f32[4,1,32,128]{3,2,1,0:T(8,128)S(1)}, u32[]{:S(2)}) copy-start(f32[4,1,32,128]{3,2,1,0:T(8,128)S(1)} %fusion.68) | copy-start | bytes 196612
  213.1 21.8 %all-to-all-start.1 = ((f32[64,32,128]{2,1,0:T(8,128)}), f32[64,32,128]{2,1,0:T(8,128)S(1)}, u32[]{:S(2)}, u32[]{:S(2)}) async-start(f32[64,32,128]{2,1,0:T(8,128)} %broadcast_select_fusion.4), calls=%async_computation.1 | async-start | bytes 2097152 | tf_op jit(solution)/shard_map/all_to_all | solution.py:50
  217.7 14.3 %collective-permute-start.2 = (f32[1,4,32,128]{3,2,1,0:T(8,128)S(1)}, f32[1,4,32,128]{3,2,1,0:T(8,128)S(1)}, u32[]{:S(2)}, u32[]{:S(2)}) collective-permute-start(f32[1,4,32,128]{3,2,1,0:T(8,128)S(1)} %get-tuple-element.24), channel_id=1, source_target_pairs={{32,0},{64,32},{96,64},{33,1},{65,33},{97,65},{34,2},{66,34},{98,6... | collective-permute-start | bytes 196616 | tf_op jit(solution)/shard_map/ppermute | solution.py:20
  227.8 5.3 collective-permute-start.3
  237.2 92.1 %copy-start.7 = (f32[4,1,32,128]{3,2,1,0:T(8,128)S(1)}, f32[4,1,32,128]{3,2,1,0:T(8,128)}, u32[]{:S(2)}) copy-start(f32[4,1,32,128]{3,2,1,0:T(8,128)} %copy-done.6) | copy-start | bytes 196612
  237.2 92.1 %copy-start.9 = (f32[4,1,32,128]{3,2,1,0:T(8,128)S(1)}, f32[4,1,32,128]{3,2,1,0:T(8,128)}, u32[]{:S(2)}) copy-start(f32[4,1,32,128]{3,2,1,0:T(8,128)} %copy-done.8) | copy-start | bytes 196612
  244.9 83.7 %all-to-all-start.2 = ((f32[64,32,128]{2,1,0:T(8,128)}), f32[64,32,128]{2,1,0:T(8,128)S(1)}, u32[]{:S(2)}, u32[]{:S(2)}) async-start(f32[64,32,128]{2,1,0:T(8,128)} %broadcast_select_fusion.3), calls=%async_computation.2 | async-start | bytes 2097152 | tf_op jit(solution)/shard_map/all_to_all | solution.py:50
  251.7 218.7 %all-reduce.7.cloned.1.call-start = ((), (), s32[]{:S(2)}) async-start(), calls=%async_computation.7 | async-start | bytes 524288 | tf_op jit(solution)/shard_map/psum | solution.py:82
  251.8 6.3 collective-permute-start.4
  258.7 69.3 %collective-permute-start.5 = (f32[1,4,32,128]{3,2,1,0:T(8,128)S(1)}, f32[1,4,32,128]{3,2,1,0:T(8,128)S(1)}, u32[]{:S(2)}, u32[]{:S(2)}) collective-permute-start(f32[1,4,32,128]{3,2,1,0:T(8,128)S(1)} %get-tuple-element.23), channel_id=1, source_target_pairs={{0,32},{32,64},{64,96},{1,33},{33,65},{65,97},{2,34},{34,66},{66,9... | collective-permute-start | bytes 196616 | tf_op jit(solution)/shard_map/ppermute | solution.py:19
  499.3 21.8 %all-to-all-start.3 = ((f32[64,32,128]{2,1,0:T(8,128)}), f32[64,32,128]{2,1,0:T(8,128)S(1)}, u32[]{:S(2)}, u32[]{:S(2)}) async-start(f32[64,32,128]{2,1,0:T(8,128)} %broadcast_select_fusion.2), calls=%async_computation.3 | async-start | bytes 2097152 | tf_op jit(solution)/shard_map/all_to_all | solution.py:50
  504.0 5.4 collective-permute-start.6
  510.0 4.1 collective-permute-start.7
  598.1 83.1 %all-to-all-start.4 = ((f32[64,32,128]{2,1,0:T(8,128)}), f32[64,32,128]{2,1,0:T(8,128)S(1)}, u32[]{:S(2)}, u32[]{:S(2)}) async-start(f32[64,32,128]{2,1,0:T(8,128)} %broadcast_select_fusion.1), calls=%async_computation.4 | async-start | bytes 2097152 | tf_op jit(solution)/shard_map/all_to_all | solution.py:50
  602.8 220.9 %all-reduce.9.cloned.1.call-start = ((), (), s32[]{:S(2)}) async-start(), calls=%async_computation.8 | async-start | bytes 524288 | tf_op jit(solution)/shard_map/psum | solution.py:82
  603.7 5.3 collective-permute-start.8
  610.5 69.2 %collective-permute-start.9 = (f32[1,4,32,128]{3,2,1,0:T(8,128)S(1)}, f32[1,4,32,128]{3,2,1,0:T(8,128)S(1)}, u32[]{:S(2)}, u32[]{:S(2)}) collective-permute-start(f32[1,4,32,128]{3,2,1,0:T(8,128)S(1)} %get-tuple-element.17), channel_id=1, source_target_pairs={{0,32},{32,64},{64,96},{1,33},{33,65},{65,97},{2,34},{34,66},{66,9... | collective-permute-start | bytes 196616 | tf_op jit(solution)/shard_map/ppermute | solution.py:19
  690.6 174.8 %copy-start.13 = (f32[32]{0:T(128)S(1)}, f32[32]{0:T(128)}, u32[]{:S(2)}) copy-start(f32[32]{0:T(128)} %div.41) | copy-start | bytes 388
  852.7 21.8 %all-to-all-start.5 = ((f32[64,32,128]{2,1,0:T(8,128)}), f32[64,32,128]{2,1,0:T(8,128)S(1)}, u32[]{:S(2)}, u32[]{:S(2)}) async-start(f32[64,32,128]{2,1,0:T(8,128)} %broadcast_select_fusion), calls=%async_computation.5 | async-start | bytes 2097152 | tf_op jit(solution)/shard_map/all_to_all | solution.py:50
  857.3 5.4 collective-permute-start.10
  862.7 4.6 collective-permute-start.11
  (5 other events, 12.0 us)
Sparse Core Ops, SparseCore 0:
  40.3 143.7 all-reduce.4
  332.2 138.0 all-reduce.6
  685.7 137.9 all-reduce.8
where the time goes:
time: 885 us; the launch traced here: 883 us
  waiting for transfers between devices  441 us (50%)
  blocking collectives  267 us (30%)
  starting transfers between devices  60.2 us (7%)
  matrix products  39.6 us (4%)
  local copies, waits for them, and re-layouts  36.1 us (4%)
  other arithmetic  24.3 us (3%)
  between operations  14.5 us (2%)
    psum x3, waiting for transfers between devices, coarse_sum(): lax.psum(coarse_part(field, weights, coarse_basis, onehot), ('grp', 'sub'))  405 us
    psum x2, blocking collectives, global_dot(): lax.psum(jnp.sum(weights * resid * precond, axis=(0, 1, 3)), ('grp', 'sub'))  129 us
    all_gather x3, blocking collectives, coarse_solve(): return lax.all_gather(piece, 'sub', axis=0, tiled=True)  72.3 us
    psum x1, blocking collectives, local(): curvature = lax.psum(curvature_local, ('grp', 'sub'))  65.8 us
    all_to_all x6, starting transfers between devices, assemble(): lax.all_to_all(outgoing, 'sub', split_axis=0, concat_axis=0, tiled=True)  34 us
    dot_general x5, matrix products, apply_blocks(): jnp.einsum('sbrk,sbkcl->scrl', field.astype(jnp.bfloat16), shaped, prefer...  26.3 us
    unnamed x38, local copies, waits for them, and re-layouts  19.8 us
    ppermute x6, starting transfers between devices, extended(): before = lax.ppermute(last, axis, up)  18.4 us
  transfers between devices with their start and end apart: 21, of which 13 were waited for; matrix products, arithmetic and copies ran while one was open for 5% of the time, Pallas kernels for 0%

commit v1 on v0

v1 whole, which is shorter than its diff:
```python
import functools

import jax
import jax.numpy as jnp
from jax import lax
from jax.experimental import pallas as pl
from jax.experimental.pallas import tpu as pltpu
from jax.sharding import PartitionSpec as P

AXES = ("grp", "sub")
PRECISE = lax.Precision.HIGHEST
F32 = jnp.float32
BF16 = jnp.bfloat16
SMEM = pl.BlockSpec(memory_space=pltpu.SMEM)
VMEM = pl.BlockSpec(memory_space=pltpu.VMEM)
HBM = pl.BlockSpec(memory_space=pltpu.HBM)
VMEM_LIMIT = 60 * 1024 * 1024


def shape(dims, dtype=F32):
    return jax.ShapeDtypeStruct(dims, dtype)


def params():
    return pltpu.CompilerParams(vmem_limit_bytes=VMEM_LIMIT)


def cost(flops, moved):
    return pl.CostEstimate(flops=flops, bytes_accessed=moved, transcendentals=0)


def face_routes(nbr_sub, nbr_block, peer_count, capacity):
    subs, blocks = nbr_sub.shape
    face_count = blocks - 2
    shared = lax.broadcasted_iota(jnp.int32, nbr_sub.shape, 1) < face_count
    place = lax.broadcasted_iota(jnp.int32, nbr_sub.shape, 0) * face_count
    place = place + lax.broadcasted_iota(jnp.int32, nbr_sub.shape, 1)
    peer = jnp.where(shared, nbr_sub // subs % peer_count, -1)
    partner_place = nbr_sub % subs * face_count + nbr_block
    same = (peer[:, :, None, None] == peer[None, None]) & shared[None, None]

    def rank(order):
        return jnp.sum(same & (order[None, None] < order[:, :, None, None]), axis=(2, 3))

    first = jnp.maximum(peer, 0) * capacity
    return (first + rank(place), first + rank(partner_place))


def weight(nbr, s, b):
    return jnp.where(nbr[s, b] >= 0, 0.5, 1.0).astype(F32)


def split(x):
    high = x.astype(BF16)
    return high, (x - high.astype(F32)).astype(BF16)


def dotted(a, b):
    return lax.dot_general(a, b, (((1,), (0,)), ((), ())), preferred_element_type=F32)


def three_part(both, other):
    product = dotted(both, other)
    rows, columns = product.shape[0] // 2, product.shape[1] // 2
    return product[:rows, :columns] + product[:rows, columns:] + product[rows:, :columns]


def slot_of(buffer, slot, cases, capacity):
    start = pl.multiple_of(lax.rem(slot, capacity) * cases, cases)
    return buffer.at[lax.div(slot, capacity), pl.ds(start, cases)]


def sends(source, slots, capacity, outgoing, sems, s):
    faces = source.shape[1] - 2
    cases = source.shape[2]
    return [
        pltpu.make_async_copy(
            source.at[s, b], slot_of(outgoing, slots[s, b], cases, capacity), sems.at[s, b]
        )
        for b in range(faces)
    ]


def rims(source, upward, downward, sems):
    faces = source.shape[1] - 2
    return [
        pltpu.make_async_copy(source.at[:, faces], upward, sems.at[0, faces]),
        pltpu.make_async_copy(source.at[:, faces + 1], downward, sems.at[0, faces + 1]),
    ]


def fetches(landing, slots, capacity, incoming, before, after, sems):
    subs, blocks, cases = landing.shape[:3]
    faces = blocks - 2
    copies = [
        [
            pltpu.make_async_copy(
                slot_of(incoming, slots[s, b], cases, capacity), landing.at[s, b], sems.at[s, b]
            )
            for b in range(faces)
        ]
        for s in range(subs)
    ]
    copies.append(
        [
            pltpu.make_async_copy(after, landing.at[:, faces], sems.at[0, faces]),
            pltpu.make_async_copy(before, landing.at[:, faces + 1], sems.at[0, faces + 1]),
        ]
    )
    return copies


def start_all(copies):
    for copy in copies:
        copy.start()
    return copies


def wait_all(copies):
    for copy in copies:
        copy.wait()


def pack_kernel(
    capacity, slots, primal, loads, outgoing, upward, downward, index_row, tall, sems, row_sem
):
    subs, blocks, cases, width = loads.shape
    coarse = primal.shape[1]
    copies = start_all(rims(loads, upward, downward, sems))
    for s in range(subs):
        copies += start_all(sends(loads, slots, capacity, outgoing, sems, s))
    lane = lax.broadcasted_iota(jnp.int32, (1, width), 1)
    row = jnp.zeros((1, width), jnp.int32)
    for s in range(subs):
        for c in range(coarse):
            row = jnp.where(lane == s * coarse + c, primal[s, c], row)
    row = row.astype(F32)
    index_row[...] = row
    tall[...] = jnp.broadcast_to(row[None], tall.shape)
    rows = outgoing.at[:, pl.ds(capacity * cases, tall.shape[1])]
    copies += start_all([pltpu.make_async_copy(tall, rows, row_sem)])
    wait_all(copies)


def project_kernel(
    dot_count, capacity, nbr, slots, incoming, before, after, base, basis, *rest
):
    dots = rest[:dot_count]
    field, message, landing, parts, tall, sems = rest[dot_count:]
    subs, blocks, cases, width = base.shape
    lanes = subs * cases
    copies = fetches(landing, slots, capacity, incoming, before, after, sems)
    for group in copies:
        start_all(group)
    wait_all(copies[subs])
    for s in range(subs):
        wait_all(copies[s])
        for b in range(blocks):
            value = weight(nbr, s, b) * (base[s, b] + landing[s, b])
            field[s, b] = value
            high, low = split(value)
            parts[s * cases : (s + 1) * cases, b * width : (b + 1) * width] = high
            parts[lanes + s * cases : lanes + (s + 1) * cases, b * width : (b + 1) * width] = low
    primal = basis.shape[0] // 4
    product = lax.dot_general(
        basis[: 2 * primal], parts[...], (((1,), (1,)), ((), ())), preferred_element_type=F32
    )
    product = product[:primal, :lanes] + product[:primal, lanes:] + product[primal:, :lanes]
    coarse = primal // subs
    lane = lax.broadcasted_iota(jnp.int32, (coarse, lanes), 1) // cases
    block = jnp.zeros((coarse, lanes), F32)
    for s in range(subs):
        block = jnp.where(lane == s, product[s * coarse : (s + 1) * coarse], block)
    if dots[0].shape[0] == 1:
        row = dots[0][...]
    else:
        tall[...] = jnp.zeros_like(tall)
        place = 0
        for part in dots:
            tall[place : place + part.shape[0]] = part[...]
            place += part.shape[0]
        row = jnp.sum(tall[...].T, axis=0, keepdims=True)
    period = coarse + 1
    for p in range(message.shape[0] // period):
        message[p * period : p * period + coarse] = block
        message[p * period + coarse : (p + 1) * period] = row


def applied(flat, matrix, fine):
    if not fine:
        return dotted(flat.astype(BF16), matrix)
    both = dotted(jnp.concatenate(split(flat), axis=0), matrix)
    return both[: flat.shape[0]] + both[flat.shape[0] :]


def inverse_kernel(fine, field, matrix, out, held, sems):
    subs, blocks, cases, width = field.shape
    copies = start_all(
        [pltpu.make_async_copy(matrix.at[s], held.at[s], sems.at[s]) for s in range(subs)]
    )
    for s in range(subs):
        flat = jnp.concatenate([field[s, b] for b in range(blocks)], axis=1)
        copies[s].wait()
        product = applied(flat, held[s], fine)
        for b in range(blocks):
            out[s, b] = product[:, b * width : (b + 1) * width]


def folded(product, primal):
    size = product.shape[0]
    turned = product.T
    row = lax.broadcasted_iota(jnp.int32, (size, size), 0) // primal
    lane = lax.broadcasted_iota(jnp.int32, (size, size), 1) // primal
    kept = jnp.where(row == lane, turned, 0.0)
    total = kept[:primal]
    for q in range(1, size // primal):
        total = total + kept[q * primal : (q + 1) * primal]
    out = total
    for q in range(1, size // primal):
        out = out + pltpu.roll(total, q * primal, 1)
    return out


def spread(picked, basis, subs, coarse):
    cases, lanes = picked.shape
    high = picked.astype(BF16).astype(F32)
    lane = lax.broadcasted_iota(jnp.int32, (cases, lanes), 1)
    parts = jnp.where(lane < lanes // 2, high, picked - high)
    owner = lane // coarse % subs
    tall = jnp.concatenate(
        [jnp.where(owner == s, parts, 0.0) for s in range(subs)], axis=0
    ).astype(BF16)
    return dotted(tall, basis[...])


def first_kernel(
    capacity, nbr, slots, columns, totals, basis, local_part, field,
    corrected, dots, outgoing, upward, downward, weighted, sems,
):
    subs, blocks, cases, width = field.shape
    primal = basis.shape[0] // 4
    high, low = split(columns[...].T)
    total_high, total_low = split(totals[...])
    product = three_part(
        jnp.concatenate([high, low], axis=0), jnp.concatenate([total_high, total_low], axis=1)
    )
    coarse_part = spread(folded(product, primal), basis, subs, primal // subs)
    dot = jnp.zeros((cases, width), F32)
    copies = []
    for s in range(subs):
        for b in range(blocks):
            value = local_part[s, b] + coarse_part[
                s * cases : (s + 1) * cases, b * width : (b + 1) * width
            ]
            corrected[s, b] = value
            weighted[s, b] = weight(nbr, s, b) * value
            dot = dot + field[s, b] * value
        copies += start_all(sends(weighted, slots, capacity, outgoing, sems, s))
    copies += start_all(rims(weighted, upward, downward, sems))
    dots[...] = dot
    wait_all(copies)


def everyone(landed, period):
    value = landed[...]
    row = lax.broadcasted_iota(jnp.int32, value.shape, 0)
    sums = lax.rem(row, period) == period - 1
    totals = jnp.sum(jnp.where(sums, value, 0.0), axis=0, keepdims=True)
    totals = jnp.broadcast_to(totals, (value.shape[1], value.shape[1])).T
    high, low = split(jnp.where(sums, 0.0, value))
    return totals, jnp.concatenate([high, low], axis=1)


def second_kernel(
    capacity, nbr, slots, landed, responses, basis, local_part, corrected, field, image,
    direction_part, out, dots, scalars, outgoing, upward, downward, weighted, sems,
):
    subs, blocks, cases, width = field.shape
    primal = basis.shape[0] // 4
    coarse = primal // subs
    totals, rows = everyone(landed, coarse + 1)
    dot0 = totals[:cases]
    curv0 = totals[cases : 2 * cases]
    alpha = dot0 / curv0
    scalars[0] = dot0
    scalars[1] = curv0
    scalars[2] = alpha
    product = three_part(responses[...], rows)
    coarse_part = spread(folded(product, primal), basis, subs, coarse)
    dot = jnp.zeros((cases, width), F32)
    copies = []
    for s in range(subs):
        for b in range(blocks):
            step = local_part[s, b] + coarse_part[
                s * cases : (s + 1) * cases, b * width : (b + 1) * width
            ]
            direction_part[s, b] = step
            value = corrected[s, b] - alpha * step
            out[s, b] = value
            weighted[s, b] = weight(nbr, s, b) * value
            dot = dot + (field[s, b] - alpha * image[s, b]) * value
        copies += start_all(sends(weighted, slots, capacity, outgoing, sems, s))
    copies += start_all(rims(weighted, upward, downward, sems))
    dots[...] = dot
    wait_all(copies)


def third_kernel(
    capacity, nbr, slots, landed, responses, basis, local_part, direction_part, corrected, scalars,
    weighted, factors, outgoing, upward, downward, sems,
):
    subs, blocks, cases, width = corrected.shape
    primal = basis.shape[0] // 4
    coarse = primal // subs
    totals, rows = everyone(landed, coarse + 1)
    dot1 = totals[:cases]
    own = totals[cases : 2 * cases]
    cross = totals[2 * cases : 3 * cases]
    beta = dot1 / scalars[0]
    curv1 = own + beta * (cross + beta * scalars[1])
    alpha = dot1 / curv1
    factors[0] = scalars[2] + alpha * beta
    factors[1] = alpha
    product = three_part(responses[...], rows)
    coarse_part = spread(folded(product, primal), basis, subs, coarse)
    copies = []
    for s in range(subs):
        for b in range(blocks):
            step = local_part[s, b] + coarse_part[
                s * cases : (s + 1) * cases, b * width : (b + 1) * width
            ]
            value = corrected[s, b] - alpha * (step + beta * direction_part[s, b])
            weighted[s, b] = weight(nbr, s, b) * value
        copies += start_all(sends(weighted, slots, capacity, outgoing, sems, s))
    copies += start_all(rims(weighted, upward, downward, sems))
    wait_all(copies)


def schur_kernel(
    older, capacity, nbr, send_slots, recv_slots, incoming, before, after, matrix, corrected, *rest
):
    if older:
        old_direction, old_product = rest[:2]
        rest = rest[2:]
    direction, product, dots, outgoing, upward, downward, landing, held, sems, held_sems = rest
    subs, blocks, cases, width = corrected.shape
    copies = fetches(landing, recv_slots, capacity, incoming, before, after, sems)
    loads = [pltpu.make_async_copy(matrix.at[s], held.at[s], held_sems.at[s]) for s in range(subs)]
    loads[0].start()
    for group in copies:
        start_all(group)
    start_all(loads[1:])
    wait_all(copies[subs])
    own = jnp.zeros((cases, width), F32)
    cross = jnp.zeros((cases, width), F32)
    out = []
    for s in range(subs):
        wait_all(copies[s])
        flat = []
        for b in range(blocks):
            value = weight(nbr, s, b) * corrected[s, b] + landing[s, b]
            direction[s, b] = value
            flat.append(value)
        flat = jnp.concatenate(flat, axis=1)
        loads[s].wait()
        both = applied(flat, held[s], older)
        for b in range(blocks):
            piece = both[:, b * width : (b + 1) * width]
            product[s, b] = piece
            own = own + direction[s, b] * piece
            if older:
                cross = cross + direction[s, b] * old_product[s, b] + old_direction[s, b] * piece
        out += start_all(sends(product, send_slots, capacity, outgoing, sems, s))
    out += start_all(rims(product, upward, downward, sems))
    dots[0:cases] = own
    if older:
        dots[cases:] = cross
    wait_all(out)


def last_kernel(capacity, slots, incoming, before, after, base, out, landing, sems):
    subs, blocks = base.shape[:2]
    copies = fetches(landing, slots, capacity, incoming, before, after, sems)
    for group in copies:
        start_all(group)
    wait_all(copies[subs])
    for s in range(subs):
        wait_all(copies[s])
        for b in range(blocks):
            out[s, b] = base[s, b] + landing[s, b]


def row_numbers(shape, rows_here, groups):
    row = lax.broadcasted_iota(jnp.int32, shape, 0)
    quarter = rows_here // groups
    return row // quarter * rows_here + row % quarter


def totals_kernel(rows_here, index_period, landed, index, totals):
    groups = index.shape[0]
    lanes = landed.shape[1]
    cases = lanes // groups
    period = index_period
    value = landed[...]
    row = lax.broadcasted_iota(jnp.int32, value.shape, 0)
    high, low = split(jnp.where(lax.rem(row, period) == period - 1, 0.0, value))
    rows = jnp.concatenate([high, low], axis=1)
    height = totals.shape[0]
    number = row_numbers((height, landed.shape[0]), rows_here, groups)
    lane = lax.broadcasted_iota(jnp.int32, (height, lanes), 1) // cases
    out = jnp.zeros((height, lanes), F32)
    for a in range(groups):
        gathered = jnp.zeros((height, lanes), F32)
        for q in range(groups):
            chosen = number == index[q : q + 1, :] - a * (rows_here // groups)
            product = dotted(jnp.where(chosen, 1.0, 0.0).astype(BF16), rows)
            gathered = jnp.where(lane == q, product[:, :lanes] + product[:, lanes:], gathered)
        summed = gathered
        for q in range(1, groups):
            summed = summed + pltpu.roll(gathered, q * cases, 1)
        out = jnp.where(lane == a, summed, out)
    totals[...] = out


def responses_kernel(rows_here, columns, index, responses):
    groups = index.shape[0]
    lanes = columns.shape[1]
    primal = lanes // groups
    high, low = split(columns[...].T)
    number = row_numbers((columns.shape[0], index.shape[1]), rows_here, groups)
    for q in range(groups):
        total = jnp.zeros((2 * primal, index.shape[1]), F32)
        for a in range(groups):
            chosen = number == index[q : q + 1, :] - a * (rows_here // groups)
            both = jnp.concatenate(
                [high[a * primal : (a + 1) * primal], low[a * primal : (a + 1) * primal]], axis=0
            )
            total = total + dotted(both, jnp.where(chosen, 1.0, 0.0).astype(BF16))
        responses[q * primal : (q + 1) * primal] = total[:primal].astype(BF16)
        responses[lanes + q * primal : lanes + (q + 1) * primal] = total[primal:].astype(BF16)


def all_to_all(block, axes):
    return lax.all_to_all(block, axes, split_axis=0, concat_axis=0, tiled=True)


def local(
    loads, schur, local_inverse, coarse_basis, coarse_inverse, primal_index, nbr_sub, nbr_block
):
    subs, blocks, cases, width = loads.shape
    coarse = primal_index.shape[1]
    primal = subs * coarse
    groups = subs
    faces = blocks - 2
    peers = lax.axis_size("sub")
    slabs = lax.axis_size("grp")
    devices = peers * slabs
    rows_here, prim_count = coarse_inverse.shape
    capacity = max(2, (subs * faces + peers - 2) // (peers - 1))
    period = coarse + 1
    size = blocks * width
    field_shape = loads.shape
    rim = (subs, cases, width)
    slot_shape = (peers, capacity * cases, width)
    face_sems = pltpu.SemaphoreType.DMA((subs, blocks))
    held_scratch = [pltpu.VMEM((subs, size, size), BF16), pltpu.SemaphoreType.DMA((subs,))]
    field_bytes = 4 * subs * blocks * cases * width
    matrix_bytes = 2 * subs * size * size
    matrix_flops = 4 * subs * cases * size * size

    send_slots, recv_slots = face_routes(nbr_sub, nbr_block, peers, capacity)
    up = [(i, i + 1) for i in range(slabs - 1)]
    down = [(j, i) for i, j in up]

    def exchange(outgoing, upward, downward):
        incoming = all_to_all(outgoing, "sub")
        before = lax.ppermute(upward, "grp", up)
        after = lax.ppermute(downward, "grp", down)
        return incoming, before, after

    def gather_rows(message):
        message = message.reshape(devices, period, 1, width)
        return all_to_all(message, AXES).reshape(devices * period, width)

    *packed, index_row = pl.pallas_call(
        functools.partial(pack_kernel, capacity),
        out_shape=(
            shape((peers, capacity * cases + 8, width)), shape(rim), shape(rim),
            shape((1, width)),
        ),
        in_specs=[SMEM, SMEM, VMEM],
        out_specs=(HBM, HBM, HBM, VMEM),
        scratch_shapes=[
            pltpu.VMEM((peers, 8, width), F32), face_sems, pltpu.SemaphoreType.DMA(())
        ],
        compiler_params=params(),
        cost_estimate=cost(0, 2 * field_bytes),
        name="pack",
    )(send_slots, primal_index, loads)
    incoming, before, after = exchange(*packed)
    slab_index = incoming[:, capacity * cases, :primal].astype(jnp.int32).reshape(-1)

    flat_basis = coarse_basis.reshape(primal, size)
    basis_high = lax.reduce_precision(flat_basis, 8, 7)
    basis_low = flat_basis - basis_high
    basis = jnp.concatenate([basis_high, basis_low, basis_high, basis_low], axis=0).astype(BF16)

    def project(incoming, base, before, after, dots):
        return pl.pallas_call(
            functools.partial(project_kernel, len(dots), capacity),
            out_shape=(shape(field_shape), shape((devices * period, width))),
            in_specs=[SMEM, SMEM] + [HBM] * 3 + [VMEM] * (2 + len(dots)),
            out_specs=(VMEM, VMEM),
            scratch_shapes=[
                pltpu.VMEM(field_shape, F32),
                pltpu.VMEM((2 * subs * cases, size), BF16),
                pltpu.VMEM((width, width), F32),
                face_sems,
            ],
            compiler_params=params(),
            cost_estimate=cost(8 * primal * subs * cases * size, 5 * field_bytes),
            name="project",
        )(nbr_sub, recv_slots, incoming, before, after, base, basis, *dots)

    def inverse(field, fine):
        return pl.pallas_call(
            functools.partial(inverse_kernel, fine),
            out_shape=shape(field_shape),
            in_specs=[VMEM, HBM],
            out_specs=VMEM,
            scratch_shapes=held_scratch,
            compiler_params=params(),
            cost_estimate=cost(matrix_flops, matrix_bytes + 2 * field_bytes),
            name="inverse",
        )(field, local_inverse)

    def apply_schur(incoming, corrected, before, after, old=()):
        count = 2 if old else 1
        return pl.pallas_call(
            functools.partial(schur_kernel, bool(old), capacity),
            out_shape=(
                shape(field_shape), shape(field_shape), shape((count * cases, width)),
                shape(slot_shape), shape(rim), shape(rim),
            ),
            in_specs=[SMEM] * 3 + [HBM] * 4 + [VMEM] * (1 + len(old)),
            out_specs=(VMEM, VMEM, VMEM, HBM, HBM, HBM),
            scratch_shapes=[
                pltpu.VMEM(field_shape, F32), held_scratch[0], face_sems, held_scratch[1]
            ],
            compiler_params=params(),
            cost_estimate=cost(matrix_flops, matrix_bytes + 6 * field_bytes),
            name="schur",
        )(nbr_sub, send_slots, recv_slots, incoming, before, after, schur, corrected, *old)

    sent_shapes = (shape(slot_shape), shape(rim), shape(rim))
    sent_specs = (HBM, HBM, HBM)
    combine_cost = cost(2 * primal * 8 * 128 * size, 8 * field_bytes)

    u0, message = project(incoming, loads, before, after, (index_row,))
    landed = gather_rows(message)

    columns_at = (
        jnp.arange(prim_count, dtype=jnp.int32)[:, None] == slab_index[None, :]
    ).astype(F32)
    asked = jnp.dot(coarse_inverse, columns_at, precision=PRECISE)
    asked = asked.reshape(groups, rows_here // groups, peers, primal).transpose(2, 1, 0, 3)
    asked = asked.reshape(peers, rows_here // groups, groups * primal)
    local0 = inverse(u0, False)
    asked, landed, local0 = lax.optimization_barrier((asked, landed, local0))
    columns = all_to_all(asked, "sub").reshape(-1, groups * primal)

    index = landed.reshape(devices, period, width)[:, coarse, :primal].astype(jnp.int32)
    index = index.reshape(devices, subs, coarse).transpose(1, 0, 2)
    index = jnp.pad(index, ((0, 0), (0, 0), (0, 1)), constant_values=-prim_count)
    index = index.reshape(subs, devices * period)
    height = prim_count // groups
    totals = pl.pallas_call(
        functools.partial(totals_kernel, rows_here, period),
        out_shape=shape((height, width)),
        in_specs=[VMEM, VMEM],
        out_specs=VMEM,
        compiler_params=params(),
        cost_estimate=cost(4 * prim_count * devices * period * groups * width, 2 * field_bytes),
        name="totals",
    )(landed, index)

    c0, dot0_part, *packed = pl.pallas_call(
        functools.partial(first_kernel, capacity),
        out_shape=(shape(field_shape), shape((cases, width))) + sent_shapes,
        in_specs=[SMEM, SMEM] + [VMEM] * 5,
        out_specs=(VMEM, VMEM) + sent_specs,
        scratch_shapes=[pltpu.VMEM(field_shape, F32), face_sems],
        compiler_params=params(),
        cost_estimate=combine_cost,
        name="first",
    )(nbr_sub, send_slots, columns, totals, basis, local0, u0)
    incoming, before, after = exchange(*packed)
    responses = pl.pallas_call(
        functools.partial(responses_kernel, rows_here),
        out_shape=shape((2 * groups * primal, devices * period), BF16),
        in_specs=[VMEM, VMEM],
        out_specs=VMEM,
        compiler_params=params(),
        cost_estimate=cost(4 * primal * prim_count * devices * period * groups, field_bytes),
        name="responses",
    )(columns, index)
    z0, q0, curv0_part, *packed = apply_schur(incoming, c0, before, after)
    incoming, before, after = exchange(*packed)

    v0, message = project(incoming, q0, before, after, (dot0_part, curv0_part))
    landed = gather_rows(message)
    local1 = inverse(v0, True)
    k0, c1, dot1_part, scalars, *packed = pl.pallas_call(
        functools.partial(second_kernel, capacity),
        out_shape=(
            shape(field_shape), shape(field_shape), shape((cases, width)),
            shape((3, cases, width)),
        )
        + sent_shapes,
        in_specs=[SMEM, SMEM] + [VMEM] * 7,
        out_specs=(VMEM,) * 4 + sent_specs,
        scratch_shapes=[pltpu.VMEM(field_shape, F32), face_sems],
        compiler_params=params(),
        cost_estimate=combine_cost,
        name="second",
    )(nbr_sub, send_slots, landed, responses, basis, local1, c0, u0, v0)
    incoming, before, after = exchange(*packed)
    z1, q1, curv1_parts, *packed = apply_schur(
        incoming, c1, before, after, (z0, q0)
    )
    incoming, before, after = exchange(*packed)

    v1, message = project(incoming, q1, before, after, (dot1_part, curv1_parts))
    landed = gather_rows(message)
    local2 = inverse(v1, True)
    weighted, factors, *packed = pl.pallas_call(
        functools.partial(third_kernel, capacity),
        out_shape=(shape(field_shape), shape((2, cases, width))) + sent_shapes,
        in_specs=[SMEM, SMEM] + [VMEM] * 7,
        out_specs=(VMEM, VMEM) + sent_specs,
        scratch_shapes=[face_sems],
        compiler_params=params(),
        cost_estimate=combine_cost,
        name="third",
    )(nbr_sub, send_slots, landed, responses, basis, local2, k0, c1, scalars)
    incoming, before, after = exchange(*packed)
    result = factors[0] * z0 + factors[1] * z1
    precond = pl.pallas_call(
        functools.partial(last_kernel, capacity),
        out_shape=shape(field_shape),
        in_specs=[SMEM] + [HBM] * 3 + [VMEM],
        out_specs=VMEM,
        scratch_shapes=[pltpu.VMEM(field_shape, F32), face_sems],
        compiler_params=params(),
        cost_estimate=cost(0, 4 * field_bytes),
        name="last",
    )(recv_slots, incoming, before, after, weighted)
    return (result, precond)


def solution(mesh):
    in_specs = (
        P(AXES, None, None, None),
        P(AXES, None, None),
        P(AXES, None, None),
        P(AXES, None, None, None),
        P("sub", None),
        P(AXES, None),
        P(AXES, None),
        P(AXES, None),
    )
    out_specs = (P(AXES, None, None, None), P(AXES, None, None, None))
    return jax.shard_map(local, mesh=mesh, in_specs=in_specs, out_specs=out_specs, check_vma=False)
```

time: 885 us -> 275 us (0.31)
  waiting for transfers between devices: 441 us -> 90.1 us
  blocking collectives: 267 us -> 0 us
  Pallas kernels: 0 us -> 78.3 us
  matrix products: 39.6 us -> 3.12 us
  local copies, waits for them, and re-layouts: 36.1 us -> 11.9 us
  starting transfers between devices: 60.2 us -> 84 us
  other arithmetic: 24.3 us -> 4.42 us
  between operations: 14.5 us -> 1.51 us
    psum x3 -> x0, waiting for transfers between devices: 405 us -> none  [coarse_sum(): lax.psum(coarse_part(field, weights, coarse_basis, onehot), ('grp', 'sub'))]
    psum x3 -> x0, blocking collectives: 195 us -> none  [the longest x2 129 us: global_dot(): lax.psum(jnp.sum(weights * resid * precond, axis=(0, 1, 3)), ('grp', 'sub'))]
    pallas_call x0 -> x15, Pallas kernels: none -> 78.3 us  [the longest x3 17.5 us: inverse(): pl.pallas_call(functools.partial(inverse_kernel, fine), out_shape=shape(f...]
    all_gather x3 -> x0, blocking collectives: 72.3 us -> none  [coarse_solve(): return lax.all_gather(piece, 'sub', axis=0, tiled=True)]
    all_to_all x6 -> x10, waiting for transfers between devices: 16.2 us -> 67.7 us  [all_to_all(): return lax.all_to_all(block, axes, split_axis=0, concat_axis=0, tiled=True)]
    dot_general x20 -> x1, matrix products: 39.6 us -> 3.12 us  [local(): asked = jnp.dot(coarse_inverse, columns_at, precision=PRECISE)]
    all_to_all x6 -> x10, starting transfers between devices: 34 us -> 57.9 us  [all_to_all(): return lax.all_to_all(block, axes, split_axis=0, concat_axis=0, tiled=True)]
    unnamed x38 -> x80, local copies, waits for them, and re-layouts: 19.8 us -> 8.68 us
  transfers between devices with their start and end apart: 21 -> 22, of which waited for: 13 -> 16; matrix products, arithmetic and copies ran while one was open for 5% -> 3% of each run, Pallas kernels for 0% -> 11%
where the time goes in v1:
time: 275 us; the launch traced here: 273 us
  waiting for transfers between devices  90.1 us (33%)
  starting transfers between devices  84 us (31%)
  Pallas kernels  78.3 us (28%)
  local copies, waits for them, and re-layouts  11.9 us (4%)
  other arithmetic  4.42 us (2%)
  matrix products  3.12 us (1%)
    all_to_all x10, waiting for transfers between devices, all_to_all(): return lax.all_to_all(block, axes, split_axis=0, concat_axis=0, tiled=True)  67.7 us
    all_to_all x10, starting transfers between devices, all_to_all(): return lax.all_to_all(block, axes, split_axis=0, concat_axis=0, tiled=True)  57.9 us
    ppermute x6, waiting for transfers between devices, exchange(): after = lax.ppermute(downward, 'grp', down)  22.4 us
    ppermute x6, starting transfers between devices, exchange(): before = lax.ppermute(upward, 'grp', up)  18.4 us
    pallas_call x3, Pallas kernels, inverse(): pl.pallas_call(functools.partial(inverse_kernel, fine), out_shape=shape(f...  17.5 us
    pallas_call x2, Pallas kernels, apply_schur(): pl.pallas_call(functools.partial(schur_kernel, bool(old), capacity), out_...  16.5 us
    pallas_call x3, Pallas kernels, project(): pl.pallas_call(functools.partial(project_kernel, len(dots), capacity), ou...  11.6 us
    unnamed x80, local copies, waits for them, and re-layouts  8.68 us
  transfers between devices with their start and end apart: 22, of which 16 were waited for; matrix products, arithmetic and copies ran while one was open for 3% of the time, Pallas kernels for 11%

profile of v1, /device:TPU:1, one launch (start us, length us, event | category | flops | bytes accessed | tf_op | source)
XLA Modules:
  0.0 273.4 jit_solution(16424853627793652221)
XLA Ops:
  5.2 8.7 %all-to-all-start = ((f32[32,72,128]{2,1,0:T(8,128)}), f32[32,72,128]{2,1,0:T(8,128)S(1)}, u32[]{:S(2)}, u32[]{:S(2)}) async-start(f32[32,72,128]{2,1,0:T(8,128)} %get-tuple-element.44), calls=%async_computation | async-start | bytes 2359296 | tf_op jit(solution)/shard_map/all_to_all | solution.py:444
  23.0 8.6 %all-to-all-done.incoming = f32[32,72,128]{2,1,0:T(8,128)S(1)} async-done(((f32[32,72,128]{2,1,0:T(8,128)}), f32[32,72,128]{2,1,0:T(8,128)S(1)}, u32[]{:S(2)}, u32[]{:S(2)}) %all-to-all-start) | async-done | bytes 1179680 | tf_op jit(solution)/shard_map/all_to_all | solution.py:444
  36.5 7.5 %all-to-all-start.1 = ((f32[128,9,1,128]{3,2,1,0:T(1,128)}), f32[128,9,1,128]{3,2,1,0:T(1,128)S(1)}, u32[]{:S(2)}, u32[]{:S(2)}) async-start(f32[128,9,1,128]{3,2,1,0:T(1,128)} %bitcast.31), calls=%async_computation.1 | async-start | bytes 1179648 | tf_op jit(solution)/shard_map/all_to_all | solution.py:444
  50.4 5.8 %inverse.3.local_part = f32[4,8,32,128]{3,2,1,0:T(8,128)} custom-call(f32[4,8,32,128]{3,2,1,0:T(8,128)} %get-tuple-element.49.field, bf16[4,1024,1024]{2,1,0:T(8,128)(2,1)} %matrix.9), custom_call_target="tpu_custom_call" | custom-call | flops 536870912 | bytes 9437184 | tf_op jit(solution)/shard_map/inverse/pallas_call | solution.py:526
  58.5 5.2 %all-to-all-start.2 = ((f32[32,16,128]{2,1,0:T(8,128)}), f32[32,16,128]{2,1,0:T(8,128)S(1)}, u32[]{:S(2)}, u32[]{:S(2)}) async-start(f32[32,16,128]{2,1,0:T(8,128)} %reshape.91), calls=%async_computation.2 | async-start | bytes 524288 | tf_op jit(solution)/shard_map/all_to_all | solution.py:444
  64.8 7.5 %totals.1 = f32[512,128]{1,0:T(8,128)} custom-call(f32[1152,128]{1,0:T(8,128)} %bitcast.26, s32[4,1152]{1,0:T(4,128)} %reshape.97.index), custom_call_target="tpu_custom_call" | custom-call | flops 4831838208 | bytes 1048576 | tf_op jit(solution)/shard_map/totals/pallas_call | solution.py:577
  73.3 4.1 %first.1 = (f32[4,8,32,128]{3,2,1,0:T(8,128)}, f32[32,128]{1,0:T(8,128)}, f32[32,64,128]{2,1,0:T(8,128)}, f32[4,32,128]{2,1,0:T(8,128)}, f32[4,32,128]{2,1,0:T(8,128)}) custom-call(s32[4,8]{1,0:T(4,128)} %nbr.15, s32[4,8]{1,0:T(4,128)} %get-tuple-element.93.slots.send_slots, f32[512,128]{1,0:T(8,128)} %bitcast.29, f32[512,128]{1,0:T(8,128)} %totals.1, ...), custom_call_target="tpu_custom_call" | custom-call | flops 67108864 | bytes 4194304 | tf_op jit(solution)/shard_map/first/pallas_call | solution.py:587
  77.4 7.4 %all-to-all-start.3 = ((f32[32,64,128]{2,1,0:T(8,128)}), f32[32,64,128]{2,1,0:T(8,128)S(1)}, u32[]{:S(2)}, u32[]{:S(2)}) async-start(f32[32,64,128]{2,1,0:T(8,128)} %get-tuple-element.53), calls=%async_computation.3 | async-start | bytes 2097152 | tf_op jit(solution)/shard_map/all_to_all | solution.py:444
  89.4 4.0 %collective-permute-done.3.after = f32[4,32,128]{2,1,0:T(8,128)S(1)} collective-permute-done((f32[4,32,128]{2,1,0:T(8,128)S(1)}, f32[4,32,128]{2,1,0:T(8,128)S(1)}, u32[]{:S(2)}, u32[]{:S(2)}) %collective-permute-start.3) | collective-permute-done | bytes 65568 | tf_op jit(solution)/shard_map/ppermute | solution.py:478
  93.4 8.5 %all-to-all-done.3.incoming = f32[32,64,128]{2,1,0:T(8,128)S(1)} async-done(((f32[32,64,128]{2,1,0:T(8,128)}), f32[32,64,128]{2,1,0:T(8,128)S(1)}, u32[]{:S(2)}, u32[]{:S(2)}) %all-to-all-start.3) | async-done | bytes 1048608 | tf_op jit(solution)/shard_map/all_to_all | solution.py:444
  102.9 8.0 %schur.2 = (f32[4,8,32,128]{3,2,1,0:T(8,128)}, f32[4,8,32,128]{3,2,1,0:T(8,128)}, f32[32,128]{1,0:T(8,128)}, f32[32,64,128]{2,1,0:T(8,128)}, f32[4,32,128]{2,1,0:T(8,128)}, /*index=5*/f32[4,32,128]{2,1,0:T(8,128)}) custom-call(s32[4,8]{1,0:T(4,128)} %nbr.15, s32[4,8]{1,0:T(4,128)} %get-tuple-element.93.slots.send_slots, ...), custom_call_target="tpu_custom_call" | custom-call | flops 536870912 | bytes 11534336 | tf_op jit(solution)/shard_map/schur/pallas_call | solution.py:539
  111.0 4.1 %all-to-all-start.4 = ((f32[32,64,128]{2,1,0:T(8,128)}), f32[32,64,128]{2,1,0:T(8,128)S(1)}, u32[]{:S(2)}, u32[]{:S(2)}) async-start(f32[32,64,128]{2,1,0:T(8,128)} %get-tuple-element.57), calls=%async_computation.4 | async-start | bytes 2097152 | tf_op jit(solution)/shard_map/all_to_all | solution.py:444
  119.8 4.0 %collective-permute-done.5.after = f32[4,32,128]{2,1,0:T(8,128)S(1)} collective-permute-done((f32[4,32,128]{2,1,0:T(8,128)S(1)}, f32[4,32,128]{2,1,0:T(8,128)S(1)}, u32[]{:S(2)}, u32[]{:S(2)}) %collective-permute-start.5) | collective-permute-done | bytes 65568 | tf_op jit(solution)/shard_map/ppermute | solution.py:478
  123.8 8.6 %all-to-all-done.4.incoming = f32[32,64,128]{2,1,0:T(8,128)S(1)} async-done(((f32[32,64,128]{2,1,0:T(8,128)}), f32[32,64,128]{2,1,0:T(8,128)S(1)}, u32[]{:S(2)}, u32[]{:S(2)}) %all-to-all-start.4) | async-done | bytes 1048608 | tf_op jit(solution)/shard_map/all_to_all | solution.py:444
  137.3 6.1 %all-to-all-start.5 = ((f32[128,9,1,128]{3,2,1,0:T(1,128)}), f32[128,9,1,128]{3,2,1,0:T(1,128)S(1)}, u32[]{:S(2)}, u32[]{:S(2)}) async-start(f32[128,9,1,128]{3,2,1,0:T(1,128)} %bitcast.32), calls=%async_computation.5 | async-start | bytes 1179648 | tf_op jit(solution)/shard_map/all_to_all | solution.py:444
  143.4 5.3 %responses.1 = bf16[256,1152]{1,0:T(8,128)(2,1)} custom-call(f32[512,128]{1,0:T(8,128)} %bitcast.30, s32[4,1152]{1,0:T(4,128)} %reshape.97.index), custom_call_target="tpu_custom_call" | custom-call | flops 1207959552 | bytes 524288 | tf_op jit(solution)/shard_map/responses/pallas_call | solution.py:598
  148.6 5.8 %inverse.4.local_part = f32[4,8,32,128]{3,2,1,0:T(8,128)} custom-call(f32[4,8,32,128]{3,2,1,0:T(8,128)} %get-tuple-element.64.field.image, bf16[4,1024,1024]{2,1,0:T(8,128)(2,1)} %matrix.9), custom_call_target="tpu_custom_call" | custom-call | flops 536870912 | bytes 9437184 | tf_op jit(solution)/shard_map/inverse/pallas_call | solution.py:526
  158.6 5.1 %second.1 = (f32[4,8,32,128]{3,2,1,0:T(8,128)}, f32[4,8,32,128]{3,2,1,0:T(8,128)}, f32[32,128]{1,0:T(8,128)}, f32[3,32,128]{2,1,0:T(8,128)}, f32[32,64,128]{2,1,...) custom-call(s32[4,8]{1,0:T(4,128)} %nbr.15, s32[4,8]{1,0:T(4,128)} %get-tuple-element.93.slots.send_slots, ...), custom_call_target="tpu_custom_call" | custom-call | flops 67108864 | bytes 4194304 | tf_op jit(solution)/shard_map/second/pallas_call | solution.py:613
  163.7 4.5 %all-to-all-start.6 = ((f32[32,64,128]{2,1,0:T(8,128)}), f32[32,64,128]{2,1,0:T(8,128)S(1)}, u32[]{:S(2)}, u32[]{:S(2)}) async-start(f32[32,64,128]{2,1,0:T(8,128)} %get-tuple-element.65), calls=%async_computation.6 | async-start | bytes 2097152 | tf_op jit(solution)/shard_map/all_to_all | solution.py:444
  172.6 4.0 %collective-permute-done.7.after = f32[4,32,128]{2,1,0:T(8,128)S(1)} collective-permute-done((f32[4,32,128]{2,1,0:T(8,128)S(1)}, f32[4,32,128]{2,1,0:T(8,128)S(1)}, u32[]{:S(2)}, u32[]{:S(2)}) %collective-permute-start.7) | collective-permute-done | bytes 65568 | tf_op jit(solution)/shard_map/ppermute | solution.py:478
  176.6 8.9 %all-to-all-done.6.incoming = f32[32,64,128]{2,1,0:T(8,128)S(1)} async-done(((f32[32,64,128]{2,1,0:T(8,128)}), f32[32,64,128]{2,1,0:T(8,128)S(1)}, u32[]{:S(2)}, u32[]{:S(2)}) %all-to-all-start.6) | async-done | bytes 1048608 | tf_op jit(solution)/shard_map/all_to_all | solution.py:444
  186.5 8.4 %schur.3 = (f32[4,8,32,128]{3,2,1,0:T(8,128)}, f32[4,8,32,128]{3,2,1,0:T(8,128)}, f32[64,128]{1,0:T(8,128)}, f32[32,64,128]{2,1,0:T(8,128)}, f32[4,32,128]{2,1,0:T(8,128)}, /*index=5*/f32[4,32,128]{2,1,0:T(8,128)}) custom-call(s32[4,8]{1,0:T(4,128)} %nbr.15, s32[4,8]{1,0:T(4,128)} %get-tuple-element.93.slots.send_slots, ...), custom_call_target="tpu_custom_call" | custom-call | flops 536870912 | bytes 11534336 | tf_op jit(solution)/shard_map/schur/pallas_call | solution.py:539
  195.0 4.1 %all-to-all-start.7 = ((f32[32,64,128]{2,1,0:T(8,128)}), f32[32,64,128]{2,1,0:T(8,128)S(1)}, u32[]{:S(2)}, u32[]{:S(2)}) async-start(f32[32,64,128]{2,1,0:T(8,128)} %get-tuple-element.70), calls=%async_computation.7 | async-start | bytes 2097152 | tf_op jit(solution)/shard_map/all_to_all | solution.py:444
  203.4 4.0 %collective-permute-done.9.after = f32[4,32,128]{2,1,0:T(8,128)S(1)} collective-permute-done((f32[4,32,128]{2,1,0:T(8,128)S(1)}, f32[4,32,128]{2,1,0:T(8,128)S(1)}, u32[]{:S(2)}, u32[]{:S(2)}) %collective-permute-start.9) | collective-permute-done | bytes 65568 | tf_op jit(solution)/shard_map/ppermute | solution.py:478
  207.4 9.1 %all-to-all-done.7.incoming = f32[32,64,128]{2,1,0:T(8,128)S(1)} async-done(((f32[32,64,128]{2,1,0:T(8,128)}), f32[32,64,128]{2,1,0:T(8,128)S(1)}, u32[]{:S(2)}, u32[]{:S(2)}) %all-to-all-start.7) | async-done | bytes 1048608 | tf_op jit(solution)/shard_map/all_to_all | solution.py:444
  217.4 3.9 %project.5 = (f32[4,8,32,128]{3,2,1,0:T(8,128)}, f32[1152,128]{1,0:T(8,128)}) custom-call(s32[4,8]{1,0:T(4,128)} %nbr.15, s32[4,8]{1,0:T(4,128)} %get-tuple-element.92.slots.recv_slots, f32[32,64,128]{2,1,0:T(8,128)} %copy-done.5, f32[4,32,128]{2,1,0:T(8,128)} %copy-done.23, f32[4,32,128]{2,1,0:T(8,128)} %copy-done.25, ...), custom_call_target="tpu_custom_call" | custom-call | flops 33554432 | bytes 2621440 | tf_op jit(solution)/shard_map/project/pallas_call | solution.py:509
  221.3 5.6 %all-to-all-start.8 = ((f32[128,9,1,128]{3,2,1,0:T(1,128)}), f32[128,9,1,128]{3,2,1,0:T(1,128)S(1)}, u32[]{:S(2)}, u32[]{:S(2)}) async-start(f32[128,9,1,128]{3,2,1,0:T(1,128)} %bitcast.33), calls=%async_computation.8 | async-start | bytes 1179648 | tf_op jit(solution)/shard_map/all_to_all | solution.py:444
  226.9 5.8 %inverse.5.local_part = f32[4,8,32,128]{3,2,1,0:T(8,128)} custom-call(f32[4,8,32,128]{3,2,1,0:T(8,128)} %get-tuple-element.77.field, bf16[4,1024,1024]{2,1,0:T(8,128)(2,1)} %matrix.9), custom_call_target="tpu_custom_call" | custom-call | flops 536870912 | bytes 9437184 | tf_op jit(solution)/shard_map/inverse/pallas_call | solution.py:526
  232.7 8.6 %all-to-all-done.8 = f32[128,9,1,128]{3,2,1,0:T(1,128)S(1)} async-done(((f32[128,9,1,128]{3,2,1,0:T(1,128)}), f32[128,9,1,128]{3,2,1,0:T(1,128)S(1)}, u32[]{:S(2)}, u32[]{:S(2)}) %all-to-all-start.8) | async-done | bytes 589856 | tf_op jit(solution)/shard_map/all_to_all | solution.py:444
  242.2 4.7 %third.1 = (f32[4,8,32,128]{3,2,1,0:T(8,128)}, f32[2,32,128]{2,1,0:T(8,128)}, f32[32,64,128]{2,1,0:T(8,128)}, f32[4,32,128]{2,1,0:T(8,128)}, f32[4,32,128]{2,1,0:T(8,128)}) custom-call(s32[4,8]{1,0:T(4,128)} %nbr.15, s32[4,8]{1,0:T(4,128)} %get-tuple-element.93.slots.send_slots, f32[1152,128]{1,0:T(8,128)} %bitcast.28, bf16[256,1152]{1,0:T(8,128)(2,1)} %responses.1, ...), custom_call_target="tpu_custom_call" | custom-call | flops 67108864 | bytes 4194304 | tf_op jit(solution)/shard_map/third/pallas_call | solution.py:636
  246.9 4.6 %all-to-all-start.9 = ((f32[32,64,128]{2,1,0:T(8,128)}), f32[32,64,128]{2,1,0:T(8,128)S(1)}, u32[]{:S(2)}, u32[]{:S(2)}) async-start(f32[32,64,128]{2,1,0:T(8,128)} %get-tuple-element.82), calls=%async_computation.9 | async-start | bytes 2097152 | tf_op jit(solution)/shard_map/all_to_all | solution.py:444
  259.1 9.7 %all-to-all-done.9.incoming = f32[32,64,128]{2,1,0:T(8,128)S(1)} async-done(((f32[32,64,128]{2,1,0:T(8,128)}), f32[32,64,128]{2,1,0:T(8,128)S(1)}, u32[]{:S(2)}, u32[]{:S(2)}) %all-to-all-start.9) | async-done | bytes 1048608 | tf_op jit(solution)/shard_map/all_to_all | solution.py:444
  (127 shorter events, 71.5 us)
Async XLA Ops:
  0.6 44.4 %copy-start = (f32[64,2048]{1,0:T(8,128)S(1)}, f32[64,2048]{1,0:T(8,128)}, u32[]{:S(2)}) copy-start(f32[64,2048]{1,0:T(8,128)} %param.12) | copy-start | bytes 1572868
  0.6 18.1 %copy-start.13 = (f32[4,8,8,128]{3,2,1,0:T(8,128)S(1)}, f32[4,8,8,128]{3,2,1,0:T(8,128)}, u32[]{:S(2)}) copy-start(f32[4,8,8,128]{3,2,1,0:T(8,128)} %param.11) | copy-start | bytes 393220
  5.2 12.3 %copy-start.30 = (f32[4,32,128]{2,1,0:T(8,128)S(1)}, f32[4,32,128]{2,1,0:T(8,128)}, u32[]{:S(2)}) copy-start(f32[4,32,128]{2,1,0:T(8,128)} %get-tuple-element.46) | copy-start | bytes 196612
  5.2 26.4 %all-to-all-start = ((f32[32,72,128]{2,1,0:T(8,128)}), f32[32,72,128]{2,1,0:T(8,128)S(1)}, u32[]{:S(2)}, u32[]{:S(2)}) async-start(f32[32,72,128]{2,1,0:T(8,128)} %get-tuple-element.44), calls=%async_computation | async-start | bytes 2359296 | tf_op jit(solution)/shard_map/all_to_all | solution.py:444
  13.9 5.7 %collective-permute-start = (f32[4,32,128]{2,1,0:T(8,128)S(1)}, f32[4,32,128]{2,1,0:T(8,128)S(1)}, u32[]{:S(2)}, u32[]{:S(2)}) collective-permute-start(f32[4,32,128]{2,1,0:T(8,128)S(1)} %copy-done.34), channel_id=1, source_target_pairs={{0,32},{32,64},{64,96},{1,33},{33,65},{65,97},{2,34},{34,66},{66,9... | collective-permute-start | bytes 196616 | tf_op jit(solution)/shard_map/ppermute | solution.py:477
  17.5 5.5 %collective-permute-start.1 = (f32[4,32,128]{2,1,0:T(8,128)S(1)}, f32[4,32,128]{2,1,0:T(8,128)S(1)}, u32[]{:S(2)}, u32[]{:S(2)}) collective-permute-start(f32[4,32,128]{2,1,0:T(8,128)S(1)} %copy-done.30), channel_id=1, source_target_pairs={{32,0},{64,32},{96,64},{33,1},{65,33},{97,65},{34,2},{66,34},{98,6... | collective-permute-start | bytes 196616 | tf_op jit(solution)/shard_map/ppermute | solution.py:478
  36.5 22.0 %all-to-all-start.1 = ((f32[128,9,1,128]{3,2,1,0:T(1,128)}), f32[128,9,1,128]{3,2,1,0:T(1,128)S(1)}, u32[]{:S(2)}, u32[]{:S(2)}) async-start(f32[128,9,1,128]{3,2,1,0:T(1,128)} %bitcast.31), calls=%async_computation.1 | async-start | bytes 1179648 | tf_op jit(solution)/shard_map/all_to_all | solution.py:444
  58.5 14.1 %all-to-all-start.2 = ((f32[32,16,128]{2,1,0:T(8,128)}), f32[32,16,128]{2,1,0:T(8,128)S(1)}, u32[]{:S(2)}, u32[]{:S(2)}) async-start(f32[32,16,128]{2,1,0:T(8,128)} %reshape.91), calls=%async_computation.2 | async-start | bytes 524288 | tf_op jit(solution)/shard_map/all_to_all | solution.py:444
  77.4 24.6 %all-to-all-start.3 = ((f32[32,64,128]{2,1,0:T(8,128)}), f32[32,64,128]{2,1,0:T(8,128)S(1)}, u32[]{:S(2)}, u32[]{:S(2)}) async-start(f32[32,64,128]{2,1,0:T(8,128)} %get-tuple-element.53), calls=%async_computation.3 | async-start | bytes 2097152 | tf_op jit(solution)/shard_map/all_to_all | solution.py:444
  84.8 4.7 %collective-permute-start.2 = (f32[4,32,128]{2,1,0:T(8,128)S(1)}, f32[4,32,128]{2,1,0:T(8,128)S(1)}, u32[]{:S(2)}, u32[]{:S(2)}) collective-permute-start(f32[4,32,128]{2,1,0:T(8,128)S(1)} %copy-done.38), channel_id=1, source_target_pairs={{0,32},{32,64},{64,96},{1,33},{33,65},{65,97},{2,34},{34,66},{66,9... | collective-permute-start | bytes 196616 | tf_op jit(solution)/shard_map/ppermute | solution.py:477
  88.1 5.3 %collective-permute-start.3 = (f32[4,32,128]{2,1,0:T(8,128)S(1)}, f32[4,32,128]{2,1,0:T(8,128)S(1)}, u32[]{:S(2)}, u32[]{:S(2)}) collective-permute-start(f32[4,32,128]{2,1,0:T(8,128)S(1)} %copy-done.35), channel_id=1, source_target_pairs={{32,0},{64,32},{96,64},{33,1},{65,33},{97,65},{34,2},{66,34},{98,6... | collective-permute-start | bytes 196616 | tf_op jit(solution)/shard_map/ppermute | solution.py:478
  89.4 12.5 %copy-start.15 = (f32[4,32,128]{2,1,0:T(8,128)}, f32[4,32,128]{2,1,0:T(8,128)S(1)}, u32[]{:S(2)}) copy-start(f32[4,32,128]{2,1,0:T(8,128)S(1)} %collective-permute-done.2.before) | copy-start | bytes 196612
  111.0 21.4 %all-to-all-start.4 = ((f32[32,64,128]{2,1,0:T(8,128)}), f32[32,64,128]{2,1,0:T(8,128)S(1)}, u32[]{:S(2)}, u32[]{:S(2)}) async-start(f32[32,64,128]{2,1,0:T(8,128)} %get-tuple-element.57), calls=%async_computation.4 | async-start | bytes 2097152 | tf_op jit(solution)/shard_map/all_to_all | solution.py:444
  115.1 4.7 %collective-permute-start.4 = (f32[4,32,128]{2,1,0:T(8,128)S(1)}, f32[4,32,128]{2,1,0:T(8,128)S(1)}, u32[]{:S(2)}, u32[]{:S(2)}) collective-permute-start(f32[4,32,128]{2,1,0:T(8,128)S(1)} %copy-done.37), channel_id=1, source_target_pairs={{0,32},{32,64},{64,96},{1,33},{33,65},{65,97},{2,34},{34,66},{66,9... | collective-permute-start | bytes 196616 | tf_op jit(solution)/shard_map/ppermute | solution.py:477
  118.5 5.3 %collective-permute-start.5 = (f32[4,32,128]{2,1,0:T(8,128)S(1)}, f32[4,32,128]{2,1,0:T(8,128)S(1)}, u32[]{:S(2)}, u32[]{:S(2)}) collective-permute-start(f32[4,32,128]{2,1,0:T(8,128)S(1)} %copy-done.32), channel_id=1, source_target_pairs={{32,0},{64,32},{96,64},{33,1},{65,33},{97,65},{34,2},{66,34},{98,6... | collective-permute-start | bytes 196616 | tf_op jit(solution)/shard_map/ppermute | solution.py:478
  119.8 12.6 %copy-start.22 = (f32[4,32,128]{2,1,0:T(8,128)}, f32[4,32,128]{2,1,0:T(8,128)S(1)}, u32[]{:S(2)}) copy-start(f32[4,32,128]{2,1,0:T(8,128)S(1)} %collective-permute-done.4.before) | copy-start | bytes 196612
  137.3 20.5 %all-to-all-start.5 = ((f32[128,9,1,128]{3,2,1,0:T(1,128)}), f32[128,9,1,128]{3,2,1,0:T(1,128)S(1)}, u32[]{:S(2)}, u32[]{:S(2)}) async-start(f32[128,9,1,128]{3,2,1,0:T(1,128)} %bitcast.32), calls=%async_computation.5 | async-start | bytes 1179648 | tf_op jit(solution)/shard_map/all_to_all | solution.py:444
  163.7 21.8 %all-to-all-start.6 = ((f32[32,64,128]{2,1,0:T(8,128)}), f32[32,64,128]{2,1,0:T(8,128)S(1)}, u32[]{:S(2)}, u32[]{:S(2)}) async-start(f32[32,64,128]{2,1,0:T(8,128)} %get-tuple-element.65), calls=%async_computation.6 | async-start | bytes 2097152 | tf_op jit(solution)/shard_map/all_to_all | solution.py:444
  168.3 4.3 %collective-permute-start.6 = (f32[4,32,128]{2,1,0:T(8,128)S(1)}, f32[4,32,128]{2,1,0:T(8,128)S(1)}, u32[]{:S(2)}, u32[]{:S(2)}) collective-permute-start(f32[4,32,128]{2,1,0:T(8,128)S(1)} %copy-done.33), channel_id=1, source_target_pairs={{0,32},{32,64},{64,96},{1,33},{33,65},{65,97},{2,34},{34,66},{66,9... | collective-permute-start | bytes 196616 | tf_op jit(solution)/shard_map/ppermute | solution.py:477
  171.3 5.3 %collective-permute-start.7 = (f32[4,32,128]{2,1,0:T(8,128)S(1)}, f32[4,32,128]{2,1,0:T(8,128)S(1)}, u32[]{:S(2)}, u32[]{:S(2)}) collective-permute-start(f32[4,32,128]{2,1,0:T(8,128)S(1)} %copy-done.29), channel_id=1, source_target_pairs={{32,0},{64,32},{96,64},{33,1},{65,33},{97,65},{34,2},{66,34},{98,6... | collective-permute-start | bytes 196616 | tf_op jit(solution)/shard_map/ppermute | solution.py:478
  172.6 12.9 %copy-start.14 = (f32[4,32,128]{2,1,0:T(8,128)}, f32[4,32,128]{2,1,0:T(8,128)S(1)}, u32[]{:S(2)}) copy-start(f32[4,32,128]{2,1,0:T(8,128)S(1)} %collective-permute-done.6.before) | copy-start | bytes 196612
  195.0 21.4 %all-to-all-start.7 = ((f32[32,64,128]{2,1,0:T(8,128)}), f32[32,64,128]{2,1,0:T(8,128)S(1)}, u32[]{:S(2)}, u32[]{:S(2)}) async-start(f32[32,64,128]{2,1,0:T(8,128)} %get-tuple-element.70), calls=%async_computation.7 | async-start | bytes 2097152 | tf_op jit(solution)/shard_map/all_to_all | solution.py:444
  199.1 4.2 %collective-permute-start.8 = (f32[4,32,128]{2,1,0:T(8,128)S(1)}, f32[4,32,128]{2,1,0:T(8,128)S(1)}, u32[]{:S(2)}, u32[]{:S(2)}) collective-permute-start(f32[4,32,128]{2,1,0:T(8,128)S(1)} %copy-done.36), channel_id=1, source_target_pairs={{0,32},{32,64},{64,96},{1,33},{33,65},{65,97},{2,34},{34,66},{66,9... | collective-permute-start | bytes 196616 | tf_op jit(solution)/shard_map/ppermute | solution.py:477
  202.0 5.3 %collective-permute-start.9 = (f32[4,32,128]{2,1,0:T(8,128)S(1)}, f32[4,32,128]{2,1,0:T(8,128)S(1)}, u32[]{:S(2)}, u32[]{:S(2)}) collective-permute-start(f32[4,32,128]{2,1,0:T(8,128)S(1)} %copy-done.31), channel_id=1, source_target_pairs={{32,0},{64,32},{96,64},{33,1},{65,33},{97,65},{34,2},{66,34},{98,6... | collective-permute-start | bytes 196616 | tf_op jit(solution)/shard_map/ppermute | solution.py:478
  203.4 13.1 %copy-start.23 = (f32[4,32,128]{2,1,0:T(8,128)}, f32[4,32,128]{2,1,0:T(8,128)S(1)}, u32[]{:S(2)}) copy-start(f32[4,32,128]{2,1,0:T(8,128)S(1)} %collective-permute-done.8.before) | copy-start | bytes 196612
  221.3 20.0 %all-to-all-start.8 = ((f32[128,9,1,128]{3,2,1,0:T(1,128)}), f32[128,9,1,128]{3,2,1,0:T(1,128)S(1)}, u32[]{:S(2)}, u32[]{:S(2)}) async-start(f32[128,9,1,128]{3,2,1,0:T(1,128)} %bitcast.33), calls=%async_computation.8 | async-start | bytes 1179648 | tf_op jit(solution)/shard_map/all_to_all | solution.py:444
  242.1 13.0 %copy-start.10 = (f32[4,8,32,128]{3,2,1,0:T(8,128)S(1)}, f32[4,8,32,128]{3,2,1,0:T(8,128)}, u32[]{:S(2)}) copy-start(f32[4,8,32,128]{3,2,1,0:T(8,128)} %get-tuple-element.69.rest_0_) | copy-start | bytes 1572868
  242.2 13.0 %copy-start.12 = (f32[4,8,32,128]{3,2,1,0:T(8,128)S(1)}, f32[4,8,32,128]{3,2,1,0:T(8,128)}, u32[]{:S(2)}) copy-start(f32[4,8,32,128]{3,2,1,0:T(8,128)} %get-tuple-element.81) | copy-start | bytes 1572868
  246.9 21.9 %all-to-all-start.9 = ((f32[32,64,128]{2,1,0:T(8,128)}), f32[32,64,128]{2,1,0:T(8,128)S(1)}, u32[]{:S(2)}, u32[]{:S(2)}) async-start(f32[32,64,128]{2,1,0:T(8,128)} %get-tuple-element.82), calls=%async_computation.9 | async-start | bytes 2097152 | tf_op jit(solution)/shard_map/all_to_all | solution.py:444
  251.6 4.5 %collective-permute-start.10 = (f32[4,32,128]{2,1,0:T(8,128)S(1)}, f32[4,32,128]{2,1,0:T(8,128)S(1)}, u32[]{:S(2)}, u32[]{:S(2)}) collective-permute-start(f32[4,32,128]{2,1,0:T(8,128)S(1)} %copy-done.28), channel_id=1, source_target_pairs={{0,32},{32,64},{64,96},{1,33},{33,65},{65,97},{2,34},{34,66},{66,9... | collective-permute-start | bytes 196616 | tf_op jit(solution)/shard_map/ppermute | solution.py:477
  253.8 5.3 %collective-permute-start.11 = (f32[4,32,128]{2,1,0:T(8,128)S(1)}, f32[4,32,128]{2,1,0:T(8,128)S(1)}, u32[]{:S(2)}, u32[]{:S(2)}) collective-permute-start(f32[4,32,128]{2,1,0:T(8,128)S(1)} %copy-done.27), channel_id=1, source_target_pairs={{32,0},{64,32},{96,64},{33,1},{65,33},{97,65},{34,2},{66,34},{98,6... | collective-permute-start | bytes 196616 | tf_op jit(solution)/shard_map/ppermute | solution.py:478
  256.1 12.8 %copy-start.18 = (f32[4,32,128]{2,1,0:T(8,128)}, f32[4,32,128]{2,1,0:T(8,128)S(1)}, u32[]{:S(2)}) copy-start(f32[4,32,128]{2,1,0:T(8,128)S(1)} %collective-permute-done.10.before) | copy-start | bytes 196612
  (29 other events, 162.0 us)

commit v2 on v1

v2 whole, which is shorter than its diff:
```python
import functools

import jax
import jax.numpy as jnp
from jax import lax
from jax.experimental import pallas as pl
from jax.experimental.pallas import tpu as pltpu
from jax.sharding import PartitionSpec as P

AXES = ("grp", "sub")
PRECISE = lax.Precision.HIGHEST
F32 = jnp.float32
BF16 = jnp.bfloat16
SMEM = pl.BlockSpec(memory_space=pltpu.SMEM)
VMEM = pl.BlockSpec(memory_space=pltpu.VMEM)
HBM = pl.BlockSpec(memory_space=pltpu.HBM)
VMEM_LIMIT = 63 * 1024 * 1024
PIECES = 1
FACES = 6


def shape(dims, dtype=F32):
    return jax.ShapeDtypeStruct(dims, dtype)


def params(limit=VMEM_LIMIT):
    return pltpu.CompilerParams(vmem_limit_bytes=limit)


def cost(flops, moved):
    return pl.CostEstimate(flops=flops, bytes_accessed=moved, transcendentals=0)


def face_routes(nbr_sub, nbr_block, peer_count, capacity):
    subs, blocks = nbr_sub.shape
    face_count = blocks - 2
    shared = lax.broadcasted_iota(jnp.int32, nbr_sub.shape, 1) < face_count
    place = lax.broadcasted_iota(jnp.int32, nbr_sub.shape, 0) * face_count
    place = place + lax.broadcasted_iota(jnp.int32, nbr_sub.shape, 1)
    peer = jnp.where(shared, nbr_sub // subs % peer_count, -1)
    partner_place = nbr_sub % subs * face_count + nbr_block
    same = (peer[:, :, None, None] == peer[None, None]) & shared[None, None]

    def rank(order):
        return jnp.sum(same & (order[None, None] < order[:, :, None, None]), axis=(2, 3))

    first = jnp.maximum(peer, 0) * capacity
    return (first + rank(place), first + rank(partner_place))


def weight(table, s, b):
    return jnp.where(table[s, b] >= 0, 0.5, 1.0).astype(F32)


def split(x):
    high = x.astype(BF16)
    return high, (x - high.astype(F32)).astype(BF16)


def dotted(a, b):
    return lax.dot_general(a, b, (((1,), (0,)), ((), ())), preferred_element_type=F32)


def three_part(both, other):
    product = dotted(both, other)
    rows, columns = product.shape[0] // 2, product.shape[1] // 2
    return product[:rows, :columns] + product[:rows, columns:] + product[rows:, :columns]


def slot_of(buffer, slot, cases):
    capacity = buffer.shape[1] // cases
    start = pl.multiple_of(lax.rem(slot, capacity) * cases, cases)
    return buffer.at[lax.div(slot, capacity), pl.ds(start, cases)]


def sends(source, table, outgoing, sems, s):
    subs, blocks, cases = source.shape[:3]
    return [
        pltpu.make_async_copy(
            source.at[s, b], slot_of(outgoing, table[subs + s, b], cases), sems.at[s, b]
        )
        for b in range(blocks - 2)
    ]


def rims(source, upward, downward, sems):
    faces = source.shape[1] - 2
    return [
        pltpu.make_async_copy(source.at[:, faces], upward, sems.at[0, faces]),
        pltpu.make_async_copy(source.at[:, faces + 1], downward, sems.at[0, faces + 1]),
    ]


def fetches(table, table_s, incoming, incoming_v, before, after, rims_v, sems):
    return start_all(
        copies_of(
            [table, incoming, after, before],
            [table_s, incoming_v, rims_v.at[0], rims_v.at[1]], sems, 0,
        )
    )


def received(table_s, incoming_v, rims_v, s, b):
    subs, cases = rims_v.shape[1:3]
    faces = FACES
    if b >= faces:
        return rims_v[b - faces, s]
    slot = table_s[2 * subs + s, b]
    capacity = incoming_v.shape[1] // cases
    start = pl.multiple_of(lax.rem(slot, capacity) * cases, cases)
    return incoming_v[lax.div(slot, capacity), pl.ds(start, cases)]


def start_all(copies):
    for copy in copies:
        copy.start()
    return copies


def wait_all(copies):
    for copy in copies:
        copy.wait()


def copies_of(sources, targets, sems, first):
    return [
        pltpu.make_async_copy(source, target, sems.at[first + i])
        for i, (source, target) in enumerate(zip(sources, targets))
    ]


def parts_of(ref):
    return [ref.at[s] for s in range(ref.shape[0])]


def pack_kernel(
    table, primal, loads, outgoing, upward, downward, index_row, tall, sems, row_sem
):
    subs, blocks, cases, width = loads.shape
    coarse = primal.shape[1]
    copies = start_all(rims(loads, upward, downward, sems))
    for s in range(subs):
        copies += start_all(sends(loads, table, outgoing, sems, s))
    lane = lax.broadcasted_iota(jnp.int32, (1, width), 1)
    row = jnp.zeros((1, width), jnp.int32)
    for s in range(subs):
        for c in range(coarse):
            row = jnp.where(lane == s * coarse + c, primal[s, c], row)
    row = row.astype(F32)
    index_row[...] = jnp.broadcast_to(row, index_row.shape)
    tall[...] = jnp.broadcast_to(row[None], tall.shape)
    rows = outgoing.at[:, pl.ds(outgoing.shape[1] - tall.shape[1], tall.shape[1])]
    copies += start_all([pltpu.make_async_copy(tall, rows, row_sem)])
    wait_all(copies)


def project_kernel(
    dot_count, table, incoming, before, after, base, basis, *rest
):
    dots = rest[:dot_count]
    field, message, held, parts, factors, tall, block_rows = rest[dot_count : dot_count + 7]
    table_s, incoming_v, rims_v, sems, more = rest[dot_count + 7 :]
    subs, blocks, cases, width = base.shape
    lanes = subs * cases
    primal = basis.shape[0] // 4
    coarse = primal // subs
    arriving = fetches(table, table_s, incoming, incoming_v, before, after, rims_v, sems)
    base_in = start_all(copies_of(parts_of(base), parts_of(held), more, 0))
    others = [basis.at[pl.ds(0, 2 * primal)]]
    targets = [factors]
    place = 0
    for part in dots:
        others.append(part)
        targets.append(tall.at[pl.ds(place, part.shape[0])])
        place += part.shape[0]
    others = start_all(copies_of(others, targets, more, subs))
    tall[place:] = jnp.zeros((tall.shape[0] - place, width), F32)
    wait_all(arriving)
    out = []
    for s in range(subs):
        wait_all(base_in[s : s + 1])
        for b in range(blocks):
            other = received(table_s, incoming_v, rims_v, s, b)
            value = weight(table_s, s, b) * (held[s, b] + other)
            held[s, b] = value
            high, low = split(value)
            parts[s * cases : (s + 1) * cases, b * width : (b + 1) * width] = high
            parts[lanes + s * cases : lanes + (s + 1) * cases, b * width : (b + 1) * width] = low
        out += start_all(copies_of([held.at[s]], [field.at[s]], more, 8 + s))
    wait_all(others)
    product = lax.dot_general(
        factors[...], parts[...], (((1,), (1,)), ((), ())), preferred_element_type=F32
    )
    product = product[:primal, :lanes] + product[:primal, lanes:] + product[primal:, :lanes]
    lane = lax.broadcasted_iota(jnp.int32, (coarse, lanes), 1) // cases
    block = jnp.zeros((coarse, lanes), F32)
    for s in range(subs):
        block = jnp.where(lane == s, product[s * coarse : (s + 1) * coarse], block)
    if dot_count == 1:
        row = tall[0:1]
    else:
        row = jnp.sum(tall[...].T, axis=0, keepdims=True)
    period = coarse + 1
    height = block_rows.shape[0]
    for p in range(height // period):
        block_rows[p * period : p * period + coarse] = block
        block_rows[p * period + coarse : (p + 1) * period] = row
    count = message.shape[0] // height
    rows = [message.at[pl.ds(i * height, height)] for i in range(count)]
    out += start_all(copies_of([block_rows] * count, rows, more, 8 + subs))
    wait_all(out)


def applied(flat, matrix, fine):
    if not fine:
        return dotted(flat.astype(BF16), matrix)
    both = dotted(jnp.concatenate(split(flat), axis=0), matrix)
    return both[: flat.shape[0]] + both[flat.shape[0] :]


def pieces(matrix, held, sems):
    subs, rows = matrix.shape[:2]
    count = sems.shape[1]
    height = rows // count
    return [
        [
            pltpu.make_async_copy(
                matrix.at[s, pl.ds(i * height, height)],
                held.at[s, pl.ds(i * height, height)],
                sems.at[s, i],
            )
            for i in range(count)
        ]
        for s in range(subs)
    ]


def inverse_kernel(fine, field, matrix, out, held, sems):
    subs, blocks, cases, width = field.shape
    copies = [start_all(group) for group in pieces(matrix, held, sems)]
    for s in range(subs):
        flat = jnp.concatenate([field[s, b] for b in range(blocks)], axis=1)
        wait_all(copies[s])
        product = applied(flat, held[s], fine)
        for b in range(blocks):
            out[s, b] = product[:, b * width : (b + 1) * width]


def folded(product, primal):
    size = product.shape[0]
    turned = product.T
    row = lax.broadcasted_iota(jnp.int32, (size, size), 0) // primal
    lane = lax.broadcasted_iota(jnp.int32, (size, size), 1) // primal
    kept = jnp.where(row == lane, turned, 0.0)
    total = kept[:primal]
    for q in range(1, size // primal):
        total = total + kept[q * primal : (q + 1) * primal]
    out = total
    for q in range(1, size // primal):
        out = out + pltpu.roll(total, q * primal, 1)
    return out


def spread(picked, basis, subs, coarse):
    cases, lanes = picked.shape
    high = picked.astype(BF16).astype(F32)
    lane = lax.broadcasted_iota(jnp.int32, (cases, lanes), 1)
    parts = jnp.where(lane < lanes // 2, high, picked - high)
    owner = lane // coarse % subs
    tall = jnp.concatenate(
        [jnp.where(owner == s, parts, 0.0) for s in range(subs)], axis=0
    ).astype(BF16)
    return dotted(tall, basis[...])


def first_kernel(
    table, columns, totals, basis, local_part,
    corrected, outgoing, upward, downward,
    columns_v, totals_v, basis_v, local_v, weighted, table_s, sems, more,
):
    subs, blocks, cases, width = local_part.shape
    primal = basis.shape[0] // 4
    routes = start_all([pltpu.make_async_copy(table, table_s, sems.at[0, 0])])
    small = start_all(
        copies_of([columns, totals, basis], [columns_v, totals_v, basis_v], more, 0)
    )
    local_in = start_all(copies_of(parts_of(local_part), parts_of(local_v), more, 3))
    wait_all(small)
    wait_all(routes)
    high, low = split(columns_v[...].T)
    total_high, total_low = split(totals_v[...])
    product = three_part(
        jnp.concatenate([high, low], axis=0), jnp.concatenate([total_high, total_low], axis=1)
    )
    coarse_part = spread(folded(product, primal), basis_v, subs, primal // subs)
    out = []
    for s in range(subs):
        wait_all([local_in[s]])
        for b in range(blocks):
            value = local_v[s, b] + coarse_part[
                s * cases : (s + 1) * cases, b * width : (b + 1) * width
            ]
            local_v[s, b] = value
            weighted[s, b] = weight(table_s, s, b) * value
        out += start_all(sends(weighted, table_s, outgoing, sems, s))
        out += start_all(copies_of([local_v.at[s]], [corrected.at[s]], more, 3 + 2 * subs + s))
    out += start_all(rims(weighted, upward, downward, sems))
    wait_all(out)


def everyone(value, period):
    row = lax.broadcasted_iota(jnp.int32, value.shape, 0)
    sums = lax.rem(row, period) == period - 1
    totals = jnp.sum(jnp.where(sums, value, 0.0), axis=0, keepdims=True)
    totals = jnp.broadcast_to(totals, (value.shape[1], value.shape[1])).T
    high, low = split(jnp.where(sums, 0.0, value))
    return totals, jnp.concatenate([high, low], axis=1)


def second_kernel(
    table, landed, responses, basis, local_part, corrected,
    step_out, out_field, scalars, outgoing, upward, downward,
    landed_v, responses_v, basis_v, local_v, corrected_v, weighted, scalars_v, table_s, sems, more,
):
    subs, blocks, cases, width = corrected.shape
    primal = basis.shape[0] // 4
    coarse = primal // subs
    routes = start_all([pltpu.make_async_copy(table, table_s, sems.at[0, 0])])
    small = start_all(
        copies_of([landed, responses, basis], [landed_v, responses_v, basis_v], more, 0)
    )
    fields = [
        start_all(copies_of(parts_of(source), parts_of(target), more, 3 + i * subs))
        for i, (source, target) in enumerate(
            [(local_part, local_v), (corrected, corrected_v)]
        )
    ]
    wait_all(small)
    wait_all(routes)
    totals, rows = everyone(landed_v[...], coarse + 1)
    dot0 = totals[:cases]
    curv0 = totals[cases : 2 * cases]
    alpha = dot0 / curv0
    scalars_v[0] = dot0
    scalars_v[1] = curv0
    scalars_v[2] = alpha
    out = start_all(copies_of([scalars_v], [scalars], more, 3 + 6 * subs))
    product = three_part(responses_v[...], rows)
    coarse_part = spread(folded(product, primal), basis_v, subs, coarse)
    for s in range(subs):
        wait_all([group[s] for group in fields])
        for b in range(blocks):
            step = local_v[s, b] + coarse_part[
                s * cases : (s + 1) * cases, b * width : (b + 1) * width
            ]
            local_v[s, b] = step
            value = corrected_v[s, b] - alpha * step
            corrected_v[s, b] = value
            weighted[s, b] = weight(table_s, s, b) * value
        out += start_all(sends(weighted, table_s, outgoing, sems, s))
        out += start_all(
            copies_of(
                [local_v.at[s], corrected_v.at[s]], [step_out.at[s], out_field.at[s]],
                more, 3 + 4 * subs + 2 * s,
            )
        )
    out += start_all(rims(weighted, upward, downward, sems))
    wait_all(out)


def third_kernel(
    table, landed, responses, basis, local_part, older_step, corrected, scalars,
    weighted_out, factors, outgoing, upward, downward,
    landed_v, responses_v, basis_v, scalars_v, local_v, older_v, corrected_v, weighted,
    factors_v, table_s, sems, more,
):
    subs, blocks, cases, width = corrected.shape
    primal = basis.shape[0] // 4
    coarse = primal // subs
    routes = start_all([pltpu.make_async_copy(table, table_s, sems.at[0, 0])])
    small = start_all(
        copies_of(
            [landed, responses, basis, scalars],
            [landed_v, responses_v, basis_v, scalars_v], more, 0,
        )
    )
    fields = [
        start_all(copies_of(parts_of(source), parts_of(target), more, 4 + i * subs))
        for i, (source, target) in enumerate(
            [(local_part, local_v), (older_step, older_v), (corrected, corrected_v)]
        )
    ]
    wait_all(small)
    wait_all(routes)
    totals, rows = everyone(landed_v[...], coarse + 1)
    dot1 = totals[:cases]
    own = totals[cases : 2 * cases]
    cross = totals[2 * cases : 3 * cases]
    beta = dot1 / scalars_v[0]
    curv1 = own + beta * (cross + beta * scalars_v[1])
    alpha = dot1 / curv1
    factors_v[0] = scalars_v[2] + alpha * beta
    factors_v[1] = alpha
    out = start_all(copies_of([factors_v], [factors], more, 4 + 3 * subs))
    product = three_part(responses_v[...], rows)
    coarse_part = spread(folded(product, primal), basis_v, subs, coarse)
    for s in range(subs):
        wait_all([group[s] for group in fields])
        for b in range(blocks):
            step = local_v[s, b] + coarse_part[
                s * cases : (s + 1) * cases, b * width : (b + 1) * width
            ]
            value = corrected_v[s, b] - alpha * (step + beta * older_v[s, b])
            weighted[s, b] = weight(table_s, s, b) * value
        out += start_all(sends(weighted, table_s, outgoing, sems, s))
        out += start_all(
            copies_of([weighted.at[s]], [weighted_out.at[s]], more, 5 + 3 * subs + s)
        )
    out += start_all(rims(weighted, upward, downward, sems))
    wait_all(out)


def schur_kernel(
    fine, table, incoming, before, after, corrected, matrix,
    direction, product, outgoing, upward, downward,
    corrected_v, product_v, held, held_sems, table_s, incoming_v, rims_v, arrive_sems, sems, more,
):
    subs, blocks, cases, width = corrected.shape
    arriving = fetches(table, table_s, incoming, incoming_v, before, after, rims_v, arrive_sems)
    base_in = start_all(copies_of(parts_of(corrected), parts_of(corrected_v), more, 0))
    matrix_in = [start_all(group) for group in pieces(matrix, held, held_sems)]
    wait_all(arriving)
    out = []
    for s in range(subs):
        wait_all(base_in[s : s + 1])
        flat = []
        for b in range(blocks):
            other = received(table_s, incoming_v, rims_v, s, b)
            value = weight(table_s, s, b) * corrected_v[s, b] + other
            corrected_v[s, b] = value
            flat.append(value)
        out += start_all(copies_of([corrected_v.at[s]], [direction.at[s]], more, 8 + s))
        wait_all(matrix_in[s])
        both = applied(jnp.concatenate(flat, axis=1), held[s], fine)
        for b in range(blocks):
            product_v[s, b] = both[:, b * width : (b + 1) * width]
        out += start_all(sends(product_v, table_s, outgoing, sems, s))
        out += start_all(copies_of([product_v.at[s]], [product.at[s]], more, 12 + s))
    out += start_all(rims(product_v, upward, downward, sems))
    wait_all(out)


def last_kernel(
    table, incoming, before, after, base, out, held, table_s, incoming_v, rims_v, sems, more
):
    subs, blocks = base.shape[:2]
    arriving = fetches(table, table_s, incoming, incoming_v, before, after, rims_v, sems)
    base_in = start_all(copies_of(parts_of(base), parts_of(held), more, 0))
    wait_all(arriving)
    leaving = []
    for s in range(subs):
        wait_all(base_in[s : s + 1])
        for b in range(blocks):
            held[s, b] = held[s, b] + received(table_s, incoming_v, rims_v, s, b)
        leaving += start_all(copies_of([held.at[s]], [out.at[s]], more, subs + s))
    wait_all(leaving)


def row_numbers(shape, rows_here, groups):
    row = lax.broadcasted_iota(jnp.int32, shape, 0)
    quarter = rows_here // groups
    return row // quarter * rows_here + row % quarter


def totals_kernel(rows_here, index_period, landed, index, totals):
    groups = index.shape[0]
    lanes = landed.shape[1]
    cases = lanes // groups
    period = index_period
    value = landed[...]
    row = lax.broadcasted_iota(jnp.int32, value.shape, 0)
    high, low = split(jnp.where(lax.rem(row, period) == period - 1, 0.0, value))
    rows = jnp.concatenate([high, low], axis=1)
    height = totals.shape[0]
    number = row_numbers((height, landed.shape[0]), rows_here, groups)
    lane = lax.broadcasted_iota(jnp.int32, (height, lanes), 1) // cases
    out = jnp.zeros((height, lanes), F32)
    for a in range(groups):
        gathered = jnp.zeros((height, lanes), F32)
        for q in range(groups):
            chosen = number == index[q : q + 1, :] - a * (rows_here // groups)
            product = dotted(jnp.where(chosen, 1.0, 0.0).astype(BF16), rows)
            gathered = jnp.where(lane == q, product[:, :lanes] + product[:, lanes:], gathered)
        summed = gathered
        for q in range(1, groups):
            summed = summed + pltpu.roll(gathered, q * cases, 1)
        out = jnp.where(lane == a, summed, out)
    totals[...] = out


def responses_kernel(rows_here, columns, index, responses):
    groups = index.shape[0]
    lanes = columns.shape[1]
    primal = lanes // groups
    high, low = split(columns[...].T)
    number = row_numbers((columns.shape[0], index.shape[1]), rows_here, groups)
    for q in range(groups):
        total = jnp.zeros((2 * primal, index.shape[1]), F32)
        for a in range(groups):
            chosen = number == index[q : q + 1, :] - a * (rows_here // groups)
            both = jnp.concatenate(
                [high[a * primal : (a + 1) * primal], low[a * primal : (a + 1) * primal]], axis=0
            )
            total = total + dotted(both, jnp.where(chosen, 1.0, 0.0).astype(BF16))
        responses[q * primal : (q + 1) * primal] = total[:primal].astype(BF16)
        responses[lanes + q * primal : lanes + (q + 1) * primal] = total[primal:].astype(BF16)


def all_to_all(block, axes):
    return lax.all_to_all(block, axes, split_axis=0, concat_axis=0, tiled=True)


def local(
    loads, schur, local_inverse, coarse_basis, coarse_inverse, primal_index, nbr_sub, nbr_block
):
    subs, blocks, cases, width = loads.shape
    coarse = primal_index.shape[1]
    primal = subs * coarse
    groups = subs
    faces = blocks - 2
    peers = lax.axis_size("sub")
    slabs = lax.axis_size("grp")
    devices = peers * slabs
    rows_here, prim_count = coarse_inverse.shape
    capacity = max(2, (subs * faces + peers - 2) // (peers - 1))
    period = coarse + 1
    size = blocks * width
    field_shape = loads.shape
    rim = (subs, cases, width)
    slot_shape = (peers, capacity * cases, width)
    face_sems = pltpu.SemaphoreType.DMA((subs, blocks))
    held_scratch = [pltpu.VMEM((subs, size, size), BF16), pltpu.SemaphoreType.DMA((subs, PIECES))]
    field_scratch = pltpu.VMEM(field_shape, F32)
    more_sems = pltpu.SemaphoreType.DMA((32,))
    field_bytes = 4 * subs * blocks * cases * width
    matrix_bytes = 2 * subs * size * size
    matrix_flops = 4 * subs * cases * size * size

    send_slots, recv_slots = face_routes(nbr_sub, nbr_block, peers, capacity)
    table = jnp.concatenate([nbr_sub, send_slots, recv_slots], axis=0)
    table = jnp.pad(table, ((0, 16 - 3 * subs), (0, width - blocks)))
    table_scratch = pltpu.SMEM(table.shape, jnp.int32)
    arrive_sems = pltpu.SemaphoreType.DMA((4,))
    rims_scratch = pltpu.VMEM((2, subs, cases, width), F32)
    slots_scratch = pltpu.VMEM((peers, capacity * cases, width), F32)
    up = [(i, i + 1) for i in range(slabs - 1)]
    down = [(j, i) for i, j in up]

    def exchange(outgoing, upward, downward):
        incoming = all_to_all(outgoing, "sub")
        before = lax.ppermute(upward, "grp", up)
        after = lax.ppermute(downward, "grp", down)
        return incoming, before, after

    def gather_rows(message):
        message = message.reshape(devices, period, 1, width)
        return all_to_all(message, AXES).reshape(devices * period, width)

    *packed, index_row = pl.pallas_call(
        pack_kernel,
        out_shape=(
            shape((peers, capacity * cases + 8, width)), shape(rim), shape(rim),
            shape((8, width)),
        ),
        in_specs=[SMEM, SMEM, VMEM],
        out_specs=(HBM, HBM, HBM, VMEM),
        scratch_shapes=[
            pltpu.VMEM((peers, 8, width), F32), face_sems, pltpu.SemaphoreType.DMA(())
        ],
        compiler_params=params(),
        cost_estimate=cost(0, 2 * field_bytes),
        name="pack",
    )(table, primal_index, loads)
    incoming, before, after = exchange(*packed)
    slab_index = incoming[:, capacity * cases, :primal].astype(jnp.int32).reshape(-1)

    flat_basis = coarse_basis.reshape(primal, size)
    basis_high = lax.reduce_precision(flat_basis, 8, 7)
    basis_low = flat_basis - basis_high
    basis = jnp.concatenate([basis_high, basis_low, basis_high, basis_low], axis=0).astype(BF16)

    def project(incoming, base, before, after, dots):
        return pl.pallas_call(
            functools.partial(project_kernel, len(dots)),
            out_shape=(shape(field_shape), shape((devices * period, width))),
            in_specs=[HBM] * (6 + len(dots)),
            out_specs=(HBM, HBM),
            scratch_shapes=[
                field_scratch,
                pltpu.VMEM((2 * subs * cases, size), BF16),
                pltpu.VMEM((2 * primal, size), BF16),
                pltpu.VMEM((width, width), F32),
                pltpu.VMEM((devices * period // 4, width), F32),
                table_scratch,
                pltpu.VMEM(incoming.shape, F32),
                rims_scratch,
                arrive_sems,
                more_sems,
            ],
            compiler_params=params(),
            cost_estimate=cost(8 * primal * subs * cases * size, 5 * field_bytes),
            name="project",
        )(table, incoming, before, after, base, basis, *dots)

    def inverse(field, fine):
        return pl.pallas_call(
            functools.partial(inverse_kernel, fine),
            out_shape=shape(field_shape),
            in_specs=[VMEM, HBM],
            out_specs=VMEM,
            scratch_shapes=held_scratch,
            compiler_params=params(),
            cost_estimate=cost(matrix_flops, matrix_bytes + 2 * field_bytes),
            name="inverse",
        )(field, local_inverse)

    def apply_schur(incoming, corrected, before, after, fine):
        return pl.pallas_call(
            functools.partial(schur_kernel, fine),
            out_shape=(
                shape(field_shape), shape(field_shape),
                shape(slot_shape), shape(rim), shape(rim),
            ),
            in_specs=[HBM] * 6,
            out_specs=(HBM,) * 5,
            scratch_shapes=[field_scratch] * 2
            + held_scratch
            + [table_scratch, slots_scratch, rims_scratch, arrive_sems, face_sems, more_sems],
            compiler_params=params(),
            cost_estimate=cost(matrix_flops, matrix_bytes + 6 * field_bytes),
            name="schur",
        )(
            table, incoming, before, after, corrected, schur,
        )

    def dot(a, b):
        return jnp.sum(a * b, axis=(0, 1))

    sent_shapes = (shape(slot_shape), shape(rim), shape(rim))
    sent_specs = (HBM, HBM, HBM)
    landed_scratch = pltpu.VMEM((devices * period, width), F32)
    responses_scratch = pltpu.VMEM((2 * groups * primal, devices * period), BF16)
    basis_scratch = pltpu.VMEM((4 * primal, size), BF16)
    combine_cost = cost(2 * primal * 8 * 128 * size, 8 * field_bytes)

    u0, message = project(incoming, loads, before, after, (index_row,))
    landed = gather_rows(message)

    columns_at = (
        jnp.arange(prim_count, dtype=jnp.int32)[:, None] == slab_index[None, :]
    ).astype(F32)
    asked = jnp.dot(coarse_inverse, columns_at, precision=PRECISE)
    asked = asked.reshape(groups, rows_here // groups, peers, primal).transpose(2, 1, 0, 3)
    asked = asked.reshape(peers, rows_here // groups, groups * primal)
    local0 = inverse(u0, False)
    asked, landed, local0 = lax.optimization_barrier((asked, landed, local0))
    columns = all_to_all(asked, "sub").reshape(-1, groups * primal)

    index = landed.reshape(devices, period, width)[:, coarse, :primal].astype(jnp.int32)
    index = index.reshape(devices, subs, coarse).transpose(1, 0, 2)
    index = jnp.pad(index, ((0, 0), (0, 0), (0, 1)), constant_values=-prim_count)
    index = index.reshape(subs, devices * period)
    height = prim_count // groups
    totals = pl.pallas_call(
        functools.partial(totals_kernel, rows_here, period),
        out_shape=shape((height, width)),
        in_specs=[VMEM, VMEM],
        out_specs=VMEM,
        compiler_params=params(),
        cost_estimate=cost(4 * prim_count * devices * period * groups * width, 2 * field_bytes),
        name="totals",
    )(landed, index)

    c0, *packed = pl.pallas_call(
        first_kernel,
        out_shape=(shape(field_shape),) + sent_shapes,
        in_specs=[HBM] * 5,
        out_specs=(HBM,) + sent_specs,
        scratch_shapes=[
            pltpu.VMEM((height, width), F32), pltpu.VMEM((height, width), F32), basis_scratch,
            field_scratch, field_scratch, table_scratch, face_sems, more_sems,
        ],
        compiler_params=params(),
        cost_estimate=combine_cost,
        name="first",
    )(table, columns, totals, basis, local0)
    incoming, before, after = exchange(*packed)
    responses = pl.pallas_call(
        functools.partial(responses_kernel, rows_here),
        out_shape=shape((2 * groups * primal, devices * period), BF16),
        in_specs=[VMEM, VMEM],
        out_specs=VMEM,
        compiler_params=params(),
        cost_estimate=cost(4 * primal * prim_count * devices * period * groups, field_bytes),
        name="responses",
    )(columns, index)
    dot0_part = dot(u0, c0)
    z0, q0, *packed = apply_schur(incoming, c0, before, after, False)
    incoming, before, after = exchange(*packed)

    v0, message = project(incoming, q0, before, after, (dot0_part, dot(z0, q0)))
    landed = gather_rows(message)
    local1 = inverse(v0, True)
    k0, c1, scalars, *packed = pl.pallas_call(
        second_kernel,
        out_shape=(
            shape(field_shape), shape(field_shape), shape((3, cases, width)),
        )
        + sent_shapes,
        in_specs=[HBM] * 6,
        out_specs=(HBM,) * 3 + sent_specs,
        scratch_shapes=[landed_scratch, responses_scratch, basis_scratch]
        + [field_scratch] * 3
        + [pltpu.VMEM((3, cases, width), F32), table_scratch, face_sems, more_sems],
        compiler_params=params(),
        cost_estimate=combine_cost,
        name="second",
    )(table, landed, responses, basis, local1, c0)
    incoming, before, after = exchange(*packed)
    dot1_part = dot(u0 - scalars[2] * v0, c1)
    z1, q1, *packed = apply_schur(incoming, c1, before, after, True)
    incoming, before, after = exchange(*packed)

    v1, message = project(incoming, q1, before, after, (dot1_part, dot(z1, q1), dot(z1, q0) + dot(z0, q1)))
    landed = gather_rows(message)
    local2 = inverse(v1, True)
    weighted, factors, *packed = pl.pallas_call(
        third_kernel,
        out_shape=(shape(field_shape), shape((2, cases, width))) + sent_shapes,
        in_specs=[HBM] * 8,
        out_specs=(HBM, HBM) + sent_specs,
        scratch_shapes=[
            landed_scratch, responses_scratch, basis_scratch, pltpu.VMEM((3, cases, width), F32)
        ]
        + [field_scratch] * 4
        + [pltpu.VMEM((2, cases, width), F32), table_scratch, face_sems, more_sems],
        compiler_params=params(),
        cost_estimate=combine_cost,
        name="third",
    )(table, landed, responses, basis, local2, k0, c1, scalars)
    incoming, before, after = exchange(*packed)
    result = factors[0] * z0 + factors[1] * z1
    precond = pl.pallas_call(
        last_kernel,
        out_shape=shape(field_shape),
        in_specs=[HBM] * 5,
        out_specs=HBM,
        scratch_shapes=[
            field_scratch, table_scratch, slots_scratch, rims_scratch, arrive_sems, more_sems
        ],
        compiler_params=params(),
        cost_estimate=cost(0, 4 * field_bytes),
        name="last",
    )(table, incoming, before, after, weighted)
    return (result, precond)


def solution(mesh):
    in_specs = (
        P(AXES, None, None, None),
        P(AXES, None, None),
        P(AXES, None, None),
        P(AXES, None, None, None),
        P("sub", None),
        P(AXES, None),
        P(AXES, None),
        P(AXES, None),
    )
    out_specs = (P(AXES, None, None, None), P(AXES, None, None, None))
    return jax.shard_map(local, mesh=mesh, in_specs=in_specs, out_specs=out_specs, check_vma=False)
```

time: 275 us -> 264 us (0.960)
  Pallas kernels: 78.3 us -> 69.4 us
  waiting for transfers between devices: 90.1 us -> 83.7 us
  other arithmetic: 4.42 us -> 10.1 us
  local copies, waits for them, and re-layouts: 11.9 us -> 6.67 us
  starting transfers between devices: 84 us -> 87.4 us
    pallas_call x10, Pallas kernels: 48 us -> 39.1 us  [the longest x2 13.2 us: apply_schur(): pl.pallas_call(functools.partial(schur_kernel, fine), out_shape=(shape(fi...]
    unnamed x80, local copies, waits for them, and re-layouts: 8.68 us -> 1.08 us
    reduce_sum x0 -> x4, other arithmetic: none -> 4.99 us  [dot(): return jnp.sum(a * b, axis=(0, 1))]
    all_to_all x10, starting transfers between devices: 57.9 us -> 61.9 us  [all_to_all(): return lax.all_to_all(block, axes, split_axis=0, concat_axis=0, tiled=True)]
    all_to_all x10, waiting for transfers between devices: 67.7 us -> 63.9 us  [all_to_all(): return lax.all_to_all(block, axes, split_axis=0, concat_axis=0, tiled=True)]
  transfers between devices with their start and end apart: 22 -> 22, of which waited for: 16 -> 15; matrix products, arithmetic and copies ran while one was open for 3% -> 6% of each run, Pallas kernels for 11% -> 12%
where the time goes in v2:
time: 264 us; the launch traced here: 262 us
  starting transfers between devices  87.4 us (33%)
  waiting for transfers between devices  83.7 us (32%)
  Pallas kernels  69.4 us (26%)
  other arithmetic  10.1 us (4%)
  local copies, waits for them, and re-layouts  6.67 us (3%)
  matrix products  3.11 us (1%)
    all_to_all x10, waiting for transfers between devices, all_to_all(): return lax.all_to_all(block, axes, split_axis=0, concat_axis=0, tiled=True)  63.9 us
    all_to_all x10, starting transfers between devices, all_to_all(): return lax.all_to_all(block, axes, split_axis=0, concat_axis=0, tiled=True)  61.9 us
    ppermute x6, waiting for transfers between devices, exchange(): after = lax.ppermute(downward, 'grp', down)  19.9 us
    ppermute x6, starting transfers between devices, exchange(): before = lax.ppermute(upward, 'grp', up)  17.7 us
    pallas_call x3, Pallas kernels, inverse(): pl.pallas_call(functools.partial(inverse_kernel, fine), out_shape=shape(f...  17.5 us
    pallas_call x2, Pallas kernels, apply_schur(): pl.pallas_call(functools.partial(schur_kernel, fine), out_shape=(shape(fi...  13.2 us
    pallas_call x3, Pallas kernels, project(): pl.pallas_call(functools.partial(project_kernel, len(dots)), out_shape=(s...  9.48 us
    ppermute x6, starting transfers between devices, exchange(): after = lax.ppermute(downward, 'grp', down)  7.75 us
  transfers between devices with their start and end apart: 22, of which 15 were waited for; matrix products, arithmetic and copies ran while one was open for 6% of the time, Pallas kernels for 12%

profile of v2, /device:TPU:1, one launch (start us, length us, event | category | flops | bytes accessed | tf_op | source)
XLA Modules:
  0.0 262.0 jit_solution(17839852888944734388)
XLA Ops:
  6.0 8.8 %all-to-all-start = ((f32[32,72,128]{2,1,0:T(8,128)}), f32[32,72,128]{2,1,0:T(8,128)}, u32[]{:S(2)}, u32[]{:S(2)}) async-start(f32[32,72,128]{2,1,0:T(8,128)} %get-tuple-element.40), calls=%async_computation | async-start | bytes 2359296 | tf_op jit(solution)/shard_map/all_to_all | solution.py:520
  14.8 3.5 %collective-permute-start = (f32[4,32,128]{2,1,0:T(8,128)S(1)}, f32[4,32,128]{2,1,0:T(8,128)S(1)}, u32[]{:S(2)}, u32[]{:S(2)}) collective-permute-start(f32[4,32,128]{2,1,0:T(8,128)S(1)} %copy-done.34), channel_id=1, source_target_pairs={{0,32},{32,64},{64,96},{1,33},{33,65},{65,97},{2,34},{34,66},{66,9... | collective-permute-start | bytes 196616 | tf_op jit(solution)/shard_map/ppermute | solution.py:561
  20.4 3.5 %collective-permute-done.1.after = f32[4,32,128]{2,1,0:T(8,128)S(1)} collective-permute-done((f32[4,32,128]{2,1,0:T(8,128)S(1)}, f32[4,32,128]{2,1,0:T(8,128)S(1)}, u32[]{:S(2)}, u32[]{:S(2)}) %collective-permute-start.1) | collective-permute-done | bytes 65568 | tf_op jit(solution)/shard_map/ppermute | solution.py:562
  23.9 8.6 %all-to-all-done.incoming = f32[32,72,128]{2,1,0:T(8,128)} async-done(((f32[32,72,128]{2,1,0:T(8,128)}), f32[32,72,128]{2,1,0:T(8,128)}, u32[]{:S(2)}, u32[]{:S(2)}) %all-to-all-start) | async-done | bytes 1179680 | tf_op jit(solution)/shard_map/all_to_all | solution.py:520
  35.7 7.9 %all-to-all-start.1 = ((f32[128,9,1,128]{3,2,1,0:T(1,128)}), f32[128,9,1,128]{3,2,1,0:T(1,128)}, u32[]{:S(2)}, u32[]{:S(2)}) async-start(f32[128,9,1,128]{3,2,1,0:T(1,128)} %bitcast.29), calls=%async_computation.1 | async-start | bytes 1179648 | tf_op jit(solution)/shard_map/all_to_all | solution.py:520
  49.9 5.8 %inverse.3.local_part = f32[4,8,32,128]{3,2,1,0:T(8,128)} custom-call(f32[4,8,32,128]{3,2,1,0:T(8,128)} %get-tuple-element.45.field, bf16[4,1024,1024]{2,1,0:T(8,128)(2,1)} %matrix.9), custom_call_target="tpu_custom_call" | custom-call | flops 536870912 | bytes 9437184 | tf_op jit(solution)/shard_map/inverse/pallas_call | solution.py:616
  57.7 5.4 %all-to-all-start.2 = ((f32[32,16,128]{2,1,0:T(8,128)}), f32[32,16,128]{2,1,0:T(8,128)S(1)}, u32[]{:S(2)}, u32[]{:S(2)}) async-start(f32[32,16,128]{2,1,0:T(8,128)} %reshape.92), calls=%async_computation.2 | async-start | bytes 524288 | tf_op jit(solution)/shard_map/all_to_all | solution.py:520
  65.4 7.5 %totals.1 = f32[512,128]{1,0:T(8,128)} custom-call(f32[1152,128]{1,0:T(8,128)} %bitcast.3.landed, s32[4,1152]{1,0:T(4,128)} %reshape.98.index), custom_call_target="tpu_custom_call" | custom-call | flops 4831838208 | bytes 1048576 | tf_op jit(solution)/shard_map/totals/pallas_call | solution.py:674
  73.7 3.4 %first.1 = (f32[4,8,32,128]{3,2,1,0:T(8,128)}, f32[32,64,128]{2,1,0:T(8,128)}, f32[4,32,128]{2,1,0:T(8,128)}, f32[4,32,128]{2,1,0:T(8,128)}) custom-call(s32[16,128]{1,0:T(8,128)} %pad.8.table, f32[512,128]{1,0:T(8,128)} %bitcast.27, f32[512,128]{1,0:T(8,128)} %totals.1, bf16[128,1024]{1,0:T(8,128)(2,1)} %pad_maximum_fusion.basis, ...), custom_call_target="tpu_custom_call" | custom-call | flops 67108864 | bytes 4194304 | tf_op jit(solution)/shard_map/first/pallas_call | solution.py:684
  77.1 7.6 %all-to-all-start.3 = ((f32[32,64,128]{2,1,0:T(8,128)}), f32[32,64,128]{2,1,0:T(8,128)}, u32[]{:S(2)}, u32[]{:S(2)}) async-start(f32[32,64,128]{2,1,0:T(8,128)} %get-tuple-element.49), calls=%async_computation.3 | async-start | bytes 2097152 | tf_op jit(solution)/shard_map/all_to_all | solution.py:520
  84.7 3.4 %collective-permute-start.2 = (f32[4,32,128]{2,1,0:T(8,128)S(1)}, f32[4,32,128]{2,1,0:T(8,128)S(1)}, u32[]{:S(2)}, u32[]{:S(2)}) collective-permute-start(f32[4,32,128]{2,1,0:T(8,128)S(1)} %copy-done.38), channel_id=1, source_target_pairs={{0,32},{32,64},{64,96},{1,33},{33,65},{65,97},{2,34},{34,66},{66,9... | collective-permute-start | bytes 196616 | tf_op jit(solution)/shard_map/ppermute | solution.py:561
  89.4 4.1 %collective-permute-done.3.after = f32[4,32,128]{2,1,0:T(8,128)S(1)} collective-permute-done((f32[4,32,128]{2,1,0:T(8,128)S(1)}, f32[4,32,128]{2,1,0:T(8,128)S(1)}, u32[]{:S(2)}, u32[]{:S(2)}) %collective-permute-start.3) | collective-permute-done | bytes 65568 | tf_op jit(solution)/shard_map/ppermute | solution.py:562
  93.5 8.4 %all-to-all-done.3.incoming = f32[32,64,128]{2,1,0:T(8,128)} async-done(((f32[32,64,128]{2,1,0:T(8,128)}), f32[32,64,128]{2,1,0:T(8,128)}, u32[]{:S(2)}, u32[]{:S(2)}) %all-to-all-start.3) | async-done | bytes 1048608 | tf_op jit(solution)/shard_map/all_to_all | solution.py:520
  101.9 6.5 %schur.2 = (f32[4,8,32,128]{3,2,1,0:T(8,128)}, f32[4,8,32,128]{3,2,1,0:T(8,128)}, f32[32,64,128]{2,1,0:T(8,128)}, f32[4,32,128]{2,1,0:T(8,128)}, f32[4,32,128]{2,1,0:T(8,128)}) custom-call(s32[16,128]{1,0:T(8,128)} %pad.8.table, f32[32,64,128]{2,1,0:T(8,128)} %all-to-all-done.3.incoming, f32[4,32,128]{2,1,0:T(8,128)} %copy-done.14, ...), custom_call_target="tpu_custom_call" | custom-call | flops 536870912 | bytes 11534336 | tf_op jit(solution)/shard_map/schur/pallas_call | solution.py:628
  108.5 4.8 %all-to-all-start.4 = ((f32[32,64,128]{2,1,0:T(8,128)}), f32[32,64,128]{2,1,0:T(8,128)}, u32[]{:S(2)}, u32[]{:S(2)}) async-start(f32[32,64,128]{2,1,0:T(8,128)} %get-tuple-element.53), calls=%async_computation.4 | async-start | bytes 2097152 | tf_op jit(solution)/shard_map/all_to_all | solution.py:520
  122.9 7.8 %all-to-all-done.4.incoming = f32[32,64,128]{2,1,0:T(8,128)} async-done(((f32[32,64,128]{2,1,0:T(8,128)}), f32[32,64,128]{2,1,0:T(8,128)}, u32[]{:S(2)}, u32[]{:S(2)}) %all-to-all-start.4) | async-done | bytes 1048608 | tf_op jit(solution)/shard_map/all_to_all | solution.py:520
  133.8 6.5 %all-to-all-start.5 = ((f32[128,9,1,128]{3,2,1,0:T(1,128)}), f32[128,9,1,128]{3,2,1,0:T(1,128)}, u32[]{:S(2)}, u32[]{:S(2)}) async-start(f32[128,9,1,128]{3,2,1,0:T(1,128)} %bitcast.30), calls=%async_computation.5 | async-start | bytes 1179648 | tf_op jit(solution)/shard_map/all_to_all | solution.py:520
  140.3 5.3 %responses.1 = bf16[256,1152]{1,0:T(8,128)(2,1)} custom-call(f32[512,128]{1,0:T(8,128)} %bitcast.28, s32[4,1152]{1,0:T(4,128)} %reshape.98.index), custom_call_target="tpu_custom_call" | custom-call | flops 1207959552 | bytes 524288 | tf_op jit(solution)/shard_map/responses/pallas_call | solution.py:698
  145.6 5.8 %inverse.4.local_part = f32[4,8,32,128]{3,2,1,0:T(8,128)} custom-call(f32[4,8,32,128]{3,2,1,0:T(8,128)} %get-tuple-element.59.field, bf16[4,1024,1024]{2,1,0:T(8,128)(2,1)} %matrix.9), custom_call_target="tpu_custom_call" | custom-call | flops 536870912 | bytes 9437184 | tf_op jit(solution)/shard_map/inverse/pallas_call | solution.py:616
  154.4 4.0 %second.1 = (f32[4,8,32,128]{3,2,1,0:T(8,128)}, f32[4,8,32,128]{3,2,1,0:T(8,128)}, f32[3,32,128]{2,1,0:T(8,128)}, f32[32,64,128]{2,1,0:T(8,128)}, f32[4,32,128]{2,1,0:T(8,128)}, /*index=5*/f32[4,32,128]{2,1,0:T(8,128)}) custom-call(s32[16,128]{1,0:T(8,128)} %pad.8.table, f32[1152,128]{1,0:T(8,128)} %bitcast.8.landed, bf16[256,1152]{1,0:T(8,128)(2,1)} %responses.1, ...), custom_call_target="tpu_custom_call" | custom-call | flops 67108864 | bytes 4194304 | tf_op jit(solution)/shard_map/second/pallas_call | solution.py:714
  158.5 5.3 %all-to-all-start.6 = ((f32[32,64,128]{2,1,0:T(8,128)}), f32[32,64,128]{2,1,0:T(8,128)}, u32[]{:S(2)}, u32[]{:S(2)}) async-start(f32[32,64,128]{2,1,0:T(8,128)} %get-tuple-element.60), calls=%async_computation.6 | async-start | bytes 2097152 | tf_op jit(solution)/shard_map/all_to_all | solution.py:520
  167.8 4.1 %collective-permute-done.7.after = f32[4,32,128]{2,1,0:T(8,128)S(1)} collective-permute-done((f32[4,32,128]{2,1,0:T(8,128)S(1)}, f32[4,32,128]{2,1,0:T(8,128)S(1)}, u32[]{:S(2)}, u32[]{:S(2)}) %collective-permute-start.7) | collective-permute-done | bytes 65568 | tf_op jit(solution)/shard_map/ppermute | solution.py:562
  171.9 9.2 %all-to-all-done.6.incoming = f32[32,64,128]{2,1,0:T(8,128)} async-done(((f32[32,64,128]{2,1,0:T(8,128)}), f32[32,64,128]{2,1,0:T(8,128)}, u32[]{:S(2)}, u32[]{:S(2)}) %all-to-all-start.6) | async-done | bytes 1048608 | tf_op jit(solution)/shard_map/all_to_all | solution.py:520
  181.1 6.6 %schur.3 = (f32[4,8,32,128]{3,2,1,0:T(8,128)}, f32[4,8,32,128]{3,2,1,0:T(8,128)}, f32[32,64,128]{2,1,0:T(8,128)}, f32[4,32,128]{2,1,0:T(8,128)}, f32[4,32,128]{2,1,0:T(8,128)}) custom-call(s32[16,128]{1,0:T(8,128)} %pad.8.table, f32[32,64,128]{2,1,0:T(8,128)} %all-to-all-done.6.incoming, f32[4,32,128]{2,1,0:T(8,128)} %copy-done.15, ...), custom_call_target="tpu_custom_call" | custom-call | flops 536870912 | bytes 11534336 | tf_op jit(solution)/shard_map/schur/pallas_call | solution.py:628
  187.8 4.8 %all-to-all-start.7 = ((f32[32,64,128]{2,1,0:T(8,128)}), f32[32,64,128]{2,1,0:T(8,128)}, u32[]{:S(2)}, u32[]{:S(2)}) async-start(f32[32,64,128]{2,1,0:T(8,128)} %get-tuple-element.64), calls=%async_computation.7 | async-start | bytes 2097152 | tf_op jit(solution)/shard_map/all_to_all | solution.py:520
  203.1 6.8 %all-to-all-done.7.incoming = f32[32,64,128]{2,1,0:T(8,128)} async-done(((f32[32,64,128]{2,1,0:T(8,128)}), f32[32,64,128]{2,1,0:T(8,128)}, u32[]{:S(2)}, u32[]{:S(2)}) %all-to-all-start.7) | async-done | bytes 1048608 | tf_op jit(solution)/shard_map/all_to_all | solution.py:520
  213.1 5.7 %all-to-all-start.8 = ((f32[128,9,1,128]{3,2,1,0:T(1,128)}), f32[128,9,1,128]{3,2,1,0:T(1,128)}, u32[]{:S(2)}, u32[]{:S(2)}) async-start(f32[128,9,1,128]{3,2,1,0:T(1,128)} %bitcast.31), calls=%async_computation.8 | async-start | bytes 1179648 | tf_op jit(solution)/shard_map/all_to_all | solution.py:520
  218.8 5.8 %inverse.5.local_part = f32[4,8,32,128]{3,2,1,0:T(8,128)} custom-call(f32[4,8,32,128]{3,2,1,0:T(8,128)} %get-tuple-element.71.field, bf16[4,1024,1024]{2,1,0:T(8,128)(2,1)} %matrix.9), custom_call_target="tpu_custom_call" | custom-call | flops 536870912 | bytes 9437184 | tf_op jit(solution)/shard_map/inverse/pallas_call | solution.py:616
  224.6 8.3 %all-to-all-done.8 = f32[128,9,1,128]{3,2,1,0:T(1,128)} async-done(((f32[128,9,1,128]{3,2,1,0:T(1,128)}), f32[128,9,1,128]{3,2,1,0:T(1,128)}, u32[]{:S(2)}, u32[]{:S(2)}) %all-to-all-start.8) | async-done | bytes 589856 | tf_op jit(solution)/shard_map/all_to_all | solution.py:520
  232.9 3.8 %third.1 = (f32[4,8,32,128]{3,2,1,0:T(8,128)}, f32[2,32,128]{2,1,0:T(8,128)}, f32[32,64,128]{2,1,0:T(8,128)}, f32[4,32,128]{2,1,0:T(8,128)}, f32[4,32,128]{2,1,0:T(8,128)}) custom-call(s32[16,128]{1,0:T(8,128)} %pad.8.table, f32[1152,128]{1,0:T(8,128)} %bitcast.11.landed, bf16[256,1152]{1,0:T(8,128)(2,1)} %responses.1, ...), custom_call_target="tpu_custom_call" | custom-call | flops 67108864 | bytes 4194304 | tf_op jit(solution)/shard_map/third/pallas_call | solution.py:737
  236.7 5.3 %all-to-all-start.9 = ((f32[32,64,128]{2,1,0:T(8,128)}), f32[32,64,128]{2,1,0:T(8,128)}, u32[]{:S(2)}, u32[]{:S(2)}) async-start(f32[32,64,128]{2,1,0:T(8,128)} %get-tuple-element.74), calls=%async_computation.9 | async-start | bytes 2097152 | tf_op jit(solution)/shard_map/all_to_all | solution.py:520
  249.5 9.8 %all-to-all-done.9.incoming = f32[32,64,128]{2,1,0:T(8,128)} async-done(((f32[32,64,128]{2,1,0:T(8,128)}), f32[32,64,128]{2,1,0:T(8,128)}, u32[]{:S(2)}, u32[]{:S(2)}) %all-to-all-start.9) | async-done | bytes 1048608 | tf_op jit(solution)/shard_map/all_to_all | solution.py:520
  (135 shorter events, 66.2 us)
Async XLA Ops:
  0.6 44.0 %copy-start = (f32[64,2048]{1,0:T(8,128)S(1)}, f32[64,2048]{1,0:T(8,128)}, u32[]{:S(2)}) copy-start(f32[64,2048]{1,0:T(8,128)} %param.12) | copy-start | bytes 1572868
  0.6 19.0 %copy-start.13 = (f32[4,8,8,128]{3,2,1,0:T(8,128)S(1)}, f32[4,8,8,128]{3,2,1,0:T(8,128)}, u32[]{:S(2)}) copy-start(f32[4,8,8,128]{3,2,1,0:T(8,128)} %param.11) | copy-start | bytes 393220
  6.0 12.4 %copy-start.31 = (f32[4,32,128]{2,1,0:T(8,128)S(1)}, f32[4,32,128]{2,1,0:T(8,128)}, u32[]{:S(2)}) copy-start(f32[4,32,128]{2,1,0:T(8,128)} %get-tuple-element.42) | copy-start | bytes 196612
  6.0 26.5 %all-to-all-start = ((f32[32,72,128]{2,1,0:T(8,128)}), f32[32,72,128]{2,1,0:T(8,128)}, u32[]{:S(2)}, u32[]{:S(2)}) async-start(f32[32,72,128]{2,1,0:T(8,128)} %get-tuple-element.40), calls=%async_computation | async-start | bytes 2359296 | tf_op jit(solution)/shard_map/all_to_all | solution.py:520
  14.8 5.7 %collective-permute-start = (f32[4,32,128]{2,1,0:T(8,128)S(1)}, f32[4,32,128]{2,1,0:T(8,128)S(1)}, u32[]{:S(2)}, u32[]{:S(2)}) collective-permute-start(f32[4,32,128]{2,1,0:T(8,128)S(1)} %copy-done.34), channel_id=1, source_target_pairs={{0,32},{32,64},{64,96},{1,33},{33,65},{65,97},{2,34},{34,66},{66,9... | collective-permute-start | bytes 196616 | tf_op jit(solution)/shard_map/ppermute | solution.py:561
  18.3 5.6 %collective-permute-start.1 = (f32[4,32,128]{2,1,0:T(8,128)S(1)}, f32[4,32,128]{2,1,0:T(8,128)S(1)}, u32[]{:S(2)}, u32[]{:S(2)}) collective-permute-start(f32[4,32,128]{2,1,0:T(8,128)S(1)} %copy-done.31), channel_id=1, source_target_pairs={{32,0},{64,32},{96,64},{33,1},{65,33},{97,65},{34,2},{66,34},{98,6... | collective-permute-start | bytes 196616 | tf_op jit(solution)/shard_map/ppermute | solution.py:562
  20.4 12.1 %copy-start.21 = (f32[4,32,128]{2,1,0:T(8,128)}, f32[4,32,128]{2,1,0:T(8,128)S(1)}, u32[]{:S(2)}) copy-start(f32[4,32,128]{2,1,0:T(8,128)S(1)} %collective-permute-done.before) | copy-start | bytes 196612
  35.7 22.1 %all-to-all-start.1 = ((f32[128,9,1,128]{3,2,1,0:T(1,128)}), f32[128,9,1,128]{3,2,1,0:T(1,128)}, u32[]{:S(2)}, u32[]{:S(2)}) async-start(f32[128,9,1,128]{3,2,1,0:T(1,128)} %bitcast.29), calls=%async_computation.1 | async-start | bytes 1179648 | tf_op jit(solution)/shard_map/all_to_all | solution.py:520
  57.7 15.2 %all-to-all-start.2 = ((f32[32,16,128]{2,1,0:T(8,128)}), f32[32,16,128]{2,1,0:T(8,128)S(1)}, u32[]{:S(2)}, u32[]{:S(2)}) async-start(f32[32,16,128]{2,1,0:T(8,128)} %reshape.92), calls=%async_computation.2 | async-start | bytes 524288 | tf_op jit(solution)/shard_map/all_to_all | solution.py:520
  77.1 24.8 %all-to-all-start.3 = ((f32[32,64,128]{2,1,0:T(8,128)}), f32[32,64,128]{2,1,0:T(8,128)}, u32[]{:S(2)}, u32[]{:S(2)}) async-start(f32[32,64,128]{2,1,0:T(8,128)} %get-tuple-element.49), calls=%async_computation.3 | async-start | bytes 2097152 | tf_op jit(solution)/shard_map/all_to_all | solution.py:520
  84.7 4.7 %collective-permute-start.2 = (f32[4,32,128]{2,1,0:T(8,128)S(1)}, f32[4,32,128]{2,1,0:T(8,128)S(1)}, u32[]{:S(2)}, u32[]{:S(2)}) collective-permute-start(f32[4,32,128]{2,1,0:T(8,128)S(1)} %copy-done.38), channel_id=1, source_target_pairs={{0,32},{32,64},{64,96},{1,33},{33,65},{65,97},{2,34},{34,66},{66,9... | collective-permute-start | bytes 196616 | tf_op jit(solution)/shard_map/ppermute | solution.py:561
  88.1 5.4 %collective-permute-start.3 = (f32[4,32,128]{2,1,0:T(8,128)S(1)}, f32[4,32,128]{2,1,0:T(8,128)S(1)}, u32[]{:S(2)}, u32[]{:S(2)}) collective-permute-start(f32[4,32,128]{2,1,0:T(8,128)S(1)} %copy-done.36), channel_id=1, source_target_pairs={{32,0},{64,32},{96,64},{33,1},{65,33},{97,65},{34,2},{66,34},{98,6... | collective-permute-start | bytes 196616 | tf_op jit(solution)/shard_map/ppermute | solution.py:562
  89.4 12.5 %copy-start.14 = (f32[4,32,128]{2,1,0:T(8,128)}, f32[4,32,128]{2,1,0:T(8,128)S(1)}, u32[]{:S(2)}) copy-start(f32[4,32,128]{2,1,0:T(8,128)S(1)} %collective-permute-done.2.before) | copy-start | bytes 196612
  108.5 22.1 %all-to-all-start.4 = ((f32[32,64,128]{2,1,0:T(8,128)}), f32[32,64,128]{2,1,0:T(8,128)}, u32[]{:S(2)}, u32[]{:S(2)}) async-start(f32[32,64,128]{2,1,0:T(8,128)} %get-tuple-element.53), calls=%async_computation.4 | async-start | bytes 2097152 | tf_op jit(solution)/shard_map/all_to_all | solution.py:520
  114.0 5.4 %collective-permute-start.4 = (f32[4,32,128]{2,1,0:T(8,128)S(1)}, f32[4,32,128]{2,1,0:T(8,128)S(1)}, u32[]{:S(2)}, u32[]{:S(2)}) collective-permute-start(f32[4,32,128]{2,1,0:T(8,128)S(1)} %copy-done.35), channel_id=1, source_target_pairs={{0,32},{32,64},{64,96},{1,33},{33,65},{65,97},{2,34},{34,66},{66,9... | collective-permute-start | bytes 196616 | tf_op jit(solution)/shard_map/ppermute | solution.py:561
  117.4 5.4 %collective-permute-start.5 = (f32[4,32,128]{2,1,0:T(8,128)S(1)}, f32[4,32,128]{2,1,0:T(8,128)S(1)}, u32[]{:S(2)}, u32[]{:S(2)}) collective-permute-start(f32[4,32,128]{2,1,0:T(8,128)S(1)} %copy-done.32), channel_id=1, source_target_pairs={{32,0},{64,32},{96,64},{33,1},{65,33},{97,65},{34,2},{66,34},{98,6... | collective-permute-start | bytes 196616 | tf_op jit(solution)/shard_map/ppermute | solution.py:562
  119.5 11.2 %copy-start.24 = (f32[4,32,128]{2,1,0:T(8,128)}, f32[4,32,128]{2,1,0:T(8,128)S(1)}, u32[]{:S(2)}) copy-start(f32[4,32,128]{2,1,0:T(8,128)S(1)} %collective-permute-done.4.before) | copy-start | bytes 196612
  133.8 20.6 %all-to-all-start.5 = ((f32[128,9,1,128]{3,2,1,0:T(1,128)}), f32[128,9,1,128]{3,2,1,0:T(1,128)}, u32[]{:S(2)}, u32[]{:S(2)}) async-start(f32[128,9,1,128]{3,2,1,0:T(1,128)} %bitcast.30), calls=%async_computation.5 | async-start | bytes 1179648 | tf_op jit(solution)/shard_map/all_to_all | solution.py:520
  158.5 22.6 %all-to-all-start.6 = ((f32[32,64,128]{2,1,0:T(8,128)}), f32[32,64,128]{2,1,0:T(8,128)}, u32[]{:S(2)}, u32[]{:S(2)}) async-start(f32[32,64,128]{2,1,0:T(8,128)} %get-tuple-element.60), calls=%async_computation.6 | async-start | bytes 2097152 | tf_op jit(solution)/shard_map/all_to_all | solution.py:520
  163.8 4.0 %collective-permute-start.6 = (f32[4,32,128]{2,1,0:T(8,128)S(1)}, f32[4,32,128]{2,1,0:T(8,128)S(1)}, u32[]{:S(2)}, u32[]{:S(2)}) collective-permute-start(f32[4,32,128]{2,1,0:T(8,128)S(1)} %copy-done.37), channel_id=1, source_target_pairs={{0,32},{32,64},{64,96},{1,33},{33,65},{65,97},{2,34},{34,66},{66,9... | collective-permute-start | bytes 196616 | tf_op jit(solution)/shard_map/ppermute | solution.py:561
  166.5 5.4 %collective-permute-start.7 = (f32[4,32,128]{2,1,0:T(8,128)S(1)}, f32[4,32,128]{2,1,0:T(8,128)S(1)}, u32[]{:S(2)}, u32[]{:S(2)}) collective-permute-start(f32[4,32,128]{2,1,0:T(8,128)S(1)} %copy-done.33), channel_id=1, source_target_pairs={{32,0},{64,32},{96,64},{33,1},{65,33},{97,65},{34,2},{66,34},{98,6... | collective-permute-start | bytes 196616 | tf_op jit(solution)/shard_map/ppermute | solution.py:562
  167.8 13.3 %copy-start.15 = (f32[4,32,128]{2,1,0:T(8,128)}, f32[4,32,128]{2,1,0:T(8,128)S(1)}, u32[]{:S(2)}) copy-start(f32[4,32,128]{2,1,0:T(8,128)S(1)} %collective-permute-done.6.before) | copy-start | bytes 196612
  187.8 11.2 %copy-start.6 = (f32[4,8,32,128]{3,2,1,0:T(8,128)S(1)}, f32[4,8,32,128]{3,2,1,0:T(8,128)}, u32[]{:S(2)}) copy-start(f32[4,8,32,128]{3,2,1,0:T(8,128)} %get-tuple-element.57) | copy-start | bytes 1572868
  187.8 11.2 %copy-start.9 = (f32[4,8,32,128]{3,2,1,0:T(8,128)S(1)}, f32[4,8,32,128]{3,2,1,0:T(8,128)}, u32[]{:S(2)}) copy-start(f32[4,8,32,128]{3,2,1,0:T(8,128)} %get-tuple-element.56.base) | copy-start | bytes 1572868
  187.8 22.1 %all-to-all-start.7 = ((f32[32,64,128]{2,1,0:T(8,128)}), f32[32,64,128]{2,1,0:T(8,128)}, u32[]{:S(2)}, u32[]{:S(2)}) async-start(f32[32,64,128]{2,1,0:T(8,128)} %get-tuple-element.64), calls=%async_computation.7 | async-start | bytes 2097152 | tf_op jit(solution)/shard_map/all_to_all | solution.py:520
  195.1 6.4 %collective-permute-start.8 = (f32[4,32,128]{2,1,0:T(8,128)S(1)}, f32[4,32,128]{2,1,0:T(8,128)S(1)}, u32[]{:S(2)}, u32[]{:S(2)}) collective-permute-start(f32[4,32,128]{2,1,0:T(8,128)S(1)} %copy-done.29), channel_id=1, source_target_pairs={{0,32},{32,64},{64,96},{1,33},{33,65},{65,97},{2,34},{34,66},{66,9... | collective-permute-start | bytes 196616 | tf_op jit(solution)/shard_map/ppermute | solution.py:561
  197.6 5.4 %collective-permute-start.9 = (f32[4,32,128]{2,1,0:T(8,128)S(1)}, f32[4,32,128]{2,1,0:T(8,128)S(1)}, u32[]{:S(2)}, u32[]{:S(2)}) collective-permute-start(f32[4,32,128]{2,1,0:T(8,128)S(1)} %copy-done.27), channel_id=1, source_target_pairs={{32,0},{64,32},{96,64},{33,1},{65,33},{97,65},{34,2},{66,34},{98,6... | collective-permute-start | bytes 196616 | tf_op jit(solution)/shard_map/ppermute | solution.py:562
  213.1 19.8 %all-to-all-start.8 = ((f32[128,9,1,128]{3,2,1,0:T(1,128)}), f32[128,9,1,128]{3,2,1,0:T(1,128)}, u32[]{:S(2)}, u32[]{:S(2)}) async-start(f32[128,9,1,128]{3,2,1,0:T(1,128)} %bitcast.31), calls=%async_computation.8 | async-start | bytes 1179648 | tf_op jit(solution)/shard_map/all_to_all | solution.py:520
  236.7 22.6 %all-to-all-start.9 = ((f32[32,64,128]{2,1,0:T(8,128)}), f32[32,64,128]{2,1,0:T(8,128)}, u32[]{:S(2)}, u32[]{:S(2)}) async-start(f32[32,64,128]{2,1,0:T(8,128)} %get-tuple-element.74), calls=%async_computation.9 | async-start | bytes 2097152 | tf_op jit(solution)/shard_map/all_to_all | solution.py:520
  242.0 4.4 %collective-permute-start.10 = (f32[4,32,128]{2,1,0:T(8,128)S(1)}, f32[4,32,128]{2,1,0:T(8,128)S(1)}, u32[]{:S(2)}, u32[]{:S(2)}) collective-permute-start(f32[4,32,128]{2,1,0:T(8,128)S(1)} %copy-done.30), channel_id=1, source_target_pairs={{0,32},{32,64},{64,96},{1,33},{33,65},{65,97},{2,34},{34,66},{66,9... | collective-permute-start | bytes 196616 | tf_op jit(solution)/shard_map/ppermute | solution.py:561
  244.1 5.4 %collective-permute-start.11 = (f32[4,32,128]{2,1,0:T(8,128)S(1)}, f32[4,32,128]{2,1,0:T(8,128)S(1)}, u32[]{:S(2)}, u32[]{:S(2)}) collective-permute-start(f32[4,32,128]{2,1,0:T(8,128)S(1)} %copy-done.28), channel_id=1, source_target_pairs={{32,0},{64,32},{96,64},{33,1},{65,33},{97,65},{34,2},{66,34},{98,6... | collective-permute-start | bytes 196616 | tf_op jit(solution)/shard_map/ppermute | solution.py:562
  246.4 13.0 %copy-start.19 = (f32[4,32,128]{2,1,0:T(8,128)}, f32[4,32,128]{2,1,0:T(8,128)S(1)}, u32[]{:S(2)}) copy-start(f32[4,32,128]{2,1,0:T(8,128)S(1)} %collective-permute-done.10.before) | copy-start | bytes 196612
  (29 other events, 223.7 us)

commit v3 on v2

--- a/solution.py
+++ b/solution.py
@@ -472,42 +472,50 @@
     return row // quarter * rows_here + row % quarter
 
 
-def totals_kernel(rows_here, index_period, landed, index, totals):
-    groups = index.shape[0]
-    lanes = landed.shape[1]
+def totals_kernel(rows_here, period, landed, index, totals, landed_v, index_v, totals_v, sems):
+    groups, width = index.shape
+    height, lanes = totals.shape
     cases = lanes // groups
-    period = index_period
-    value = landed[...]
+    quarter = rows_here // groups
+    copies = start_all(copies_of([index, landed], [index_v, landed_v], sems, 0))
+    copies[0].wait()
+    unknowns = index_v[...]
+    place = lax.div(unknowns, rows_here) * quarter + lax.rem(unknowns, quarter)
+    place = jnp.where(unknowns >= 0, place, -1)
+    group = lax.rem(lax.div(unknowns, quarter), groups)
+    turned = jnp.concatenate([group, group], axis=0).astype(F32).T
+    copies[1].wait()
+    value = landed_v[...]
     row = lax.broadcasted_iota(jnp.int32, value.shape, 0)
-    high, low = split(jnp.where(lax.rem(row, period) == period - 1, 0.0, value))
-    rows = jnp.concatenate([high, low], axis=1)
-    height = totals.shape[0]
-    number = row_numbers((height, landed.shape[0]), rows_here, groups)
-    lane = lax.broadcasted_iota(jnp.int32, (height, lanes), 1) // cases
+    value = jnp.where(lax.rem(row, period) == period - 1, 0.0, value)
+    rolled = [value] + [pltpu.roll(value, k * cases, 1) for k in range(1, groups)]
+    lane = lax.broadcasted_iota(jnp.int32, value.shape, 1) // cases
+    lane_value = lane.astype(F32)
+    number = lax.broadcasted_iota(jnp.int32, (height, width), 0)
     out = jnp.zeros((height, lanes), F32)
-    for a in range(groups):
-        gathered = jnp.zeros((height, lanes), F32)
-        for q in range(groups):
-            chosen = number == index[q : q + 1, :] - a * (rows_here // groups)
-            product = dotted(jnp.where(chosen, 1.0, 0.0).astype(BF16), rows)
-            gathered = jnp.where(lane == q, product[:, :lanes] + product[:, lanes:], gathered)
-        summed = gathered
-        for q in range(1, groups):
-            summed = summed + pltpu.roll(gathered, q * cases, 1)
-        out = jnp.where(lane == a, summed, out)
-    totals[...] = out
-
-
-def responses_kernel(rows_here, columns, index, responses):
+    for q in range(groups):
+        copied = rolled[(0 - q) % groups]
+        for a in range(1, groups):
+            copied = jnp.where(lane == a, rolled[(a - q) % groups], copied)
+        copied = jnp.where(lane_value == turned[:, q : q + 1], copied, 0.0)
+        chosen = jnp.where(number == place[q : q + 1, :], 1.0, 0.0).astype(BF16)
+        product = dotted(chosen, jnp.concatenate(split(copied), axis=1))
+        out = out + (product[:, :lanes] + product[:, lanes:])
+    totals_v[...] = out
+    wait_all(start_all(copies_of([totals_v], [totals], sems, 2)))
+
+
+def responses_kernel(rows_here, columns, index, responses, columns_v, index_v, sems):
     groups = index.shape[0]
     lanes = columns.shape[1]
     primal = lanes // groups
-    high, low = split(columns[...].T)
+    wait_all(start_all(copies_of([columns, index], [columns_v, index_v], sems, 0)))
+    high, low = split(columns_v[...].T)
     number = row_numbers((columns.shape[0], index.shape[1]), rows_here, groups)
     for q in range(groups):
         total = jnp.zeros((2 * primal, index.shape[1]), F32)
         for a in range(groups):
-            chosen = number == index[q : q + 1, :] - a * (rows_here // groups)
+            chosen = number == index_v[q : q + 1, :] - a * (rows_here // groups)
             both = jnp.concatenate(
                 [high[a * primal : (a + 1) * primal], low[a * primal : (a + 1) * primal]], axis=0
             )
@@ -648,6 +656,7 @@
 
     sent_shapes = (shape(slot_shape), shape(rim), shape(rim))
     sent_specs = (HBM, HBM, HBM)
+    index_scratch = pltpu.VMEM((subs, devices * period), jnp.int32)
     landed_scratch = pltpu.VMEM((devices * period, width), F32)
     responses_scratch = pltpu.VMEM((2 * groups * primal, devices * period), BF16)
     basis_scratch = pltpu.VMEM((4 * primal, size), BF16)
@@ -666,7 +675,7 @@
     asked, landed, local0 = lax.optimization_barrier((asked, landed, local0))
     columns = all_to_all(asked, "sub").reshape(-1, groups * primal)
 
-    index = landed.reshape(devices, period, width)[:, coarse, :primal].astype(jnp.int32)
+    index = landed.reshape(devices, period, 1, width)[:, coarse, 0, :primal].astype(jnp.int32)
     index = index.reshape(devices, subs, coarse).transpose(1, 0, 2)
     index = jnp.pad(index, ((0, 0), (0, 0), (0, 1)), constant_values=-prim_count)
     index = index.reshape(subs, devices * period)
@@ -674,10 +683,13 @@
     totals = pl.pallas_call(
         functools.partial(totals_kernel, rows_here, period),
         out_shape=shape((height, width)),
-        in_specs=[VMEM, VMEM],
-        out_specs=VMEM,
+        in_specs=[HBM, HBM],
+        out_specs=HBM,
+        scratch_shapes=[
+            landed_scratch, index_scratch, pltpu.VMEM((height, width), F32), arrive_sems
+        ],
         compiler_params=params(),
-        cost_estimate=cost(4 * prim_count * devices * period * groups * width, 2 * field_bytes),
+        cost_estimate=cost(4 * prim_count * devices * period * width, 2 * field_bytes),
         name="totals",
     )(landed, index)
 
@@ -698,8 +710,9 @@
     responses = pl.pallas_call(
         functools.partial(responses_kernel, rows_here),
         out_shape=shape((2 * groups * primal, devices * period), BF16),
-        in_specs=[VMEM, VMEM],
+        in_specs=[HBM, HBM],
         out_specs=VMEM,
+        scratch_shapes=[pltpu.VMEM((height, width), F32), index_scratch, arrive_sems],
         compiler_params=params(),
         cost_estimate=cost(4 * primal * prim_count * devices * period * groups, field_bytes),
         name="responses",

time: 264 us -> 261 us (0.989)
  Pallas kernels: 69.4 us -> 66.2 us
    pallas_call x1, Pallas kernels: 7.54 us -> 4.31 us  [local(): pl.pallas_call(functools.partial(totals_kernel, rows_here, period), out_s...]
  transfers between devices with their start and end apart: 22 -> 22, of which waited for: 15 -> 16; matrix products, arithmetic and copies ran while one was open for 6% -> 6% of each run, Pallas kernels for 12% -> 10%
where the time goes in v3:
time: 261 us; the launch traced here: 259 us
  waiting for transfers between devices  85.9 us (33%)
  starting transfers between devices  85.2 us (33%)
  Pallas kernels  66.2 us (25%)
  other arithmetic  10.1 us (4%)
  local copies, waits for them, and re-layouts  6.67 us (3%)
  matrix products  3.11 us (1%)
    all_to_all x10, waiting for transfers between devices, all_to_all(): return lax.all_to_all(block, axes, split_axis=0, concat_axis=0, tiled=True)  66 us
    all_to_all x10, starting transfers between devices, all_to_all(): return lax.all_to_all(block, axes, split_axis=0, concat_axis=0, tiled=True)  59.6 us
    ppermute x6, waiting for transfers between devices, exchange(): after = lax.ppermute(downward, 'grp', down)  19.9 us
    ppermute x6, starting transfers between devices, exchange(): before = lax.ppermute(upward, 'grp', up)  17.8 us
    pallas_call x3, Pallas kernels, inverse(): pl.pallas_call(functools.partial(inverse_kernel, fine), out_shape=shape(f...  17.5 us
    pallas_call x2, Pallas kernels, apply_schur(): pl.pallas_call(functools.partial(schur_kernel, fine), out_shape=(shape(fi...  13.2 us
    pallas_call x3, Pallas kernels, project(): pl.pallas_call(functools.partial(project_kernel, len(dots)), out_shape=(s...  9.49 us
    ppermute x6, starting transfers between devices, exchange(): after = lax.ppermute(downward, 'grp', down)  7.75 us
  transfers between devices with their start and end apart: 22, of which 16 were waited for; matrix products, arithmetic and copies ran while one was open for 6% of the time, Pallas kernels for 10%

profile of v3, /device:TPU:1, one launch (start us, length us, event | category | flops | bytes accessed | tf_op | source)
XLA Modules:
  0.0 258.8 jit_solution(8803350062743029940)
XLA Ops:
  6.0 8.8 %all-to-all-start = ((f32[32,72,128]{2,1,0:T(8,128)}), f32[32,72,128]{2,1,0:T(8,128)}, u32[]{:S(2)}, u32[]{:S(2)}) async-start(f32[32,72,128]{2,1,0:T(8,128)} %get-tuple-element.40), calls=%async_computation | async-start | bytes 2359296 | tf_op jit(solution)/shard_map/all_to_all | solution.py:528
  14.8 3.5 %collective-permute-start = (f32[4,32,128]{2,1,0:T(8,128)S(1)}, f32[4,32,128]{2,1,0:T(8,128)S(1)}, u32[]{:S(2)}, u32[]{:S(2)}) collective-permute-start(f32[4,32,128]{2,1,0:T(8,128)S(1)} %copy-done.34), channel_id=1, source_target_pairs={{0,32},{32,64},{64,96},{1,33},{33,65},{65,97},{2,34},{34,66},{66,9... | collective-permute-start | bytes 196616 | tf_op jit(solution)/shard_map/ppermute | solution.py:569
  20.4 3.5 %collective-permute-done.1.after = f32[4,32,128]{2,1,0:T(8,128)S(1)} collective-permute-done((f32[4,32,128]{2,1,0:T(8,128)S(1)}, f32[4,32,128]{2,1,0:T(8,128)S(1)}, u32[]{:S(2)}, u32[]{:S(2)}) %collective-permute-start.1) | collective-permute-done | bytes 65568 | tf_op jit(solution)/shard_map/ppermute | solution.py:570
  23.9 8.6 %all-to-all-done.incoming = f32[32,72,128]{2,1,0:T(8,128)} async-done(((f32[32,72,128]{2,1,0:T(8,128)}), f32[32,72,128]{2,1,0:T(8,128)}, u32[]{:S(2)}, u32[]{:S(2)}) %all-to-all-start) | async-done | bytes 1179680 | tf_op jit(solution)/shard_map/all_to_all | solution.py:528
  35.7 7.9 %all-to-all-start.1 = ((f32[128,9,1,128]{3,2,1,0:T(1,128)}), f32[128,9,1,128]{3,2,1,0:T(1,128)}, u32[]{:S(2)}, u32[]{:S(2)}) async-start(f32[128,9,1,128]{3,2,1,0:T(1,128)} %bitcast.29), calls=%async_computation.1 | async-start | bytes 1179648 | tf_op jit(solution)/shard_map/all_to_all | solution.py:528
  49.9 5.8 %inverse.3.local_part = f32[4,8,32,128]{3,2,1,0:T(8,128)} custom-call(f32[4,8,32,128]{3,2,1,0:T(8,128)} %get-tuple-element.45.field, bf16[4,1024,1024]{2,1,0:T(8,128)(2,1)} %matrix.9), custom_call_target="tpu_custom_call" | custom-call | flops 536870912 | bytes 9437184 | tf_op jit(solution)/shard_map/inverse/pallas_call | solution.py:624
  57.7 5.4 %all-to-all-start.2 = ((f32[32,16,128]{2,1,0:T(8,128)}), f32[32,16,128]{2,1,0:T(8,128)S(1)}, u32[]{:S(2)}, u32[]{:S(2)}) async-start(f32[32,16,128]{2,1,0:T(8,128)} %reshape.92), calls=%async_computation.2 | async-start | bytes 524288 | tf_op jit(solution)/shard_map/all_to_all | solution.py:528
  65.4 4.3 %totals.1 = f32[512,128]{1,0:T(8,128)} custom-call(f32[1152,128]{1,0:T(8,128)} %bitcast.3.landed, s32[4,1152]{1,0:T(4,128)} %reshape.98.index), custom_call_target="tpu_custom_call" | custom-call | flops 1207959552 | bytes 1048576 | tf_op jit(solution)/shard_map/totals/pallas_call | solution.py:683
  72.8 3.4 %first.1 = (f32[4,8,32,128]{3,2,1,0:T(8,128)}, f32[32,64,128]{2,1,0:T(8,128)}, f32[4,32,128]{2,1,0:T(8,128)}, f32[4,32,128]{2,1,0:T(8,128)}) custom-call(s32[16,128]{1,0:T(8,128)} %pad.8.table, f32[512,128]{1,0:T(8,128)} %bitcast.27, f32[512,128]{1,0:T(8,128)} %totals.1, bf16[128,1024]{1,0:T(8,128)(2,1)} %pad_maximum_fusion.basis, ...), custom_call_target="tpu_custom_call" | custom-call | flops 67108864 | bytes 4194304 | tf_op jit(solution)/shard_map/first/pallas_call | solution.py:696
  76.2 5.2 %all-to-all-start.3 = ((f32[32,64,128]{2,1,0:T(8,128)}), f32[32,64,128]{2,1,0:T(8,128)}, u32[]{:S(2)}, u32[]{:S(2)}) async-start(f32[32,64,128]{2,1,0:T(8,128)} %get-tuple-element.49), calls=%async_computation.3 | async-start | bytes 2097152 | tf_op jit(solution)/shard_map/all_to_all | solution.py:528
  86.2 4.1 %collective-permute-done.3.after = f32[4,32,128]{2,1,0:T(8,128)S(1)} collective-permute-done((f32[4,32,128]{2,1,0:T(8,128)S(1)}, f32[4,32,128]{2,1,0:T(8,128)S(1)}, u32[]{:S(2)}, u32[]{:S(2)}) %collective-permute-start.3) | collective-permute-done | bytes 65568 | tf_op jit(solution)/shard_map/ppermute | solution.py:570
  90.3 8.4 %all-to-all-done.3.incoming = f32[32,64,128]{2,1,0:T(8,128)} async-done(((f32[32,64,128]{2,1,0:T(8,128)}), f32[32,64,128]{2,1,0:T(8,128)}, u32[]{:S(2)}, u32[]{:S(2)}) %all-to-all-start.3) | async-done | bytes 1048608 | tf_op jit(solution)/shard_map/all_to_all | solution.py:528
  98.7 6.5 %schur.2 = (f32[4,8,32,128]{3,2,1,0:T(8,128)}, f32[4,8,32,128]{3,2,1,0:T(8,128)}, f32[32,64,128]{2,1,0:T(8,128)}, f32[4,32,128]{2,1,0:T(8,128)}, f32[4,32,128]{2,1,0:T(8,128)}) custom-call(s32[16,128]{1,0:T(8,128)} %pad.8.table, f32[32,64,128]{2,1,0:T(8,128)} %all-to-all-done.3.incoming, f32[4,32,128]{2,1,0:T(8,128)} %copy-done.14, ...), custom_call_target="tpu_custom_call" | custom-call | flops 536870912 | bytes 11534336 | tf_op jit(solution)/shard_map/schur/pallas_call | solution.py:636
  105.3 4.8 %all-to-all-start.4 = ((f32[32,64,128]{2,1,0:T(8,128)}), f32[32,64,128]{2,1,0:T(8,128)}, u32[]{:S(2)}, u32[]{:S(2)}) async-start(f32[32,64,128]{2,1,0:T(8,128)} %get-tuple-element.53), calls=%async_computation.4 | async-start | bytes 2097152 | tf_op jit(solution)/shard_map/all_to_all | solution.py:528
  116.2 3.4 %collective-permute-done.5.after = f32[4,32,128]{2,1,0:T(8,128)S(1)} collective-permute-done((f32[4,32,128]{2,1,0:T(8,128)S(1)}, f32[4,32,128]{2,1,0:T(8,128)S(1)}, u32[]{:S(2)}, u32[]{:S(2)}) %collective-permute-start.5) | collective-permute-done | bytes 65568 | tf_op jit(solution)/shard_map/ppermute | solution.py:570
  119.6 7.8 %all-to-all-done.4.incoming = f32[32,64,128]{2,1,0:T(8,128)} async-done(((f32[32,64,128]{2,1,0:T(8,128)}), f32[32,64,128]{2,1,0:T(8,128)}, u32[]{:S(2)}, u32[]{:S(2)}) %all-to-all-start.4) | async-done | bytes 1048608 | tf_op jit(solution)/shard_map/all_to_all | solution.py:528
  130.6 6.5 %all-to-all-start.5 = ((f32[128,9,1,128]{3,2,1,0:T(1,128)}), f32[128,9,1,128]{3,2,1,0:T(1,128)}, u32[]{:S(2)}, u32[]{:S(2)}) async-start(f32[128,9,1,128]{3,2,1,0:T(1,128)} %bitcast.30), calls=%async_computation.5 | async-start | bytes 1179648 | tf_op jit(solution)/shard_map/all_to_all | solution.py:528
  137.1 5.3 %responses.1 = bf16[256,1152]{1,0:T(8,128)(2,1)} custom-call(f32[512,128]{1,0:T(8,128)} %bitcast.28, s32[4,1152]{1,0:T(4,128)} %reshape.98.index), custom_call_target="tpu_custom_call" | custom-call | flops 1207959552 | bytes 524288 | tf_op jit(solution)/shard_map/responses/pallas_call | solution.py:710
  142.4 5.8 %inverse.4.local_part = f32[4,8,32,128]{3,2,1,0:T(8,128)} custom-call(f32[4,8,32,128]{3,2,1,0:T(8,128)} %get-tuple-element.59.field, bf16[4,1024,1024]{2,1,0:T(8,128)(2,1)} %matrix.9), custom_call_target="tpu_custom_call" | custom-call | flops 536870912 | bytes 9437184 | tf_op jit(solution)/shard_map/inverse/pallas_call | solution.py:624
  151.2 4.0 %second.1 = (f32[4,8,32,128]{3,2,1,0:T(8,128)}, f32[4,8,32,128]{3,2,1,0:T(8,128)}, f32[3,32,128]{2,1,0:T(8,128)}, f32[32,64,128]{2,1,0:T(8,128)}, f32[4,32,128]{2,1,0:T(8,128)}, /*index=5*/f32[4,32,128]{2,1,0:T(8,128)}) custom-call(s32[16,128]{1,0:T(8,128)} %pad.8.table, f32[1152,128]{1,0:T(8,128)} %bitcast.8.landed, bf16[256,1152]{1,0:T(8,128)(2,1)} %responses.1, ...), custom_call_target="tpu_custom_call" | custom-call | flops 67108864 | bytes 4194304 | tf_op jit(solution)/shard_map/second/pallas_call | solution.py:727
  155.3 5.2 %all-to-all-start.6 = ((f32[32,64,128]{2,1,0:T(8,128)}), f32[32,64,128]{2,1,0:T(8,128)}, u32[]{:S(2)}, u32[]{:S(2)}) async-start(f32[32,64,128]{2,1,0:T(8,128)} %get-tuple-element.60), calls=%async_computation.6 | async-start | bytes 2097152 | tf_op jit(solution)/shard_map/all_to_all | solution.py:528
  164.6 4.1 %collective-permute-done.7.after = f32[4,32,128]{2,1,0:T(8,128)S(1)} collective-permute-done((f32[4,32,128]{2,1,0:T(8,128)S(1)}, f32[4,32,128]{2,1,0:T(8,128)S(1)}, u32[]{:S(2)}, u32[]{:S(2)}) %collective-permute-start.7) | collective-permute-done | bytes 65568 | tf_op jit(solution)/shard_map/ppermute | solution.py:570
  168.7 9.1 %all-to-all-done.6.incoming = f32[32,64,128]{2,1,0:T(8,128)} async-done(((f32[32,64,128]{2,1,0:T(8,128)}), f32[32,64,128]{2,1,0:T(8,128)}, u32[]{:S(2)}, u32[]{:S(2)}) %all-to-all-start.6) | async-done | bytes 1048608 | tf_op jit(solution)/shard_map/all_to_all | solution.py:528
  177.9 6.6 %schur.3 = (f32[4,8,32,128]{3,2,1,0:T(8,128)}, f32[4,8,32,128]{3,2,1,0:T(8,128)}, f32[32,64,128]{2,1,0:T(8,128)}, f32[4,32,128]{2,1,0:T(8,128)}, f32[4,32,128]{2,1,0:T(8,128)}) custom-call(s32[16,128]{1,0:T(8,128)} %pad.8.table, f32[32,64,128]{2,1,0:T(8,128)} %all-to-all-done.6.incoming, f32[4,32,128]{2,1,0:T(8,128)} %copy-done.15, ...), custom_call_target="tpu_custom_call" | custom-call | flops 536870912 | bytes 11534336 | tf_op jit(solution)/shard_map/schur/pallas_call | solution.py:636
  184.5 4.8 %all-to-all-start.7 = ((f32[32,64,128]{2,1,0:T(8,128)}), f32[32,64,128]{2,1,0:T(8,128)}, u32[]{:S(2)}, u32[]{:S(2)}) async-start(f32[32,64,128]{2,1,0:T(8,128)} %get-tuple-element.64), calls=%async_computation.7 | async-start | bytes 2097152 | tf_op jit(solution)/shard_map/all_to_all | solution.py:528
  199.9 6.8 %all-to-all-done.7.incoming = f32[32,64,128]{2,1,0:T(8,128)} async-done(((f32[32,64,128]{2,1,0:T(8,128)}), f32[32,64,128]{2,1,0:T(8,128)}, u32[]{:S(2)}, u32[]{:S(2)}) %all-to-all-start.7) | async-done | bytes 1048608 | tf_op jit(solution)/shard_map/all_to_all | solution.py:528
  209.8 5.8 %all-to-all-start.8 = ((f32[128,9,1,128]{3,2,1,0:T(1,128)}), f32[128,9,1,128]{3,2,1,0:T(1,128)}, u32[]{:S(2)}, u32[]{:S(2)}) async-start(f32[128,9,1,128]{3,2,1,0:T(1,128)} %bitcast.31), calls=%async_computation.8 | async-start | bytes 1179648 | tf_op jit(solution)/shard_map/all_to_all | solution.py:528
  215.6 5.8 %inverse.5.local_part = f32[4,8,32,128]{3,2,1,0:T(8,128)} custom-call(f32[4,8,32,128]{3,2,1,0:T(8,128)} %get-tuple-element.71.field, bf16[4,1024,1024]{2,1,0:T(8,128)(2,1)} %matrix.9), custom_call_target="tpu_custom_call" | custom-call | flops 536870912 | bytes 9437184 | tf_op jit(solution)/shard_map/inverse/pallas_call | solution.py:624
  221.5 8.3 %all-to-all-done.8 = f32[128,9,1,128]{3,2,1,0:T(1,128)} async-done(((f32[128,9,1,128]{3,2,1,0:T(1,128)}), f32[128,9,1,128]{3,2,1,0:T(1,128)}, u32[]{:S(2)}, u32[]{:S(2)}) %all-to-all-start.8) | async-done | bytes 589856 | tf_op jit(solution)/shard_map/all_to_all | solution.py:528
  229.7 3.8 %third.1 = (f32[4,8,32,128]{3,2,1,0:T(8,128)}, f32[2,32,128]{2,1,0:T(8,128)}, f32[32,64,128]{2,1,0:T(8,128)}, f32[4,32,128]{2,1,0:T(8,128)}, f32[4,32,128]{2,1,0:T(8,128)}) custom-call(s32[16,128]{1,0:T(8,128)} %pad.8.table, f32[1152,128]{1,0:T(8,128)} %bitcast.11.landed, bf16[256,1152]{1,0:T(8,128)(2,1)} %responses.1, ...), custom_call_target="tpu_custom_call" | custom-call | flops 67108864 | bytes 4194304 | tf_op jit(solution)/shard_map/third/pallas_call | solution.py:750
  233.6 5.3 %all-to-all-start.9 = ((f32[32,64,128]{2,1,0:T(8,128)}), f32[32,64,128]{2,1,0:T(8,128)}, u32[]{:S(2)}, u32[]{:S(2)}) async-start(f32[32,64,128]{2,1,0:T(8,128)} %get-tuple-element.74), calls=%async_computation.9 | async-start | bytes 2097152 | tf_op jit(solution)/shard_map/all_to_all | solution.py:528
  246.4 9.8 %all-to-all-done.9.incoming = f32[32,64,128]{2,1,0:T(8,128)} async-done(((f32[32,64,128]{2,1,0:T(8,128)}), f32[32,64,128]{2,1,0:T(8,128)}, u32[]{:S(2)}, u32[]{:S(2)}) %all-to-all-start.9) | async-done | bytes 1048608 | tf_op jit(solution)/shard_map/all_to_all | solution.py:528
  (135 shorter events, 68.7 us)
Async XLA Ops:
  0.6 44.0 %copy-start = (f32[64,2048]{1,0:T(8,128)S(1)}, f32[64,2048]{1,0:T(8,128)}, u32[]{:S(2)}) copy-start(f32[64,2048]{1,0:T(8,128)} %param.12) | copy-start | bytes 1572868
  0.6 19.0 %copy-start.13 = (f32[4,8,8,128]{3,2,1,0:T(8,128)S(1)}, f32[4,8,8,128]{3,2,1,0:T(8,128)}, u32[]{:S(2)}) copy-start(f32[4,8,8,128]{3,2,1,0:T(8,128)} %param.11) | copy-start | bytes 393220
  6.0 12.4 %copy-start.31 = (f32[4,32,128]{2,1,0:T(8,128)S(1)}, f32[4,32,128]{2,1,0:T(8,128)}, u32[]{:S(2)}) copy-start(f32[4,32,128]{2,1,0:T(8,128)} %get-tuple-element.42) | copy-start | bytes 196612
  6.0 26.5 %all-to-all-start = ((f32[32,72,128]{2,1,0:T(8,128)}), f32[32,72,128]{2,1,0:T(8,128)}, u32[]{:S(2)}, u32[]{:S(2)}) async-start(f32[32,72,128]{2,1,0:T(8,128)} %get-tuple-element.40), calls=%async_computation | async-start | bytes 2359296 | tf_op jit(solution)/shard_map/all_to_all | solution.py:528
  14.8 5.7 %collective-permute-start = (f32[4,32,128]{2,1,0:T(8,128)S(1)}, f32[4,32,128]{2,1,0:T(8,128)S(1)}, u32[]{:S(2)}, u32[]{:S(2)}) collective-permute-start(f32[4,32,128]{2,1,0:T(8,128)S(1)} %copy-done.34), channel_id=1, source_target_pairs={{0,32},{32,64},{64,96},{1,33},{33,65},{65,97},{2,34},{34,66},{66,9... | collective-permute-start | bytes 196616 | tf_op jit(solution)/shard_map/ppermute | solution.py:569
  18.3 5.6 %collective-permute-start.1 = (f32[4,32,128]{2,1,0:T(8,128)S(1)}, f32[4,32,128]{2,1,0:T(8,128)S(1)}, u32[]{:S(2)}, u32[]{:S(2)}) collective-permute-start(f32[4,32,128]{2,1,0:T(8,128)S(1)} %copy-done.31), channel_id=1, source_target_pairs={{32,0},{64,32},{96,64},{33,1},{65,33},{97,65},{34,2},{66,34},{98,6... | collective-permute-start | bytes 196616 | tf_op jit(solution)/shard_map/ppermute | solution.py:570
  20.4 12.1 %copy-start.21 = (f32[4,32,128]{2,1,0:T(8,128)}, f32[4,32,128]{2,1,0:T(8,128)S(1)}, u32[]{:S(2)}) copy-start(f32[4,32,128]{2,1,0:T(8,128)S(1)} %collective-permute-done.before) | copy-start | bytes 196612
  35.7 22.1 %all-to-all-start.1 = ((f32[128,9,1,128]{3,2,1,0:T(1,128)}), f32[128,9,1,128]{3,2,1,0:T(1,128)}, u32[]{:S(2)}, u32[]{:S(2)}) async-start(f32[128,9,1,128]{3,2,1,0:T(1,128)} %bitcast.29), calls=%async_computation.1 | async-start | bytes 1179648 | tf_op jit(solution)/shard_map/all_to_all | solution.py:528
  57.7 14.3 %all-to-all-start.2 = ((f32[32,16,128]{2,1,0:T(8,128)}), f32[32,16,128]{2,1,0:T(8,128)S(1)}, u32[]{:S(2)}, u32[]{:S(2)}) async-start(f32[32,16,128]{2,1,0:T(8,128)} %reshape.92), calls=%async_computation.2 | async-start | bytes 524288 | tf_op jit(solution)/shard_map/all_to_all | solution.py:528
  76.2 22.5 %all-to-all-start.3 = ((f32[32,64,128]{2,1,0:T(8,128)}), f32[32,64,128]{2,1,0:T(8,128)}, u32[]{:S(2)}, u32[]{:S(2)}) async-start(f32[32,64,128]{2,1,0:T(8,128)} %get-tuple-element.49), calls=%async_computation.3 | async-start | bytes 2097152 | tf_op jit(solution)/shard_map/all_to_all | solution.py:528
  81.5 4.7 %collective-permute-start.2 = (f32[4,32,128]{2,1,0:T(8,128)S(1)}, f32[4,32,128]{2,1,0:T(8,128)S(1)}, u32[]{:S(2)}, u32[]{:S(2)}) collective-permute-start(f32[4,32,128]{2,1,0:T(8,128)S(1)} %copy-done.38), channel_id=1, source_target_pairs={{0,32},{32,64},{64,96},{1,33},{33,65},{65,97},{2,34},{34,66},{66,9... | collective-permute-start | bytes 196616 | tf_op jit(solution)/shard_map/ppermute | solution.py:569
  84.9 5.4 %collective-permute-start.3 = (f32[4,32,128]{2,1,0:T(8,128)S(1)}, f32[4,32,128]{2,1,0:T(8,128)S(1)}, u32[]{:S(2)}, u32[]{:S(2)}) collective-permute-start(f32[4,32,128]{2,1,0:T(8,128)S(1)} %copy-done.36), channel_id=1, source_target_pairs={{32,0},{64,32},{96,64},{33,1},{65,33},{97,65},{34,2},{66,34},{98,6... | collective-permute-start | bytes 196616 | tf_op jit(solution)/shard_map/ppermute | solution.py:570
  86.2 12.5 %copy-start.14 = (f32[4,32,128]{2,1,0:T(8,128)}, f32[4,32,128]{2,1,0:T(8,128)S(1)}, u32[]{:S(2)}) copy-start(f32[4,32,128]{2,1,0:T(8,128)S(1)} %collective-permute-done.2.before) | copy-start | bytes 196612
  105.3 22.1 %all-to-all-start.4 = ((f32[32,64,128]{2,1,0:T(8,128)}), f32[32,64,128]{2,1,0:T(8,128)}, u32[]{:S(2)}, u32[]{:S(2)}) async-start(f32[32,64,128]{2,1,0:T(8,128)} %get-tuple-element.53), calls=%async_computation.4 | async-start | bytes 2097152 | tf_op jit(solution)/shard_map/all_to_all | solution.py:528
  110.8 5.4 %collective-permute-start.4 = (f32[4,32,128]{2,1,0:T(8,128)S(1)}, f32[4,32,128]{2,1,0:T(8,128)S(1)}, u32[]{:S(2)}, u32[]{:S(2)}) collective-permute-start(f32[4,32,128]{2,1,0:T(8,128)S(1)} %copy-done.35), channel_id=1, source_target_pairs={{0,32},{32,64},{64,96},{1,33},{33,65},{65,97},{2,34},{34,66},{66,9... | collective-permute-start | bytes 196616 | tf_op jit(solution)/shard_map/ppermute | solution.py:569
  114.2 5.4 %collective-permute-start.5 = (f32[4,32,128]{2,1,0:T(8,128)S(1)}, f32[4,32,128]{2,1,0:T(8,128)S(1)}, u32[]{:S(2)}, u32[]{:S(2)}) collective-permute-start(f32[4,32,128]{2,1,0:T(8,128)S(1)} %copy-done.32), channel_id=1, source_target_pairs={{32,0},{64,32},{96,64},{33,1},{65,33},{97,65},{34,2},{66,34},{98,6... | collective-permute-start | bytes 196616 | tf_op jit(solution)/shard_map/ppermute | solution.py:570
  130.6 20.6 %all-to-all-start.5 = ((f32[128,9,1,128]{3,2,1,0:T(1,128)}), f32[128,9,1,128]{3,2,1,0:T(1,128)}, u32[]{:S(2)}, u32[]{:S(2)}) async-start(f32[128,9,1,128]{3,2,1,0:T(1,128)} %bitcast.30), calls=%async_computation.5 | async-start | bytes 1179648 | tf_op jit(solution)/shard_map/all_to_all | solution.py:528
  155.3 22.5 %all-to-all-start.6 = ((f32[32,64,128]{2,1,0:T(8,128)}), f32[32,64,128]{2,1,0:T(8,128)}, u32[]{:S(2)}, u32[]{:S(2)}) async-start(f32[32,64,128]{2,1,0:T(8,128)} %get-tuple-element.60), calls=%async_computation.6 | async-start | bytes 2097152 | tf_op jit(solution)/shard_map/all_to_all | solution.py:528
  160.5 4.1 %collective-permute-start.6 = (f32[4,32,128]{2,1,0:T(8,128)S(1)}, f32[4,32,128]{2,1,0:T(8,128)S(1)}, u32[]{:S(2)}, u32[]{:S(2)}) collective-permute-start(f32[4,32,128]{2,1,0:T(8,128)S(1)} %copy-done.37), channel_id=1, source_target_pairs={{0,32},{32,64},{64,96},{1,33},{33,65},{65,97},{2,34},{34,66},{66,9... | collective-permute-start | bytes 196616 | tf_op jit(solution)/shard_map/ppermute | solution.py:569
  163.3 5.4 %collective-permute-start.7 = (f32[4,32,128]{2,1,0:T(8,128)S(1)}, f32[4,32,128]{2,1,0:T(8,128)S(1)}, u32[]{:S(2)}, u32[]{:S(2)}) collective-permute-start(f32[4,32,128]{2,1,0:T(8,128)S(1)} %copy-done.33), channel_id=1, source_target_pairs={{32,0},{64,32},{96,64},{33,1},{65,33},{97,65},{34,2},{66,34},{98,6... | collective-permute-start | bytes 196616 | tf_op jit(solution)/shard_map/ppermute | solution.py:570
  164.6 13.2 %copy-start.15 = (f32[4,32,128]{2,1,0:T(8,128)}, f32[4,32,128]{2,1,0:T(8,128)S(1)}, u32[]{:S(2)}) copy-start(f32[4,32,128]{2,1,0:T(8,128)S(1)} %collective-permute-done.6.before) | copy-start | bytes 196612
  184.5 11.3 %copy-start.6 = (f32[4,8,32,128]{3,2,1,0:T(8,128)S(1)}, f32[4,8,32,128]{3,2,1,0:T(8,128)}, u32[]{:S(2)}) copy-start(f32[4,8,32,128]{3,2,1,0:T(8,128)} %get-tuple-element.57) | copy-start | bytes 1572868
  184.5 11.3 %copy-start.9 = (f32[4,8,32,128]{3,2,1,0:T(8,128)S(1)}, f32[4,8,32,128]{3,2,1,0:T(8,128)}, u32[]{:S(2)}) copy-start(f32[4,8,32,128]{3,2,1,0:T(8,128)} %get-tuple-element.56.base) | copy-start | bytes 1572868
  184.5 11.3 %copy-start.10 = (f32[4,8,32,128]{3,2,1,0:T(8,128)S(1)}, f32[4,8,32,128]{3,2,1,0:T(8,128)}, u32[]{:S(2)}) copy-start(f32[4,8,32,128]{3,2,1,0:T(8,128)} %get-tuple-element.69) | copy-start | bytes 1572868
  184.5 22.1 %all-to-all-start.7 = ((f32[32,64,128]{2,1,0:T(8,128)}), f32[32,64,128]{2,1,0:T(8,128)}, u32[]{:S(2)}, u32[]{:S(2)}) async-start(f32[32,64,128]{2,1,0:T(8,128)} %get-tuple-element.64), calls=%async_computation.7 | async-start | bytes 2097152 | tf_op jit(solution)/shard_map/all_to_all | solution.py:528
  191.8 6.5 %collective-permute-start.8 = (f32[4,32,128]{2,1,0:T(8,128)S(1)}, f32[4,32,128]{2,1,0:T(8,128)S(1)}, u32[]{:S(2)}, u32[]{:S(2)}) collective-permute-start(f32[4,32,128]{2,1,0:T(8,128)S(1)} %copy-done.29), channel_id=1, source_target_pairs={{0,32},{32,64},{64,96},{1,33},{33,65},{65,97},{2,34},{34,66},{66,9... | collective-permute-start | bytes 196616 | tf_op jit(solution)/shard_map/ppermute | solution.py:569
  194.5 5.4 %collective-permute-start.9 = (f32[4,32,128]{2,1,0:T(8,128)S(1)}, f32[4,32,128]{2,1,0:T(8,128)S(1)}, u32[]{:S(2)}, u32[]{:S(2)}) collective-permute-start(f32[4,32,128]{2,1,0:T(8,128)S(1)} %copy-done.27), channel_id=1, source_target_pairs={{32,0},{64,32},{96,64},{33,1},{65,33},{97,65},{34,2},{66,34},{98,6... | collective-permute-start | bytes 196616 | tf_op jit(solution)/shard_map/ppermute | solution.py:570
  209.8 19.9 %all-to-all-start.8 = ((f32[128,9,1,128]{3,2,1,0:T(1,128)}), f32[128,9,1,128]{3,2,1,0:T(1,128)}, u32[]{:S(2)}, u32[]{:S(2)}) async-start(f32[128,9,1,128]{3,2,1,0:T(1,128)} %bitcast.31), calls=%async_computation.8 | async-start | bytes 1179648 | tf_op jit(solution)/shard_map/all_to_all | solution.py:528
  233.6 22.6 %all-to-all-start.9 = ((f32[32,64,128]{2,1,0:T(8,128)}), f32[32,64,128]{2,1,0:T(8,128)}, u32[]{:S(2)}, u32[]{:S(2)}) async-start(f32[32,64,128]{2,1,0:T(8,128)} %get-tuple-element.74), calls=%async_computation.9 | async-start | bytes 2097152 | tf_op jit(solution)/shard_map/all_to_all | solution.py:528
  238.9 4.4 %collective-permute-start.10 = (f32[4,32,128]{2,1,0:T(8,128)S(1)}, f32[4,32,128]{2,1,0:T(8,128)S(1)}, u32[]{:S(2)}, u32[]{:S(2)}) collective-permute-start(f32[4,32,128]{2,1,0:T(8,128)S(1)} %copy-done.30), channel_id=1, source_target_pairs={{0,32},{32,64},{64,96},{1,33},{33,65},{65,97},{2,34},{34,66},{66,9... | collective-permute-start | bytes 196616 | tf_op jit(solution)/shard_map/ppermute | solution.py:569
  241.0 5.4 %collective-permute-start.11 = (f32[4,32,128]{2,1,0:T(8,128)S(1)}, f32[4,32,128]{2,1,0:T(8,128)S(1)}, u32[]{:S(2)}, u32[]{:S(2)}) collective-permute-start(f32[4,32,128]{2,1,0:T(8,128)S(1)} %copy-done.28), channel_id=1, source_target_pairs={{32,0},{64,32},{96,64},{33,1},{65,33},{97,65},{34,2},{66,34},{98,6... | collective-permute-start | bytes 196616 | tf_op jit(solution)/shard_map/ppermute | solution.py:570
  243.2 13.0 %copy-start.19 = (f32[4,32,128]{2,1,0:T(8,128)}, f32[4,32,128]{2,1,0:T(8,128)S(1)}, u32[]{:S(2)}) copy-start(f32[4,32,128]{2,1,0:T(8,128)S(1)} %collective-permute-done.10.before) | copy-start | bytes 196612
  (29 other events, 218.8 us)

commit v4 on v3

--- a/solution.py
+++ b/solution.py
@@ -428,7 +428,10 @@
     subs, blocks, cases, width = corrected.shape
     arriving = fetches(table, table_s, incoming, incoming_v, before, after, rims_v, arrive_sems)
     base_in = start_all(copies_of(parts_of(corrected), parts_of(corrected_v), more, 0))
-    matrix_in = [start_all(group) for group in pieces(matrix, held, held_sems)]
+    matrix_in = pieces(matrix, held, held_sems)
+    for s, group in enumerate(matrix_in):
+        for copy in group:
+            copy.start(priority=s % 2)
     wait_all(arriving)
     out = []
     for s in range(subs):

time: 261 us -> 260 us (level)
  no operation moved by 1% of the time
where the time goes in v4:
time: 260 us; the launch traced here: 258 us
  waiting for transfers between devices  86 us (33%)
  starting transfers between devices  85.2 us (33%)
  Pallas kernels  65.5 us (25%)
  other arithmetic  10.1 us (4%)
  local copies, waits for them, and re-layouts  6.67 us (3%)
  matrix products  3.11 us (1%)
    all_to_all x10, waiting for transfers between devices, all_to_all(): return lax.all_to_all(block, axes, split_axis=0, concat_axis=0, tiled=True)  66.1 us
    all_to_all x10, starting transfers between devices, all_to_all(): return lax.all_to_all(block, axes, split_axis=0, concat_axis=0, tiled=True)  59.7 us
    ppermute x6, waiting for transfers between devices, exchange(): after = lax.ppermute(downward, 'grp', down)  19.9 us
    ppermute x6, starting transfers between devices, exchange(): before = lax.ppermute(upward, 'grp', up)  17.7 us
    pallas_call x3, Pallas kernels, inverse(): pl.pallas_call(functools.partial(inverse_kernel, fine), out_shape=shape(f...  17.5 us
    pallas_call x2, Pallas kernels, apply_schur(): pl.pallas_call(functools.partial(schur_kernel, fine), out_shape=(shape(fi...  12.5 us
    pallas_call x3, Pallas kernels, project(): pl.pallas_call(functools.partial(project_kernel, len(dots)), out_shape=(s...  9.48 us
    ppermute x6, starting transfers between devices, exchange(): after = lax.ppermute(downward, 'grp', down)  7.75 us
  transfers between devices with their start and end apart: 22, of which 16 were waited for; matrix products, arithmetic and copies ran while one was open for 6% of the time, Pallas kernels for 10%

profile of v4, /device:TPU:1, one launch (start us, length us, event | category | flops | bytes accessed | tf_op | source)
XLA Modules:
  0.0 258.2 jit_solution(1216863848378090395)
XLA Ops:
  6.0 8.8 %all-to-all-start = ((f32[32,72,128]{2,1,0:T(8,128)}), f32[32,72,128]{2,1,0:T(8,128)}, u32[]{:S(2)}, u32[]{:S(2)}) async-start(f32[32,72,128]{2,1,0:T(8,128)} %get-tuple-element.40), calls=%async_computation | async-start | bytes 2359296 | tf_op jit(solution)/shard_map/all_to_all | solution.py:531
  14.8 3.5 %collective-permute-start = (f32[4,32,128]{2,1,0:T(8,128)S(1)}, f32[4,32,128]{2,1,0:T(8,128)S(1)}, u32[]{:S(2)}, u32[]{:S(2)}) collective-permute-start(f32[4,32,128]{2,1,0:T(8,128)S(1)} %copy-done.34), channel_id=1, source_target_pairs={{0,32},{32,64},{64,96},{1,33},{33,65},{65,97},{2,34},{34,66},{66,9... | collective-permute-start | bytes 196616 | tf_op jit(solution)/shard_map/ppermute | solution.py:572
  20.4 3.5 %collective-permute-done.1.after = f32[4,32,128]{2,1,0:T(8,128)S(1)} collective-permute-done((f32[4,32,128]{2,1,0:T(8,128)S(1)}, f32[4,32,128]{2,1,0:T(8,128)S(1)}, u32[]{:S(2)}, u32[]{:S(2)}) %collective-permute-start.1) | collective-permute-done | bytes 65568 | tf_op jit(solution)/shard_map/ppermute | solution.py:573
  23.9 8.6 %all-to-all-done.incoming = f32[32,72,128]{2,1,0:T(8,128)} async-done(((f32[32,72,128]{2,1,0:T(8,128)}), f32[32,72,128]{2,1,0:T(8,128)}, u32[]{:S(2)}, u32[]{:S(2)}) %all-to-all-start) | async-done | bytes 1179680 | tf_op jit(solution)/shard_map/all_to_all | solution.py:531
  35.7 7.9 %all-to-all-start.1 = ((f32[128,9,1,128]{3,2,1,0:T(1,128)}), f32[128,9,1,128]{3,2,1,0:T(1,128)}, u32[]{:S(2)}, u32[]{:S(2)}) async-start(f32[128,9,1,128]{3,2,1,0:T(1,128)} %bitcast.29), calls=%async_computation.1 | async-start | bytes 1179648 | tf_op jit(solution)/shard_map/all_to_all | solution.py:531
  49.9 5.8 %inverse.3.local_part = f32[4,8,32,128]{3,2,1,0:T(8,128)} custom-call(f32[4,8,32,128]{3,2,1,0:T(8,128)} %get-tuple-element.45.field, bf16[4,1024,1024]{2,1,0:T(8,128)(2,1)} %matrix.9), custom_call_target="tpu_custom_call" | custom-call | flops 536870912 | bytes 9437184 | tf_op jit(solution)/shard_map/inverse/pallas_call | solution.py:627
  57.7 5.4 %all-to-all-start.2 = ((f32[32,16,128]{2,1,0:T(8,128)}), f32[32,16,128]{2,1,0:T(8,128)S(1)}, u32[]{:S(2)}, u32[]{:S(2)}) async-start(f32[32,16,128]{2,1,0:T(8,128)} %reshape.92), calls=%async_computation.2 | async-start | bytes 524288 | tf_op jit(solution)/shard_map/all_to_all | solution.py:531
  65.4 4.3 %totals.1 = f32[512,128]{1,0:T(8,128)} custom-call(f32[1152,128]{1,0:T(8,128)} %bitcast.3.landed, s32[4,1152]{1,0:T(4,128)} %reshape.98.index), custom_call_target="tpu_custom_call" | custom-call | flops 1207959552 | bytes 1048576 | tf_op jit(solution)/shard_map/totals/pallas_call | solution.py:686
  72.8 3.4 %first.1 = (f32[4,8,32,128]{3,2,1,0:T(8,128)}, f32[32,64,128]{2,1,0:T(8,128)}, f32[4,32,128]{2,1,0:T(8,128)}, f32[4,32,128]{2,1,0:T(8,128)}) custom-call(s32[16,128]{1,0:T(8,128)} %pad.8.table, f32[512,128]{1,0:T(8,128)} %bitcast.27, f32[512,128]{1,0:T(8,128)} %totals.1, bf16[128,1024]{1,0:T(8,128)(2,1)} %pad_maximum_fusion.basis, ...), custom_call_target="tpu_custom_call" | custom-call | flops 67108864 | bytes 4194304 | tf_op jit(solution)/shard_map/first/pallas_call | solution.py:699
  76.2 5.3 %all-to-all-start.3 = ((f32[32,64,128]{2,1,0:T(8,128)}), f32[32,64,128]{2,1,0:T(8,128)}, u32[]{:S(2)}, u32[]{:S(2)}) async-start(f32[32,64,128]{2,1,0:T(8,128)} %get-tuple-element.49), calls=%async_computation.3 | async-start | bytes 2097152 | tf_op jit(solution)/shard_map/all_to_all | solution.py:531
  86.2 4.1 %collective-permute-done.3.after = f32[4,32,128]{2,1,0:T(8,128)S(1)} collective-permute-done((f32[4,32,128]{2,1,0:T(8,128)S(1)}, f32[4,32,128]{2,1,0:T(8,128)S(1)}, u32[]{:S(2)}, u32[]{:S(2)}) %collective-permute-start.3) | collective-permute-done | bytes 65568 | tf_op jit(solution)/shard_map/ppermute | solution.py:573
  90.3 8.4 %all-to-all-done.3.incoming = f32[32,64,128]{2,1,0:T(8,128)} async-done(((f32[32,64,128]{2,1,0:T(8,128)}), f32[32,64,128]{2,1,0:T(8,128)}, u32[]{:S(2)}, u32[]{:S(2)}) %all-to-all-start.3) | async-done | bytes 1048608 | tf_op jit(solution)/shard_map/all_to_all | solution.py:531
  98.7 6.2 %schur.2 = (f32[4,8,32,128]{3,2,1,0:T(8,128)}, f32[4,8,32,128]{3,2,1,0:T(8,128)}, f32[32,64,128]{2,1,0:T(8,128)}, f32[4,32,128]{2,1,0:T(8,128)}, f32[4,32,128]{2,1,0:T(8,128)}) custom-call(s32[16,128]{1,0:T(8,128)} %pad.8.table, f32[32,64,128]{2,1,0:T(8,128)} %all-to-all-done.3.incoming, f32[4,32,128]{2,1,0:T(8,128)} %copy-done.14, ...), custom_call_target="tpu_custom_call" | custom-call | flops 536870912 | bytes 11534336 | tf_op jit(solution)/shard_map/schur/pallas_call | solution.py:639
  105.0 4.8 %all-to-all-start.4 = ((f32[32,64,128]{2,1,0:T(8,128)}), f32[32,64,128]{2,1,0:T(8,128)}, u32[]{:S(2)}, u32[]{:S(2)}) async-start(f32[32,64,128]{2,1,0:T(8,128)} %get-tuple-element.53), calls=%async_computation.4 | async-start | bytes 2097152 | tf_op jit(solution)/shard_map/all_to_all | solution.py:531
  115.9 3.4 %collective-permute-done.5.after = f32[4,32,128]{2,1,0:T(8,128)S(1)} collective-permute-done((f32[4,32,128]{2,1,0:T(8,128)S(1)}, f32[4,32,128]{2,1,0:T(8,128)S(1)}, u32[]{:S(2)}, u32[]{:S(2)}) %collective-permute-start.5) | collective-permute-done | bytes 65568 | tf_op jit(solution)/shard_map/ppermute | solution.py:573
  119.3 7.8 %all-to-all-done.4.incoming = f32[32,64,128]{2,1,0:T(8,128)} async-done(((f32[32,64,128]{2,1,0:T(8,128)}), f32[32,64,128]{2,1,0:T(8,128)}, u32[]{:S(2)}, u32[]{:S(2)}) %all-to-all-start.4) | async-done | bytes 1048608 | tf_op jit(solution)/shard_map/all_to_all | solution.py:531
  130.3 6.5 %all-to-all-start.5 = ((f32[128,9,1,128]{3,2,1,0:T(1,128)}), f32[128,9,1,128]{3,2,1,0:T(1,128)}, u32[]{:S(2)}, u32[]{:S(2)}) async-start(f32[128,9,1,128]{3,2,1,0:T(1,128)} %bitcast.30), calls=%async_computation.5 | async-start | bytes 1179648 | tf_op jit(solution)/shard_map/all_to_all | solution.py:531
  136.8 5.3 %responses.1 = bf16[256,1152]{1,0:T(8,128)(2,1)} custom-call(f32[512,128]{1,0:T(8,128)} %bitcast.28, s32[4,1152]{1,0:T(4,128)} %reshape.98.index), custom_call_target="tpu_custom_call" | custom-call | flops 1207959552 | bytes 524288 | tf_op jit(solution)/shard_map/responses/pallas_call | solution.py:713
  142.1 5.8 %inverse.4.local_part = f32[4,8,32,128]{3,2,1,0:T(8,128)} custom-call(f32[4,8,32,128]{3,2,1,0:T(8,128)} %get-tuple-element.59.field, bf16[4,1024,1024]{2,1,0:T(8,128)(2,1)} %matrix.9), custom_call_target="tpu_custom_call" | custom-call | flops 536870912 | bytes 9437184 | tf_op jit(solution)/shard_map/inverse/pallas_call | solution.py:627
  150.9 4.0 %second.1 = (f32[4,8,32,128]{3,2,1,0:T(8,128)}, f32[4,8,32,128]{3,2,1,0:T(8,128)}, f32[3,32,128]{2,1,0:T(8,128)}, f32[32,64,128]{2,1,0:T(8,128)}, f32[4,32,128]{2,1,0:T(8,128)}, /*index=5*/f32[4,32,128]{2,1,0:T(8,128)}) custom-call(s32[16,128]{1,0:T(8,128)} %pad.8.table, f32[1152,128]{1,0:T(8,128)} %bitcast.8.landed, bf16[256,1152]{1,0:T(8,128)(2,1)} %responses.1, ...), custom_call_target="tpu_custom_call" | custom-call | flops 67108864 | bytes 4194304 | tf_op jit(solution)/shard_map/second/pallas_call | solution.py:730
  154.9 5.3 %all-to-all-start.6 = ((f32[32,64,128]{2,1,0:T(8,128)}), f32[32,64,128]{2,1,0:T(8,128)}, u32[]{:S(2)}, u32[]{:S(2)}) async-start(f32[32,64,128]{2,1,0:T(8,128)} %get-tuple-element.60), calls=%async_computation.6 | async-start | bytes 2097152 | tf_op jit(solution)/shard_map/all_to_all | solution.py:531
  164.3 4.1 %collective-permute-done.7.after = f32[4,32,128]{2,1,0:T(8,128)S(1)} collective-permute-done((f32[4,32,128]{2,1,0:T(8,128)S(1)}, f32[4,32,128]{2,1,0:T(8,128)S(1)}, u32[]{:S(2)}, u32[]{:S(2)}) %collective-permute-start.7) | collective-permute-done | bytes 65568 | tf_op jit(solution)/shard_map/ppermute | solution.py:573
  168.4 9.1 %all-to-all-done.6.incoming = f32[32,64,128]{2,1,0:T(8,128)} async-done(((f32[32,64,128]{2,1,0:T(8,128)}), f32[32,64,128]{2,1,0:T(8,128)}, u32[]{:S(2)}, u32[]{:S(2)}) %all-to-all-start.6) | async-done | bytes 1048608 | tf_op jit(solution)/shard_map/all_to_all | solution.py:531
  177.5 6.3 %schur.3 = (f32[4,8,32,128]{3,2,1,0:T(8,128)}, f32[4,8,32,128]{3,2,1,0:T(8,128)}, f32[32,64,128]{2,1,0:T(8,128)}, f32[4,32,128]{2,1,0:T(8,128)}, f32[4,32,128]{2,1,0:T(8,128)}) custom-call(s32[16,128]{1,0:T(8,128)} %pad.8.table, f32[32,64,128]{2,1,0:T(8,128)} %all-to-all-done.6.incoming, f32[4,32,128]{2,1,0:T(8,128)} %copy-done.15, ...), custom_call_target="tpu_custom_call" | custom-call | flops 536870912 | bytes 11534336 | tf_op jit(solution)/shard_map/schur/pallas_call | solution.py:639
  183.9 4.8 %all-to-all-start.7 = ((f32[32,64,128]{2,1,0:T(8,128)}), f32[32,64,128]{2,1,0:T(8,128)}, u32[]{:S(2)}, u32[]{:S(2)}) async-start(f32[32,64,128]{2,1,0:T(8,128)} %get-tuple-element.64), calls=%async_computation.7 | async-start | bytes 2097152 | tf_op jit(solution)/shard_map/all_to_all | solution.py:531
  199.3 6.8 %all-to-all-done.7.incoming = f32[32,64,128]{2,1,0:T(8,128)} async-done(((f32[32,64,128]{2,1,0:T(8,128)}), f32[32,64,128]{2,1,0:T(8,128)}, u32[]{:S(2)}, u32[]{:S(2)}) %all-to-all-start.7) | async-done | bytes 1048608 | tf_op jit(solution)/shard_map/all_to_all | solution.py:531
  209.2 5.8 %all-to-all-start.8 = ((f32[128,9,1,128]{3,2,1,0:T(1,128)}), f32[128,9,1,128]{3,2,1,0:T(1,128)}, u32[]{:S(2)}, u32[]{:S(2)}) async-start(f32[128,9,1,128]{3,2,1,0:T(1,128)} %bitcast.31), calls=%async_computation.8 | async-start | bytes 1179648 | tf_op jit(solution)/shard_map/all_to_all | solution.py:531
  214.9 5.8 %inverse.5.local_part = f32[4,8,32,128]{3,2,1,0:T(8,128)} custom-call(f32[4,8,32,128]{3,2,1,0:T(8,128)} %get-tuple-element.71.field, bf16[4,1024,1024]{2,1,0:T(8,128)(2,1)} %matrix.9), custom_call_target="tpu_custom_call" | custom-call | flops 536870912 | bytes 9437184 | tf_op jit(solution)/shard_map/inverse/pallas_call | solution.py:627
  220.8 8.3 %all-to-all-done.8 = f32[128,9,1,128]{3,2,1,0:T(1,128)} async-done(((f32[128,9,1,128]{3,2,1,0:T(1,128)}), f32[128,9,1,128]{3,2,1,0:T(1,128)}, u32[]{:S(2)}, u32[]{:S(2)}) %all-to-all-start.8) | async-done | bytes 589856 | tf_op jit(solution)/shard_map/all_to_all | solution.py:531
  229.1 3.8 %third.1 = (f32[4,8,32,128]{3,2,1,0:T(8,128)}, f32[2,32,128]{2,1,0:T(8,128)}, f32[32,64,128]{2,1,0:T(8,128)}, f32[4,32,128]{2,1,0:T(8,128)}, f32[4,32,128]{2,1,0:T(8,128)}) custom-call(s32[16,128]{1,0:T(8,128)} %pad.8.table, f32[1152,128]{1,0:T(8,128)} %bitcast.11.landed, bf16[256,1152]{1,0:T(8,128)(2,1)} %responses.1, ...), custom_call_target="tpu_custom_call" | custom-call | flops 67108864 | bytes 4194304 | tf_op jit(solution)/shard_map/third/pallas_call | solution.py:753
  232.9 5.3 %all-to-all-start.9 = ((f32[32,64,128]{2,1,0:T(8,128)}), f32[32,64,128]{2,1,0:T(8,128)}, u32[]{:S(2)}, u32[]{:S(2)}) async-start(f32[32,64,128]{2,1,0:T(8,128)} %get-tuple-element.74), calls=%async_computation.9 | async-start | bytes 2097152 | tf_op jit(solution)/shard_map/all_to_all | solution.py:531
  245.7 9.8 %all-to-all-done.9.incoming = f32[32,64,128]{2,1,0:T(8,128)} async-done(((f32[32,64,128]{2,1,0:T(8,128)}), f32[32,64,128]{2,1,0:T(8,128)}, u32[]{:S(2)}, u32[]{:S(2)}) %all-to-all-start.9) | async-done | bytes 1048608 | tf_op jit(solution)/shard_map/all_to_all | solution.py:531
  (135 shorter events, 68.6 us)
Async XLA Ops:
  0.6 44.0 %copy-start = (f32[64,2048]{1,0:T(8,128)S(1)}, f32[64,2048]{1,0:T(8,128)}, u32[]{:S(2)}) copy-start(f32[64,2048]{1,0:T(8,128)} %param.12) | copy-start | bytes 1572868
  0.6 19.0 %copy-start.13 = (f32[4,8,8,128]{3,2,1,0:T(8,128)S(1)}, f32[4,8,8,128]{3,2,1,0:T(8,128)}, u32[]{:S(2)}) copy-start(f32[4,8,8,128]{3,2,1,0:T(8,128)} %param.11) | copy-start | bytes 393220
  6.0 12.4 %copy-start.31 = (f32[4,32,128]{2,1,0:T(8,128)S(1)}, f32[4,32,128]{2,1,0:T(8,128)}, u32[]{:S(2)}) copy-start(f32[4,32,128]{2,1,0:T(8,128)} %get-tuple-element.42) | copy-start | bytes 196612
  6.0 26.5 %all-to-all-start = ((f32[32,72,128]{2,1,0:T(8,128)}), f32[32,72,128]{2,1,0:T(8,128)}, u32[]{:S(2)}, u32[]{:S(2)}) async-start(f32[32,72,128]{2,1,0:T(8,128)} %get-tuple-element.40), calls=%async_computation | async-start | bytes 2359296 | tf_op jit(solution)/shard_map/all_to_all | solution.py:531
  14.8 5.7 %collective-permute-start = (f32[4,32,128]{2,1,0:T(8,128)S(1)}, f32[4,32,128]{2,1,0:T(8,128)S(1)}, u32[]{:S(2)}, u32[]{:S(2)}) collective-permute-start(f32[4,32,128]{2,1,0:T(8,128)S(1)} %copy-done.34), channel_id=1, source_target_pairs={{0,32},{32,64},{64,96},{1,33},{33,65},{65,97},{2,34},{34,66},{66,9... | collective-permute-start | bytes 196616 | tf_op jit(solution)/shard_map/ppermute | solution.py:572
  18.3 5.6 %collective-permute-start.1 = (f32[4,32,128]{2,1,0:T(8,128)S(1)}, f32[4,32,128]{2,1,0:T(8,128)S(1)}, u32[]{:S(2)}, u32[]{:S(2)}) collective-permute-start(f32[4,32,128]{2,1,0:T(8,128)S(1)} %copy-done.31), channel_id=1, source_target_pairs={{32,0},{64,32},{96,64},{33,1},{65,33},{97,65},{34,2},{66,34},{98,6... | collective-permute-start | bytes 196616 | tf_op jit(solution)/shard_map/ppermute | solution.py:573
  20.4 12.1 %copy-start.21 = (f32[4,32,128]{2,1,0:T(8,128)}, f32[4,32,128]{2,1,0:T(8,128)S(1)}, u32[]{:S(2)}) copy-start(f32[4,32,128]{2,1,0:T(8,128)S(1)} %collective-permute-done.before) | copy-start | bytes 196612
  35.7 22.1 %all-to-all-start.1 = ((f32[128,9,1,128]{3,2,1,0:T(1,128)}), f32[128,9,1,128]{3,2,1,0:T(1,128)}, u32[]{:S(2)}, u32[]{:S(2)}) async-start(f32[128,9,1,128]{3,2,1,0:T(1,128)} %bitcast.29), calls=%async_computation.1 | async-start | bytes 1179648 | tf_op jit(solution)/shard_map/all_to_all | solution.py:531
  57.7 14.3 %all-to-all-start.2 = ((f32[32,16,128]{2,1,0:T(8,128)}), f32[32,16,128]{2,1,0:T(8,128)S(1)}, u32[]{:S(2)}, u32[]{:S(2)}) async-start(f32[32,16,128]{2,1,0:T(8,128)} %reshape.92), calls=%async_computation.2 | async-start | bytes 524288 | tf_op jit(solution)/shard_map/all_to_all | solution.py:531
  76.2 22.5 %all-to-all-start.3 = ((f32[32,64,128]{2,1,0:T(8,128)}), f32[32,64,128]{2,1,0:T(8,128)}, u32[]{:S(2)}, u32[]{:S(2)}) async-start(f32[32,64,128]{2,1,0:T(8,128)} %get-tuple-element.49), calls=%async_computation.3 | async-start | bytes 2097152 | tf_op jit(solution)/shard_map/all_to_all | solution.py:531
  81.5 4.7 %collective-permute-start.2 = (f32[4,32,128]{2,1,0:T(8,128)S(1)}, f32[4,32,128]{2,1,0:T(8,128)S(1)}, u32[]{:S(2)}, u32[]{:S(2)}) collective-permute-start(f32[4,32,128]{2,1,0:T(8,128)S(1)} %copy-done.38), channel_id=1, source_target_pairs={{0,32},{32,64},{64,96},{1,33},{33,65},{65,97},{2,34},{34,66},{66,9... | collective-permute-start | bytes 196616 | tf_op jit(solution)/shard_map/ppermute | solution.py:572
  84.9 5.4 %collective-permute-start.3 = (f32[4,32,128]{2,1,0:T(8,128)S(1)}, f32[4,32,128]{2,1,0:T(8,128)S(1)}, u32[]{:S(2)}, u32[]{:S(2)}) collective-permute-start(f32[4,32,128]{2,1,0:T(8,128)S(1)} %copy-done.36), channel_id=1, source_target_pairs={{32,0},{64,32},{96,64},{33,1},{65,33},{97,65},{34,2},{66,34},{98,6... | collective-permute-start | bytes 196616 | tf_op jit(solution)/shard_map/ppermute | solution.py:573
  86.2 12.5 %copy-start.14 = (f32[4,32,128]{2,1,0:T(8,128)}, f32[4,32,128]{2,1,0:T(8,128)S(1)}, u32[]{:S(2)}) copy-start(f32[4,32,128]{2,1,0:T(8,128)S(1)} %collective-permute-done.2.before) | copy-start | bytes 196612
  105.0 22.1 %all-to-all-start.4 = ((f32[32,64,128]{2,1,0:T(8,128)}), f32[32,64,128]{2,1,0:T(8,128)}, u32[]{:S(2)}, u32[]{:S(2)}) async-start(f32[32,64,128]{2,1,0:T(8,128)} %get-tuple-element.53), calls=%async_computation.4 | async-start | bytes 2097152 | tf_op jit(solution)/shard_map/all_to_all | solution.py:531
  110.5 5.4 %collective-permute-start.4 = (f32[4,32,128]{2,1,0:T(8,128)S(1)}, f32[4,32,128]{2,1,0:T(8,128)S(1)}, u32[]{:S(2)}, u32[]{:S(2)}) collective-permute-start(f32[4,32,128]{2,1,0:T(8,128)S(1)} %copy-done.35), channel_id=1, source_target_pairs={{0,32},{32,64},{64,96},{1,33},{33,65},{65,97},{2,34},{34,66},{66,9... | collective-permute-start | bytes 196616 | tf_op jit(solution)/shard_map/ppermute | solution.py:572
  113.9 5.4 %collective-permute-start.5 = (f32[4,32,128]{2,1,0:T(8,128)S(1)}, f32[4,32,128]{2,1,0:T(8,128)S(1)}, u32[]{:S(2)}, u32[]{:S(2)}) collective-permute-start(f32[4,32,128]{2,1,0:T(8,128)S(1)} %copy-done.32), channel_id=1, source_target_pairs={{32,0},{64,32},{96,64},{33,1},{65,33},{97,65},{34,2},{66,34},{98,6... | collective-permute-start | bytes 196616 | tf_op jit(solution)/shard_map/ppermute | solution.py:573
  130.3 20.6 %all-to-all-start.5 = ((f32[128,9,1,128]{3,2,1,0:T(1,128)}), f32[128,9,1,128]{3,2,1,0:T(1,128)}, u32[]{:S(2)}, u32[]{:S(2)}) async-start(f32[128,9,1,128]{3,2,1,0:T(1,128)} %bitcast.30), calls=%async_computation.5 | async-start | bytes 1179648 | tf_op jit(solution)/shard_map/all_to_all | solution.py:531
  154.9 22.6 %all-to-all-start.6 = ((f32[32,64,128]{2,1,0:T(8,128)}), f32[32,64,128]{2,1,0:T(8,128)}, u32[]{:S(2)}, u32[]{:S(2)}) async-start(f32[32,64,128]{2,1,0:T(8,128)} %get-tuple-element.60), calls=%async_computation.6 | async-start | bytes 2097152 | tf_op jit(solution)/shard_map/all_to_all | solution.py:531
  160.2 4.1 %collective-permute-start.6 = (f32[4,32,128]{2,1,0:T(8,128)S(1)}, f32[4,32,128]{2,1,0:T(8,128)S(1)}, u32[]{:S(2)}, u32[]{:S(2)}) collective-permute-start(f32[4,32,128]{2,1,0:T(8,128)S(1)} %copy-done.37), channel_id=1, source_target_pairs={{0,32},{32,64},{64,96},{1,33},{33,65},{65,97},{2,34},{34,66},{66,9... | collective-permute-start | bytes 196616 | tf_op jit(solution)/shard_map/ppermute | solution.py:572
  163.0 5.4 %collective-permute-start.7 = (f32[4,32,128]{2,1,0:T(8,128)S(1)}, f32[4,32,128]{2,1,0:T(8,128)S(1)}, u32[]{:S(2)}, u32[]{:S(2)}) collective-permute-start(f32[4,32,128]{2,1,0:T(8,128)S(1)} %copy-done.33), channel_id=1, source_target_pairs={{32,0},{64,32},{96,64},{33,1},{65,33},{97,65},{34,2},{66,34},{98,6... | collective-permute-start | bytes 196616 | tf_op jit(solution)/shard_map/ppermute | solution.py:573
  164.3 13.3 %copy-start.15 = (f32[4,32,128]{2,1,0:T(8,128)}, f32[4,32,128]{2,1,0:T(8,128)S(1)}, u32[]{:S(2)}) copy-start(f32[4,32,128]{2,1,0:T(8,128)S(1)} %collective-permute-done.6.before) | copy-start | bytes 196612
  183.9 11.2 %copy-start.6 = (f32[4,8,32,128]{3,2,1,0:T(8,128)S(1)}, f32[4,8,32,128]{3,2,1,0:T(8,128)}, u32[]{:S(2)}) copy-start(f32[4,8,32,128]{3,2,1,0:T(8,128)} %get-tuple-element.57) | copy-start | bytes 1572868
  183.9 11.2 %copy-start.9 = (f32[4,8,32,128]{3,2,1,0:T(8,128)S(1)}, f32[4,8,32,128]{3,2,1,0:T(8,128)}, u32[]{:S(2)}) copy-start(f32[4,8,32,128]{3,2,1,0:T(8,128)} %get-tuple-element.56.base) | copy-start | bytes 1572868
  183.9 11.2 %copy-start.10 = (f32[4,8,32,128]{3,2,1,0:T(8,128)S(1)}, f32[4,8,32,128]{3,2,1,0:T(8,128)}, u32[]{:S(2)}) copy-start(f32[4,8,32,128]{3,2,1,0:T(8,128)} %get-tuple-element.69) | copy-start | bytes 1572868
  183.9 22.1 %all-to-all-start.7 = ((f32[32,64,128]{2,1,0:T(8,128)}), f32[32,64,128]{2,1,0:T(8,128)}, u32[]{:S(2)}, u32[]{:S(2)}) async-start(f32[32,64,128]{2,1,0:T(8,128)} %get-tuple-element.64), calls=%async_computation.7 | async-start | bytes 2097152 | tf_op jit(solution)/shard_map/all_to_all | solution.py:531
  191.2 6.4 %collective-permute-start.8 = (f32[4,32,128]{2,1,0:T(8,128)S(1)}, f32[4,32,128]{2,1,0:T(8,128)S(1)}, u32[]{:S(2)}, u32[]{:S(2)}) collective-permute-start(f32[4,32,128]{2,1,0:T(8,128)S(1)} %copy-done.29), channel_id=1, source_target_pairs={{0,32},{32,64},{64,96},{1,33},{33,65},{65,97},{2,34},{34,66},{66,9... | collective-permute-start | bytes 196616 | tf_op jit(solution)/shard_map/ppermute | solution.py:572
  193.8 5.4 %collective-permute-start.9 = (f32[4,32,128]{2,1,0:T(8,128)S(1)}, f32[4,32,128]{2,1,0:T(8,128)S(1)}, u32[]{:S(2)}, u32[]{:S(2)}) collective-permute-start(f32[4,32,128]{2,1,0:T(8,128)S(1)} %copy-done.27), channel_id=1, source_target_pairs={{32,0},{64,32},{96,64},{33,1},{65,33},{97,65},{34,2},{66,34},{98,6... | collective-permute-start | bytes 196616 | tf_op jit(solution)/shard_map/ppermute | solution.py:573
  209.2 19.9 %all-to-all-start.8 = ((f32[128,9,1,128]{3,2,1,0:T(1,128)}), f32[128,9,1,128]{3,2,1,0:T(1,128)}, u32[]{:S(2)}, u32[]{:S(2)}) async-start(f32[128,9,1,128]{3,2,1,0:T(1,128)} %bitcast.31), calls=%async_computation.8 | async-start | bytes 1179648 | tf_op jit(solution)/shard_map/all_to_all | solution.py:531
  232.9 22.6 %all-to-all-start.9 = ((f32[32,64,128]{2,1,0:T(8,128)}), f32[32,64,128]{2,1,0:T(8,128)}, u32[]{:S(2)}, u32[]{:S(2)}) async-start(f32[32,64,128]{2,1,0:T(8,128)} %get-tuple-element.74), calls=%async_computation.9 | async-start | bytes 2097152 | tf_op jit(solution)/shard_map/all_to_all | solution.py:531
  238.2 4.4 %collective-permute-start.10 = (f32[4,32,128]{2,1,0:T(8,128)S(1)}, f32[4,32,128]{2,1,0:T(8,128)S(1)}, u32[]{:S(2)}, u32[]{:S(2)}) collective-permute-start(f32[4,32,128]{2,1,0:T(8,128)S(1)} %copy-done.30), channel_id=1, source_target_pairs={{0,32},{32,64},{64,96},{1,33},{33,65},{65,97},{2,34},{34,66},{66,9... | collective-permute-start | bytes 196616 | tf_op jit(solution)/shard_map/ppermute | solution.py:572
  240.3 5.4 %collective-permute-start.11 = (f32[4,32,128]{2,1,0:T(8,128)S(1)}, f32[4,32,128]{2,1,0:T(8,128)S(1)}, u32[]{:S(2)}, u32[]{:S(2)}) collective-permute-start(f32[4,32,128]{2,1,0:T(8,128)S(1)} %copy-done.28), channel_id=1, source_target_pairs={{32,0},{64,32},{96,64},{33,1},{65,33},{97,65},{34,2},{66,34},{98,6... | collective-permute-start | bytes 196616 | tf_op jit(solution)/shard_map/ppermute | solution.py:573
  242.6 13.0 %copy-start.19 = (f32[4,32,128]{2,1,0:T(8,128)}, f32[4,32,128]{2,1,0:T(8,128)S(1)}, u32[]{:S(2)}) copy-start(f32[4,32,128]{2,1,0:T(8,128)S(1)} %collective-permute-done.10.before) | copy-start | bytes 196612
  (29 other events, 219.0 us)
